TPU v7x, 512 devices: a whole 4x8x8 slice. The times are simulated.
512 devices in a mesh: group: 16 (over y, core), band: 32 (over x, z).
Axes of the slice: x: 4, y: 8, z: 8, core: 2. Of those that a mesh axis runs over, the one named last changes fastest.
Arguments:
- features: bfloat16 [131072, 256], P(('group', 'band')), may hold values from -6 to 6
- block_index: int32 [1024, 24], P(('group', 'band')), may hold values from 0 to 63
- block_count: int32 [1024], P(('group', 'band')), may hold values from 6 to 24, as said below
- block_values: bfloat16 [1024, 24, 128, 128], P(('group', 'band')), may hold values from -0.078125 to 0.078125
- cut_weight: bfloat16 [131072, 2048], P(('group', 'band')), may hold values from -0.078125 to 0.078125
- send_rows: int32 [512, 16, 128], P(('group', 'band')), may hold values from 0 to 255
- send_count: int32 [512, 16], P(('group', 'band')), may hold values from 32 to 128, as said below
- w_self: bfloat16 [256, 256], replicated, may hold values from -0.375 to 0.375
- w_neigh: bfloat16 [256, 256], replicated, may hold values from -0.375 to 0.375
- bias: float32 [256], replicated, may hold values from -3 to 3
- d_out: bfloat16 [131072, 256], P(('group', 'band')), may hold values from -6 to 6
Outputs:
- output: bfloat16 [131072, 256], P(('group', 'band'))
- d_features: bfloat16 [131072, 256], P(('group', 'band'))
- grad_blocks: bfloat16 [1024, 24, 128, 128], P(('group', 'band'))
- grad_self: float32 [256, 256], replicated
- grad_neigh: float32 [256, 256], replicated
- grad_bias: float32 [256], replicated
Inputs may be any that keep to these rules, and one draw needn't show every extreme that they name: `block_count`: the first row tile has all 24 slots live. `send_count`: band p sends 128 live rows to group p % 16.
All inputs are finite; a program needn't handle non-finite values.
Results may differ from a plain program's by a relative error of at most 0.012.
Values may be sent and summed in bfloat16 or wider, within the bound.
No kernel may reach another device: no remote copies, remote signals or barrier semaphores. Data moves between devices by JAX's collectives and lax.ppermute only.
A program may use at most 64 MiB of HBM per device.

v0:
```python
import math

import jax
import jax.numpy as jnp
from jax import lax
from jax.sharding import PartitionSpec as P


def local(
    features,
    block_index,
    block_count,
    block_values,
    cut_weight,
    send_rows,
    send_count,
    w_self,
    w_neigh,
    bias,
    d_out,
):
    tile = block_values.shape[2]
    tiles_here, slots = block_index.shape
    node_rows, width = features.shape
    groups = lax.axis_size("group")
    scale = 1.0 / math.sqrt(node_rows * groups * lax.axis_size("band"))
    live = jnp.arange(slots)[None, :] < block_count[:, None]
    live_blocks = jnp.where(live[:, :, None, None], block_values, jnp.zeros_like(block_values))
    group_rows = lax.all_gather(features, "band", axis=0, tiled=True)
    group_tiles = group_rows.reshape(-1, tile, width)
    group_count = group_tiles.shape[0]
    picked = group_tiles[block_index]
    inner = jnp.einsum(
        "tkij,tkjf->tif", live_blocks, picked, preferred_element_type=jnp.float32
    ).reshape(node_rows, width)
    row_lists = send_rows[0]
    row_counts = send_count[0]
    cut_slots = row_lists.shape[1]
    slot_live = jnp.arange(cut_slots)[None, :] < row_counts[:, None]
    outgoing = jnp.where(slot_live[:, :, None], features[row_lists], jnp.zeros((), features.dtype))
    arrived = lax.all_to_all(outgoing, "group", split_axis=0, concat_axis=0, tiled=True)
    arrived_flat = arrived.reshape(-1, width)
    outer = jnp.dot(cut_weight, arrived_flat, preferred_element_type=jnp.float32)
    aggregate = (inner + outer).astype(jnp.bfloat16)
    pre = (
        jnp.dot(features, w_self, preferred_element_type=jnp.float32)
        + jnp.dot(aggregate, w_neigh, preferred_element_type=jnp.float32)
        + bias
    )
    output = jax.nn.silu(pre).astype(jnp.bfloat16)
    sig = jax.nn.sigmoid(pre)
    d_pre = (d_out.astype(jnp.float32) * sig * (1.0 + pre * (1.0 - sig))).astype(jnp.bfloat16)
    contract_rows = (((0,), (0,)), ((), ()))
    part_self = lax.dot_general(features, d_pre, contract_rows, preferred_element_type=jnp.float32)
    part_neigh = lax.dot_general(
        aggregate, d_pre, contract_rows, preferred_element_type=jnp.float32
    )
    part_bias = jnp.sum(d_pre.astype(jnp.float32), axis=0)
    grad_self, grad_neigh, grad_bias = lax.psum(
        (part_self, part_neigh, part_bias), ("group", "band")
    )
    d_aggregate = jnp.dot(d_pre, w_neigh.T, preferred_element_type=jnp.float32).astype(jnp.bfloat16)
    d_tiles = d_aggregate.reshape(tiles_here, tile, width)
    block_grad = jnp.einsum("tif,tkjf->tkij", d_tiles, picked, preferred_element_type=jnp.float32)
    grad_blocks = jnp.where(live[:, :, None, None], block_grad, jnp.zeros_like(block_grad)).astype(
        jnp.bfloat16
    )
    terms = jnp.einsum("tkij,tif->tkjf", live_blocks, d_tiles, preferred_element_type=jnp.float32)
    flat_terms = terms.reshape(-1, tile, width)
    flat_index = block_index.reshape(-1)
    buffer = jnp.zeros((group_count, tile, width), jnp.float32).at[flat_index].add(flat_terms)
    tile_back = lax.psum_scatter(
        buffer.reshape(-1, width).astype(jnp.bfloat16), "band", scatter_dimension=0, tiled=True
    ).astype(jnp.float32)
    back_rows = lax.dot_general(
        cut_weight, d_aggregate, contract_rows, preferred_element_type=jnp.float32
    )
    back_rows = back_rows.astype(jnp.bfloat16).reshape(groups, cut_slots, width)
    returned = lax.all_to_all(back_rows, "group", split_axis=0, concat_axis=0, tiled=True)
    returned = jnp.where(
        slot_live[:, :, None], returned.astype(jnp.float32), jnp.zeros((), jnp.float32)
    )
    cut_back = (
        jnp.zeros((node_rows, width), jnp.float32)
        .at[row_lists.reshape(-1)]
        .add(returned.reshape(-1, width))
    )
    self_back = jnp.dot(d_pre, w_self.T, preferred_element_type=jnp.float32)
    d_features = (self_back + tile_back + cut_back).astype(jnp.bfloat16)
    return (
        output,
        d_features,
        grad_blocks,
        grad_self * scale,
        grad_neigh * scale,
        grad_bias * scale,
    )


def solution(mesh):
    placed = (
        P(("group", "band"), None),
        P(("group", "band"), None),
        P(("group", "band")),
        P(("group", "band"), None, None, None),
        P(("group", "band"), None),
        P(("group", "band"), None, None),
        P(("group", "band"), None),
        P(),
        P(),
        P(),
        P(("group", "band"), None),
    )
    return jax.shard_map(
        local,
        mesh=mesh,
        in_specs=placed,
        out_specs=(
            P(("group", "band"), None),
            P(("group", "band"), None),
            P(("group", "band"), None, None, None),
            P(),
            P(),
            P(),
        ),
        check_vma=False,
    )
```

profile of v0, /device:TPU:1, one launch (start us, length us, event | category | flops | bytes accessed | tf_op | source)
XLA Modules:
  0.0 638.8 jit_solution(9196811187907765937)
XLA Ops:
  8.6 7.5 %gather_fusion.1 = bf16[2048,256]{1,0:T(8,128)(2,1)S(1)} fusion(bf16[256,256]{1,0:T(8,128)(2,1)S(1)} %copy-done.1, s32[2048]{0:T(1024)S(1)} %fusion.10), kind=kCustom, calls=%fused_computation.1 | custom fusion | bytes 2105344 | tf_op jit(solution)/shard_map/gather | solution.py:40
  16.3 1.2 broadcast_select_fusion.3
  17.5 10.3 %all-to-all-start = ((bf16[16,128,256]{2,1,0:T(8,128)(2,1)}), bf16[16,128,256]{2,1,0:T(8,128)(2,1)S(1)}, u32[]{:S(2)}, u32[]{:S(2)}) async-start(bf16[16,128,256]{2,1,0:T(8,128)(2,1)} %broadcast_select_fusion.3), calls=%async_computation | async-start | bytes 2097152 | tf_op jit(solution)/shard_map/all_to_all | solution.py:41
  28.3 73.5 %all-gather.2.cloned.1.call-done = bf16[8192,256]{1,0:T(8,128)(2,1)} async-done(((bf16[256,256]{1,0:T(8,128)(2,1)}), bf16[8192,256]{1,0:T(8,128)(2,1)}) %all-gather.2.cloned.1.call-update) | async-done | bytes 4194320 | tf_op jit(solution)/shard_map/all_gather | solution.py:29
  101.8 4.7 gather_fusion
  106.5 3.0 fusion.3
  110.2 1.5 convert_reduce_fusion
  112.0 0.9 convolution_bitcast_fusion
  112.9 0.9 fusion.15
  113.9 4.2 fusion.2
  118.1 4.2 broadcast_in_dim.65
  122.3 14.7 %scatter_fusion = f32[64,128,256]{2,1,0:T(8,128)} fusion(f32[64,128,256]{2,1,0:T(8,128)} %broadcast_in_dim.65, s32[48]{0:T(128)S(1)} %fusion.11, f32[48,128,256]{2,1,0:T(8,128)} %bitcast.60), kind=kCustom, calls=%fused_computation.2 | custom fusion | flops 1572864 | bytes 18874560 | tf_op jit(solution)/shard_map/scatter-add | solution.py:71
  137.1 6.0 convert_element_type.50
  143.6 1.3 copy.28
  144.9 11.1 %all-to-all-start.1 = ((bf16[16,128,256]{2,1,0:T(8,128)(2,1)}), bf16[16,128,256]{2,1,0:T(8,128)(2,1)}, u32[]{:S(2)}, u32[]{:S(2)}) async-start(bf16[16,128,256]{2,1,0:T(8,128)(2,1)} %bitcast.20), calls=%async_computation.2 | async-start | bytes 2097152 | tf_op jit(solution)/shard_map/all_to_all | solution.py:79
  156.0 2.9 fusion.1
  158.9 1.6 copy.21
  160.4 109.4 %psum.23 = f32[256]{0:T(256)S(1)} all-reduce(f32[256]{0:T(256)S(1)} %copy-done.7), channel_id=1, replica_groups=mesh['group'=16,'band'=32] {'group','band'}, use_global_device_ids=true, to_apply=%region_6.7 | all-reduce | flops 256 | bytes 2048 | tf_op jit(solution)/shard_map/psum | solution.py:59
  270.4 124.8 %all-reduce.3.cloned.1.call-done = (f32[256,256]{0,1:T(8,128)}, f32[256,256]{0,1:T(8,128)}) async-done(((f32[256,256]{0,1:T(8,128)}, f32[256,256]{0,1:T(8,128)}), (f32[256,256]{0,1:T(8,128)}, f32[256,256]{0,1:T(8,128)})) %all-reduce.3.cloned.1.call-update) | async-done | bytes 524304 | tf_op jit(solution)/shard_map/psum | solution.py:59
  395.2 1.1 broadcast_multiply_fusion
  398.0 1.6 convert_select_fusion
  399.5 219.1 %reduce-scatter.2.cloned.1.call-done = bf16[256,256]{1,0:T(8,128)(2,1)} async-done(((bf16[8192,256]{1,0:T(8,128)(2,1)}), bf16[256,256]{1,0:T(8,128)(2,1)}) %reduce-scatter.2.cloned.1.call-update) | async-done | bytes 131088 | tf_op jit(solution)/shard_map/reduce_scatter | solution.py:72
  618.7 1.2 convolution_add_fusion
  619.9 11.7 %scatter_fusion.1 = f32[256,256]{1,0:T(8,128)S(1)} fusion(f32[256,256]{1,0:T(8,128)S(1)} %convolution_add_fusion, s32[2048]{0:T(1024)S(1)} %bitcast.71, f32[2048,256]{1,0:T(8,128)S(1)} %bitcast.62), kind=kCustom, calls=%fused_computation.3 | custom fusion | flops 524288 | bytes 6299648 | tf_op jit(solution)/shard_map/scatter-add | solution.py:86
  (50 shorter events, 6.3 us)
Async XLA Ops:
  7.2 102.5 %copy-start = (bf16[256,2048]{1,0:T(8,128)(2,1)S(1)}, bf16[256,2048]{1,0:T(8,128)(2,1)}, u32[]{:S(2)}) copy-start(bf16[256,2048]{1,0:T(8,128)(2,1)} %param.15) | copy-start | bytes 3145732
  7.2 1.5 copy-start.1
  7.2 94.6 %all-gather.2.cloned.1.call-start = ((), (), s32[]{:S(2)}) async-start(), calls=%async_computation.3 | async-start | bytes 4325376 | tf_op jit(solution)/shard_map/all_gather | solution.py:29
  8.6 7.5 %copy-start.8 = (s32[1,16]{1,0:T(1,128)S(1)}, s32[1,16]{1,0:T(1,128)}, u32[]{:S(2)}) copy-start(s32[1,16]{1,0:T(1,128)} %param.17) | copy-start | bytes 196
  16.1 11.7 %copy-start.6 = (s32[2,24]{1,0:T(2,128)S(1)}, s32[2,24]{1,0:T(2,128)}, u32[]{:S(2)}) copy-start(s32[2,24]{1,0:T(2,128)} %param.12) | copy-start | bytes 580
  16.2 11.9 %copy-start.11 = (s32[2]{0:T(128)S(1)}, s32[2]{0:T(128)}, u32[]{:S(2)}) copy-start(s32[2]{0:T(128)} %param.13) | copy-start | bytes 28
  16.2 11.9 %copy-start.3 = (bf16[256,256]{1,0:T(8,128)(2,1)S(1)}, bf16[256,256]{1,0:T(8,128)(2,1)}, u32[]{:S(2)}) copy-start(bf16[256,256]{1,0:T(8,128)(2,1)} %param.18) | copy-start | bytes 393220
  17.5 92.2 %all-to-all-start = ((bf16[16,128,256]{2,1,0:T(8,128)(2,1)}), bf16[16,128,256]{2,1,0:T(8,128)(2,1)S(1)}, u32[]{:S(2)}, u32[]{:S(2)}) async-start(bf16[16,128,256]{2,1,0:T(8,128)(2,1)} %broadcast_select_fusion.3), calls=%async_computation | async-start | bytes 2097152 | tf_op jit(solution)/shard_map/all_to_all | solution.py:41
  27.8 367.4 %all-reduce.3.cloned.1.call-start = ((), (), s32[]{:S(2)}) async-start(), calls=%async_computation.5 | async-start | bytes 1048576 | tf_op jit(solution)/shard_map/psum | solution.py:59
  106.5 3.7 copy-start.4
  106.5 3.7 copy-start.9
  106.5 3.7 copy-start.10
  110.2 3.7 copy-start.2
  113.9 504.8 %reduce-scatter.2.cloned.1.call-start = ((), (), s32[]{:S(2)}) async-start(), calls=%async_computation.4 | async-start | bytes 4325376 | tf_op jit(solution)/shard_map/reduce_scatter | solution.py:72
  143.1 12.9 %copy-start.5 = (s32[1,16,128]{2,1,0:T(8,128)S(1)}, s32[1,16,128]{2,1,0:T(8,128)}, u32[]{:S(2)}) copy-start(s32[1,16,128]{2,1,0:T(8,128)} %param.16) | copy-start | bytes 24580
  144.9 253.1 %all-to-all-start.1 = ((bf16[16,128,256]{2,1,0:T(8,128)(2,1)}), bf16[16,128,256]{2,1,0:T(8,128)(2,1)}, u32[]{:S(2)}, u32[]{:S(2)}) async-start(bf16[16,128,256]{2,1,0:T(8,128)(2,1)} %bitcast.20), calls=%async_computation.2 | async-start | bytes 2097152 | tf_op jit(solution)/shard_map/all_to_all | solution.py:79
  156.0 4.5 copy-start.7
Sparse Core Ops, SparseCore 0:
  11.2 90.5 all-gather.1
  114.0 281.1 all-reduce.2
  400.4 218.2 reduce-scatter.1
where the time goes:
time: 643 us; the launch traced here: 639 us
  waiting for transfers between devices  418 us (65%)
  blocking collectives  109 us (17%)
  other arithmetic  38.4 us (6%)
  starting transfers between devices  21.5 us (3%)
  local copies, waits for them, and re-layouts  21.3 us (3%)
  matrix products  16 us (2%)
  between operations  14 us (2%)
    reduce_scatter x1, waiting for transfers between devices, local(): lax.psum_scatter(buffer.reshape(-1, width).astype(jnp.bfloat16), 'band',...  219 us
    psum x1, waiting for transfers between devices, local(): lax.psum((part_self, part_neigh, part_bias), ('group', 'band'))  125 us
    psum x1, blocking collectives, local(): lax.psum((part_self, part_neigh, part_bias), ('group', 'band'))  109 us
    all_gather x1, waiting for transfers between devices, local(): group_rows = lax.all_gather(features, 'band', axis=0, tiled=True)  73.5 us
    scatter-add x1, other arithmetic, local(): jnp.zeros((group_count, tile, width), jnp.float32).at[flat_index]  14.7 us
  transfers between devices with their start and end apart: 5, of which 3 were waited for; matrix products, arithmetic and copies ran while one was open for 9% of the time, Pallas kernels for 0%

commit v1 on v0

v1 whole, which is shorter than its diff:
```python
import functools
import math

import jax
import jax.numpy as jnp
from jax import lax
from jax.experimental import pallas as pl
from jax.experimental.pallas import tpu as pltpu
from jax.sharding import Mesh, PartitionSpec as P

BF = jnp.bfloat16
F32 = jnp.float32
TN = (((0,), (0,)), ((), ()))
NT = (((1,), (1,)), ((), ()))
NX, NZ, NY, NC = 4, 8, 8, 2
NG = NY * NC
HALF = NX * NZ
GRAD_ROWS = 40
VMEM = pl.BlockSpec(memory_space=pltpu.VMEM)
SMEM = pl.BlockSpec(memory_space=pltpu.SMEM)
HBM = pl.BlockSpec(memory_space=pl.ANY)


def sds(shape, dtype):
    return jax.ShapeDtypeStruct(shape, dtype)


def call(body, out_shape, in_specs, out_specs, scratch=(), flops=0, nbytes=0, vmem=24):
    return pl.pallas_call(
        body,
        out_shape=out_shape,
        in_specs=in_specs,
        out_specs=out_specs,
        scratch_shapes=list(scratch),
        compiler_params=pltpu.CompilerParams(vmem_limit_bytes=vmem << 20),
        cost_estimate=pl.CostEstimate(flops=flops, bytes_accessed=nbytes, transcendentals=0),
    )


def hot_columns(rows_ref, count_ref, g, nodes):
    rows = rows_ref[g : g + 1, :]
    lane = lax.broadcasted_iota(jnp.int32, rows.shape, 1)
    rows = jnp.where(lane < count_ref[0, g], rows, -1)
    node = lax.broadcasted_iota(jnp.int32, (nodes, rows.shape[1]), 0)
    return jnp.where(node == rows, 1.0, 0.0).astype(BF)


def pick_body(count_ref, rows_ref, feat_ref, out_ref):
    feat = feat_ref[...]
    for g in range(out_ref.shape[0]):
        hot = hot_columns(rows_ref, count_ref, g, feat.shape[0])
        out_ref[g] = lax.dot_general(hot, feat, TN, preferred_element_type=F32).astype(BF)


def place(index_ref, count_ref, t, k):
    index = index_ref[t, k]
    band = lax.shift_right_logical(index, 1)
    even = (band & (NZ - 1)) * NX + lax.shift_right_logical(band, 3)
    slot = jnp.where((index & 1) == 0, even, HALF + band)
    return jnp.where(k < count_ref[t], slot, 2 * HALF)


def main_body(
    index_ref, count_ref, even_ref, odd_ref, blocks_ref, outer_ref, pre_ref, w_ref, dout_ref,
    out_ref, dpre_ref, dagg_ref, agg_ref, teven_ref, todd_ref,
    tiles, acc, sems,
):
    slots = blocks_ref.shape[1]
    copies = [
        pltpu.make_async_copy(even_ref, tiles.at[pl.ds(0, HALF)], sems.at[0]),
        pltpu.make_async_copy(odd_ref, tiles.at[pl.ds(HALF, HALF)], sems.at[1]),
    ]
    for copy in copies:
        copy.start()
    tiles[2 * HALF] = jnp.zeros(tiles.shape[1:], BF)

    def clear(i, carry):
        acc[i] = jnp.zeros(acc.shape[1:], F32)
        return carry

    lax.fori_loop(0, 2 * HALF, clear, 0)
    for copy in copies:
        copy.wait()
    where = [[place(index_ref, count_ref, t, k) for k in range(slots)] for t in range(2)]
    for t in range(2):
        rows = pl.ds(t * 128, 128)
        total = outer_ref[rows, :]
        for k in range(0, slots, 2):
            left = jnp.concatenate([blocks_ref[t, k], blocks_ref[t, k + 1]], axis=1)
            right = jnp.concatenate([tiles[where[t][k]], tiles[where[t][k + 1]]], axis=0)
            total = total + jnp.dot(left, right, preferred_element_type=F32)
        agg = total.astype(BF)
        agg_ref[rows, :] = agg
        pre = pre_ref[rows, :] + jnp.dot(agg, w_ref[...], preferred_element_type=F32)
        sig = jax.nn.sigmoid(pre)
        out_ref[rows, :] = (pre * sig).astype(BF)
        d_pre = (dout_ref[rows, :].astype(F32) * sig * (1.0 + pre * (1.0 - sig))).astype(BF)
        dpre_ref[rows, :] = d_pre
        d_agg = lax.dot_general(d_pre, w_ref[...], NT, preferred_element_type=F32).astype(BF)
        dagg_ref[rows, :] = d_agg
        for k in range(slots):
            spot = where[t][k]
            term = lax.dot_general(blocks_ref[t, k], d_agg, TN, preferred_element_type=F32)
            acc[spot] = acc[spot] + term

    def store(i, carry):
        teven_ref[i] = acc[i].astype(BF)
        todd_ref[i] = acc[HALF + i].astype(BF)
        return carry

    lax.fori_loop(0, HALF, store, 0)


def third_body(
    dagg_ref, dpre_ref, agg_ref, feat_ref, cut_ref, w_ref, back_ref, part_ref, self_ref
):
    d_pre = dpre_ref[...]
    width = d_pre.shape[1]
    part_ref[pl.ds(0, width), :] = lax.dot_general(
        feat_ref[...], d_pre, TN, preferred_element_type=F32
    )
    part_ref[pl.ds(width, width), :] = lax.dot_general(
        agg_ref[...], d_pre, TN, preferred_element_type=F32
    )
    rest = part_ref.shape[0] - 2 * width
    row = lax.broadcasted_iota(jnp.int32, (rest, width), 0)
    bias = jnp.sum(d_pre.astype(F32), axis=0, keepdims=True)
    part_ref[pl.ds(2 * width, rest), :] = jnp.where(row == 0, bias, 0.0)
    self_ref[...] = lax.dot_general(d_pre, w_ref[...], NT, preferred_element_type=F32)
    d_agg = dagg_ref[...]
    for c in range(0, cut_ref.shape[1], 256):
        back_ref[pl.ds(c, 256), :] = lax.dot_general(
            cut_ref[:, pl.ds(c, 256)], d_agg, TN, preferred_element_type=F32
        ).astype(BF)


def blocks_body(index_ref, count_ref, even_ref, odd_ref, dagg_ref, out_ref, tiles, sems):
    copies = [
        pltpu.make_async_copy(even_ref, tiles.at[pl.ds(0, HALF)], sems.at[0]),
        pltpu.make_async_copy(odd_ref, tiles.at[pl.ds(HALF, HALF)], sems.at[1]),
    ]
    for copy in copies:
        copy.start()
    tiles[2 * HALF] = jnp.zeros(tiles.shape[1:], BF)
    for copy in copies:
        copy.wait()
    for t in range(2):
        d_agg = dagg_ref[pl.ds(t * 128, 128), :]
        for k in range(out_ref.shape[1]):
            tile = tiles[place(index_ref, count_ref, t, k)]
            out_ref[t, k] = lax.dot_general(
                d_agg, tile, NT, preferred_element_type=F32
            ).astype(BF)


def base_body(count_ref, rows_ref, back_ref, self_ref, out_ref):
    total = self_ref[...]
    for g in range(0, back_ref.shape[0], 2):
        hot = jnp.concatenate(
            [hot_columns(rows_ref, count_ref, g + i, total.shape[0]) for i in range(2)], axis=1
        )
        rows = jnp.concatenate([back_ref[g], back_ref[g + 1]], axis=0)
        total = total + jnp.dot(hot, rows, preferred_element_type=F32)
    out_ref[...] = total


def a2a(x, axis):
    return lax.all_to_all(x, axis, 0, 0, tiled=True)


def spread(x, axis, n):
    return a2a(jnp.broadcast_to(x[None], (n, *x.shape)), axis)


def local(
    features, block_index, block_count, block_values, cut_weight, send_rows, send_count,
    w_self, w_neigh, bias, d_out,
):
    nodes, width = features.shape
    tiles_here, slots = block_index.shape
    scale = 1.0 / math.sqrt(nodes * NG * HALF)
    rows2 = send_rows.reshape(NG, -1)
    cut = rows2.shape[1]

    even = spread(features[:128], "x", NX)
    even = lax.all_gather(even, "z", axis=0, tiled=True)
    odd = spread(features[128:], "z", NZ)
    odd = spread(odd, "x", NX).reshape(HALF, 128, width)

    outgoing = call(
        pick_body, sds((NG, cut, width), BF), [SMEM, VMEM, VMEM], VMEM,
        flops=2 * NG * cut * width * nodes, nbytes=1 << 20,
    )(send_count, rows2, features)
    arrived = a2a(outgoing, ("y", "c")).reshape(NG * cut, width)
    outer = jnp.dot(cut_weight, arrived, preferred_element_type=F32)
    own_pre = jnp.dot(features, w_self, preferred_element_type=F32) + bias

    node_bf = sds((nodes, width), BF)
    half_bf = sds((HALF, 128, width), BF)
    gathered = pltpu.VMEM((2 * HALF + 1, 128, width), BF)
    output, d_pre, d_agg, aggregate, t_even, t_odd = call(
        main_body,
        (node_bf, node_bf, node_bf, node_bf, half_bf, half_bf),
        [SMEM, SMEM, HBM, HBM, VMEM, VMEM, VMEM, VMEM, VMEM],
        (VMEM,) * 6,
        [gathered, pltpu.VMEM((2 * HALF + 1, 128, width), F32), pltpu.SemaphoreType.DMA((2,))],
        flops=2 << 30, nbytes=16 << 20, vmem=40,
    )(block_index, block_count, even, odd, block_values, outer, own_pre, w_neigh, d_out)

    t_even = lax.psum_scatter(t_even.reshape(NZ, NX * 128, width), "z", scatter_dimension=0)
    t_odd = a2a(t_odd.reshape(NX, NZ, 128, width), "x")
    t_odd = jnp.sum(t_odd.astype(F32), axis=0).astype(BF)
    t_odd = a2a(t_odd, "z")
    t_odd = jnp.sum(t_odd.astype(F32), axis=0)
    t_even = a2a(t_even.reshape(NX, 128, width), "x")
    t_even = jnp.sum(t_even.astype(F32), axis=0)

    back, part, self_back = call(
        third_body,
        (sds((NG * cut, width), BF), sds((NG * GRAD_ROWS, width), F32), sds((nodes, width), F32)),
        [VMEM] * 6, (VMEM,) * 3, flops=400 << 20, nbytes=4 << 20,
    )(d_agg, d_pre, aggregate, features, cut_weight, w_self)
    returned = a2a(back.reshape(NG, cut, width), ("y", "c"))
    base = call(
        base_body, sds((nodes, width), F32), [SMEM, VMEM, VMEM, VMEM], VMEM,
        flops=2 * NG * cut * width * nodes, nbytes=2 << 20,
    )(send_count, rows2, returned, self_back)
    d_features = (base + jnp.concatenate([t_even, t_odd], axis=0)).astype(BF)

    part = jnp.sum(a2a(part.reshape(NG, GRAD_ROWS, width), ("y", "c")), axis=0)
    part = jnp.sum(spread(part, "x", NX), axis=0)
    part = jnp.sum(spread(part, "z", NZ), axis=0) * scale
    grads = spread(part, ("y", "c"), NG).reshape(-1, width)

    grad_blocks = call(
        blocks_body, sds(block_values.shape, BF), [SMEM, SMEM, HBM, HBM, VMEM], VMEM,
        [gathered, pltpu.SemaphoreType.DMA((2,))],
        flops=2 * tiles_here * slots * 128 * 128 * width, nbytes=6 << 20,
    )(block_index, block_count, even, odd, d_agg)

    return (
        output,
        d_features,
        grad_blocks,
        grads[:width],
        grads[width : 2 * width],
        grads[2 * width],
    )


def solution(mesh):
    mesh = Mesh(mesh.devices.reshape(NY, NC, NX, NZ), ("y", "c", "x", "z"))
    rows = ("y", "c", "x", "z")
    split = [P(rows)] * 7 + [P()] * 3 + [P(rows)]
    return jax.shard_map(
        local,
        mesh=mesh,
        in_specs=tuple(split),
        out_specs=(P(rows), P(rows), P(rows), P(), P(), P()),
        check_vma=False,
    )
```

time: 643 us -> 312 us (0.49)
  waiting for transfers between devices: 418 us -> 132 us
  other arithmetic: 38.4 us -> 5.79 us
  blocking collectives: 109 us -> 81.4 us
  starting transfers between devices: 21.5 us -> 40.4 us
  matrix products: 16 us -> 3.26 us
  Pallas kernels: 0 us -> 11.2 us
    reduce_scatter x1, waiting for transfers between devices: 219 us -> 0.01 us  [local(): lax.psum_scatter(t_even.reshape(NZ, NX * 128, width), 'z', scatter_dimens...]
    all_to_all x2 -> x8, waiting for transfers between devices: 0.01 us -> 131 us  [a2a(): return lax.all_to_all(x, axis, 0, 0, tiled=True)]
    psum x1 -> x0, waiting for transfers between devices: 125 us -> none  [local(): lax.psum((part_self, part_neigh, part_bias), ('group', 'band'))]
    psum x1 -> x0, blocking collectives: 109 us -> none  [local(): lax.psum((part_self, part_neigh, part_bias), ('group', 'band'))]
    all_to_all x0 -> x4, blocking collectives: none -> 81.4 us  [a2a(): return lax.all_to_all(x, axis, 0, 0, tiled=True)]
    all_gather x1, waiting for transfers between devices: 73.5 us -> 0.01 us  [local(): even = lax.all_gather(even, 'z', axis=0, tiled=True)]
    scatter-add x2 -> x0, other arithmetic: 26.4 us -> none  [the longest x1 14.7 us: local(): jnp.zeros((group_count, tile, width), jnp.float32).at[flat_index]]
    all_to_all x2 -> x8, starting transfers between devices: 21.4 us -> 40.3 us  [a2a(): return lax.all_to_all(x, axis, 0, 0, tiled=True)]
  transfers between devices with their start and end apart: 5 -> 10, of which waited for: 3 -> 8; matrix products, arithmetic and copies ran while one was open for 9% -> 4% of each run, Pallas kernels for 0% -> 2%
where the time goes in v1:
time: 312 us; the launch traced here: 310 us
  waiting for transfers between devices  132 us (42%)
  blocking collectives  81.4 us (26%)
  starting transfers between devices  40.4 us (13%)
  local copies, waits for them, and re-layouts  22.2 us (7%)
  between operations  14.3 us (5%)
  Pallas kernels  11.2 us (4%)
  other arithmetic  5.79 us (2%)
  matrix products  3.26 us (1%)
    all_to_all x8, waiting for transfers between devices, a2a(): return lax.all_to_all(x, axis, 0, 0, tiled=True)  131 us
    all_to_all x4, blocking collectives, a2a(): return lax.all_to_all(x, axis, 0, 0, tiled=True)  81.4 us
    all_to_all x8, starting transfers between devices, a2a(): return lax.all_to_all(x, axis, 0, 0, tiled=True)  40.3 us
    unnamed x44, local copies, waits for them, and re-layouts  14.1 us
  transfers between devices with their start and end apart: 10, of which 8 were waited for; matrix products, arithmetic and copies ran while one was open for 4% of the time, Pallas kernels for 2%

profile of v1, /device:TPU:1, one launch (start us, length us, event | category | flops | bytes accessed | tf_op | source)
XLA Modules:
  0.0 310.4 jit_solution(11384606479301928781)
XLA Ops:
  8.2 10.3 %all_to_all.60 = bf16[4,128,256]{2,1,0:T(8,128)(2,1)} all-to-all(bf16[4,128,256]{2,1,0:T(8,128)(2,1)S(1)} %broadcast_in_dim.12), channel_id=1, replica_groups=mesh['y'=8,'c'=2,'x'=4,'z'=8] {'x'}, dimensions={0} | all-to-all | bytes 524288 | tf_op jit(solution)/shard_map/all_to_all | solution.py:168
  19.3 10.1 %all-to-all-start.1 = ((bf16[8,128,256]{2,1,0:T(8,128)(2,1)}), bf16[8,128,256]{2,1,0:T(8,128)(2,1)S(1)}, u32[]{:S(2)}, u32[]{:S(2)}) async-start(bf16[8,128,256]{2,1,0:T(8,128)(2,1)} %broadcast_in_dim.13), calls=%async_computation.1 | async-start | bytes 1048576 | tf_op jit(solution)/shard_map/all_to_all | solution.py:168
  31.2 13.3 %all-to-all-done.1 = bf16[8,128,256]{2,1,0:T(8,128)(2,1)S(1)} async-done(((bf16[8,128,256]{2,1,0:T(8,128)(2,1)}), bf16[8,128,256]{2,1,0:T(8,128)(2,1)S(1)}, u32[]{:S(2)}, u32[]{:S(2)}) %all-to-all-start.1) | async-done | bytes 524320 | tf_op jit(solution)/shard_map/all_to_all | solution.py:168
  44.5 38.9 %all_to_all.61 = bf16[16,128,256]{2,1,0:T(8,128)(2,1)} all-to-all(bf16[16,128,256]{2,1,0:T(8,128)(2,1)S(1)} %shard_map.154), channel_id=1, replica_groups=mesh['y'=8,'c'=2,'x'=4,'z'=8] {'y','c'}, dimensions={0} | all-to-all | bytes 2097152 | tf_op jit(solution)/shard_map/all_to_all | solution.py:168
  84.9 3.7 %all-to-all-start.2 = ((bf16[4,8,128,256]{3,2,1,0:T(8,128)(2,1)}), bf16[4,8,128,256]{3,2,1,0:T(8,128)(2,1)S(1)}, u32[]{:S(2)}, u32[]{:S(2)}) async-start(bf16[4,8,128,256]{3,2,1,0:T(8,128)(2,1)} %broadcast_in_dim.14), calls=%async_computation.2 | async-start | bytes 4194304 | tf_op jit(solution)/shard_map/all_to_all | solution.py:168
  89.6 2.4 convolution_bitcast_fusion.outer_ref
  91.9 22.5 %all-to-all-done.2 = bf16[4,8,128,256]{3,2,1,0:T(8,128)(2,1)S(1)} async-done(((bf16[4,8,128,256]{3,2,1,0:T(8,128)(2,1)}), bf16[4,8,128,256]{3,2,1,0:T(8,128)(2,1)S(1)}, u32[]{:S(2)}, u32[]{:S(2)}) %all-to-all-start.2) | async-done | bytes 2097184 | tf_op jit(solution)/shard_map/all_to_all | solution.py:168
  121.8 5.6 %shard_map.155 = (bf16[256,256]{1,0:T(8,128)(2,1)}, bf16[256,256]{1,0:T(8,128)(2,1)S(1)}, bf16[256,256]{1,0:T(8,128)(2,1)S(1)}, bf16[256,256]{1,0:T(8,128)(2,1)S...) custom-call(s32[2,24]{1,0:T(2,128)S(1)} %copy-done.14, s32[2]{0:T(128)S(1)} %copy-done.15, ...), custom_call_target="tpu_custom_call" | custom-call | flops 2147483648 | bytes 16777216 | tf_op jit(solution)/shard_map/pallas_call | solution.py:201
  132.4 23.9 %all_to_all.62 = f32[16,40,256]{2,1,0:T(8,128)S(1)} all-to-all(f32[16,40,256]{2,1,0:T(8,128)S(1)} %bitcast.21), channel_id=1, replica_groups=mesh['y'=8,'c'=2,'x'=4,'z'=8] {'y','c'}, dimensions={0} | all-to-all | bytes 1310720 | tf_op jit(solution)/shard_map/all_to_all | solution.py:168
  156.4 8.3 %all_to_all.63 = f32[4,40,256]{2,1,0:T(8,128)S(1)} all-to-all(f32[4,40,256]{2,1,0:T(8,128)S(1)} %broadcast_in_dim.15), channel_id=1, replica_groups=mesh['y'=8,'c'=2,'x'=4,'z'=8] {'x'}, dimensions={0} | all-to-all | bytes 327680 | tf_op jit(solution)/shard_map/all_to_all | solution.py:168
  164.6 4.5 %all-to-all-start.6 = ((bf16[4,8,128,256]{3,2,1,0:T(8,128)(2,1)}), bf16[4,8,128,256]{3,2,1,0:T(8,128)(2,1)}, u32[]{:S(2)}, u32[]{:S(2)}) async-start(bf16[4,8,128,256]{3,2,1,0:T(8,128)(2,1)} %bitcast.19), calls=%async_computation.7 | async-start | bytes 4194304 | tf_op jit(solution)/shard_map/all_to_all | solution.py:168
  169.1 25.8 %all-to-all-done.6 = bf16[4,8,128,256]{3,2,1,0:T(8,128)(2,1)} async-done(((bf16[4,8,128,256]{3,2,1,0:T(8,128)(2,1)}), bf16[4,8,128,256]{3,2,1,0:T(8,128)(2,1)}, u32[]{:S(2)}, u32[]{:S(2)}) %all-to-all-start.6) | async-done | bytes 2097184 | tf_op jit(solution)/shard_map/all_to_all | solution.py:168
  195.7 3.4 %all-to-all-start.10 = ((f32[8,40,256]{2,1,0:T(8,128)}), f32[8,40,256]{2,1,0:T(8,128)S(1)}, u32[]{:S(2)}, u32[]{:S(2)}) async-start(f32[8,40,256]{2,1,0:T(8,128)} %broadcast_in_dim.16), calls=%async_computation.11 | async-start | bytes 655360 | tf_op jit(solution)/shard_map/all_to_all | solution.py:168
  199.9 10.3 %all-to-all-done.10 = f32[8,40,256]{2,1,0:T(8,128)S(1)} async-done(((f32[8,40,256]{2,1,0:T(8,128)}), f32[8,40,256]{2,1,0:T(8,128)S(1)}, u32[]{:S(2)}, u32[]{:S(2)}) %all-to-all-start.10) | async-done | bytes 327712 | tf_op jit(solution)/shard_map/all_to_all | solution.py:168
  210.9 6.6 %all-to-all-start.4 = ((bf16[16,128,256]{2,1,0:T(8,128)(2,1)}), bf16[16,128,256]{2,1,0:T(8,128)(2,1)S(1)}, u32[]{:S(2)}, u32[]{:S(2)}) async-start(bf16[16,128,256]{2,1,0:T(8,128)(2,1)} %bitcast.20), calls=%async_computation.4 | async-start | bytes 2097152 | tf_op jit(solution)/shard_map/all_to_all | solution.py:168
  217.4 2.9 reduce_sum.58
  220.3 25.1 %all-to-all-done.4.back_ref = bf16[16,128,256]{2,1,0:T(8,128)(2,1)S(1)} async-done(((bf16[16,128,256]{2,1,0:T(8,128)(2,1)}), bf16[16,128,256]{2,1,0:T(8,128)(2,1)S(1)}, u32[]{:S(2)}, u32[]{:S(2)}) %all-to-all-start.4) | async-done | bytes 1048608 | tf_op jit(solution)/shard_map/all_to_all | solution.py:168
  245.4 4.1 %all-to-all-start.7 = ((bf16[8,128,256]{2,1,0:T(8,128)(2,1)}), bf16[8,128,256]{2,1,0:T(8,128)(2,1)}, u32[]{:S(2)}, u32[]{:S(2)}) async-start(bf16[8,128,256]{2,1,0:T(8,128)(2,1)} %reduce_sum.58), calls=%async_computation.8 | async-start | bytes 1048576 | tf_op jit(solution)/shard_map/all_to_all | solution.py:168
  250.6 16.3 %all-to-all-done.7 = bf16[8,128,256]{2,1,0:T(8,128)(2,1)} async-done(((bf16[8,128,256]{2,1,0:T(8,128)(2,1)}), bf16[8,128,256]{2,1,0:T(8,128)(2,1)}, u32[]{:S(2)}, u32[]{:S(2)}) %all-to-all-start.7) | async-done | bytes 524320 | tf_op jit(solution)/shard_map/all_to_all | solution.py:168
  267.8 4.5 %all-to-all-start.11 = ((f32[16,40,256]{2,1,0:T(8,128)}), f32[16,40,256]{2,1,0:T(8,128)}, u32[]{:S(2)}, u32[]{:S(2)}) async-start(f32[16,40,256]{2,1,0:T(8,128)} %broadcast_in_dim.17), calls=%async_computation.12 | async-start | bytes 1310720 | tf_op jit(solution)/shard_map/all_to_all | solution.py:168
  273.9 3.0 shard_map.158
  279.0 13.4 %all-to-all-done.11 = f32[16,40,256]{2,1,0:T(8,128)} async-done(((f32[16,40,256]{2,1,0:T(8,128)}), f32[16,40,256]{2,1,0:T(8,128)}, u32[]{:S(2)}, u32[]{:S(2)}) %all-to-all-start.11) | async-done | bytes 655392 | tf_op jit(solution)/shard_map/all_to_all | solution.py:168
  293.7 3.4 %all-to-all-start.5 = ((bf16[4,128,256]{2,1,0:T(8,128)(2,1)}), bf16[4,128,256]{2,1,0:T(8,128)(2,1)S(1)}, u32[]{:S(2)}, u32[]{:S(2)}) async-start(bf16[4,128,256]{2,1,0:T(8,128)(2,1)} %bitcast.25), calls=%async_computation.6 | async-start | bytes 524288 | tf_op jit(solution)/shard_map/all_to_all | solution.py:168
  298.9 3.9 %all-to-all-done.5 = bf16[4,128,256]{2,1,0:T(8,128)(2,1)S(1)} async-done(((bf16[4,128,256]{2,1,0:T(8,128)(2,1)}), bf16[4,128,256]{2,1,0:T(8,128)(2,1)S(1)}, u32[]{:S(2)}, u32[]{:S(2)}) %all-to-all-start.5) | async-done | bytes 262176 | tf_op jit(solution)/shard_map/all_to_all | solution.py:168
  (70 shorter events, 30.0 us)
Async XLA Ops:
  7.2 22.9 %copy-start.5 = (bf16[256,256]{1,0:T(8,128)(2,1)S(1)}, bf16[256,256]{1,0:T(8,128)(2,1)}, u32[]{:S(2)}) copy-start(bf16[256,256]{1,0:T(8,128)(2,1)} %feat_ref.3) | copy-start | bytes 393220
  7.2 22.9 %copy-start.13 = (s32[1,16]{1,0:T(1,128)S(1)}, s32[1,16]{1,0:T(1,128)}, u32[]{:S(2)}) copy-start(s32[1,16]{1,0:T(1,128)} %count_ref.6) | copy-start | bytes 196
  7.2 22.9 %copy-start.12 = (s32[1,16,128]{2,1,0:T(8,128)S(1)}, s32[1,16,128]{2,1,0:T(8,128)}, u32[]{:S(2)}) copy-start(s32[1,16,128]{2,1,0:T(8,128)} %param.16) | copy-start | bytes 24580
  19.3 25.2 %all-to-all-start.1 = ((bf16[8,128,256]{2,1,0:T(8,128)(2,1)}), bf16[8,128,256]{2,1,0:T(8,128)(2,1)S(1)}, u32[]{:S(2)}, u32[]{:S(2)}) async-start(bf16[8,128,256]{2,1,0:T(8,128)(2,1)} %broadcast_in_dim.13), calls=%async_computation.1 | async-start | bytes 1048576 | tf_op jit(solution)/shard_map/all_to_all | solution.py:168
  29.3 85.1 %all-gather.2.cloned.1.call-start = ((), (), s32[]{:S(2)}) async-start(), calls=%async_computation.13 | async-start | bytes 2359296 | tf_op jit(solution)/shard_map/all_gather | solution.py:186
  84.9 3.8 %copy-start.7 = (bf16[256,256]{1,0:T(8,128)(2,1)S(1)}, bf16[256,256]{1,0:T(8,128)(2,1)}, u32[]{:S(2)}) copy-start(bf16[256,256]{1,0:T(8,128)(2,1)} %w_ref.3) | copy-start | bytes 393220
  84.9 3.8 %copy-start.21 = (f32[256]{0:T(256)S(1)}, f32[256]{0:T(256)}, u32[]{:S(2)}) copy-start(f32[256]{0:T(256)} %param.20) | copy-start | bytes 3076
  84.9 4.7 %copy-start = (bf16[256,2048]{1,0:T(8,128)(2,1)S(1)}, bf16[256,2048]{1,0:T(8,128)(2,1)}, u32[]{:S(2)}) copy-start(bf16[256,2048]{1,0:T(8,128)(2,1)} %cut_ref.1) | copy-start | bytes 3145732
  84.9 29.6 %all-to-all-start.2 = ((bf16[4,8,128,256]{3,2,1,0:T(8,128)(2,1)}), bf16[4,8,128,256]{3,2,1,0:T(8,128)(2,1)S(1)}, u32[]{:S(2)}, u32[]{:S(2)}) async-start(bf16[4,8,128,256]{3,2,1,0:T(8,128)(2,1)} %broadcast_in_dim.14), calls=%async_computation.2 | async-start | bytes 4194304 | tf_op jit(solution)/shard_map/all_to_all | solution.py:168
  88.7 25.8 %copy-start.14 = (s32[2,24]{1,0:T(2,128)S(1)}, s32[2,24]{1,0:T(2,128)}, u32[]{:S(2)}) copy-start(s32[2,24]{1,0:T(2,128)} %index_ref.3) | copy-start | bytes 580
  114.5 1.6 copy-start.1
  118.6 1.4 copy-start.17
  127.4 1.3 copy-start.3
  128.7 1.4 copy-start.4
  164.6 30.3 %all-to-all-start.6 = ((bf16[4,8,128,256]{3,2,1,0:T(8,128)(2,1)}), bf16[4,8,128,256]{3,2,1,0:T(8,128)(2,1)}, u32[]{:S(2)}, u32[]{:S(2)}) async-start(bf16[4,8,128,256]{3,2,1,0:T(8,128)(2,1)} %bitcast.19), calls=%async_computation.7 | async-start | bytes 4194304 | tf_op jit(solution)/shard_map/all_to_all | solution.py:168
  195.7 14.5 %all-to-all-start.10 = ((f32[8,40,256]{2,1,0:T(8,128)}), f32[8,40,256]{2,1,0:T(8,128)S(1)}, u32[]{:S(2)}, u32[]{:S(2)}) async-start(f32[8,40,256]{2,1,0:T(8,128)} %broadcast_in_dim.16), calls=%async_computation.11 | async-start | bytes 655360 | tf_op jit(solution)/shard_map/all_to_all | solution.py:168
  199.1 94.5 %reduce-scatter.2.cloned.1.call-start = ((), (), s32[]{:S(2)}) async-start(), calls=%async_computation.14 | async-start | bytes 2359296 | tf_op jit(solution)/shard_map/reduce_scatter | solution.py:210
  210.9 34.5 %all-to-all-start.4 = ((bf16[16,128,256]{2,1,0:T(8,128)(2,1)}), bf16[16,128,256]{2,1,0:T(8,128)(2,1)S(1)}, u32[]{:S(2)}, u32[]{:S(2)}) async-start(bf16[16,128,256]{2,1,0:T(8,128)(2,1)} %bitcast.20), calls=%async_computation.4 | async-start | bytes 2097152 | tf_op jit(solution)/shard_map/all_to_all | solution.py:168
  220.3 51.9 %copy-start.16 = (s32[2]{0:T(128)S(1)}, s32[2]{0:T(128)}, u32[]{:S(2)}) copy-start(s32[2]{0:T(128)} %count_ref.7) | copy-start | bytes 28
  245.4 21.4 %all-to-all-start.7 = ((bf16[8,128,256]{2,1,0:T(8,128)(2,1)}), bf16[8,128,256]{2,1,0:T(8,128)(2,1)}, u32[]{:S(2)}, u32[]{:S(2)}) async-start(bf16[8,128,256]{2,1,0:T(8,128)(2,1)} %reduce_sum.58), calls=%async_computation.8 | async-start | bytes 1048576 | tf_op jit(solution)/shard_map/all_to_all | solution.py:168
  267.8 24.6 %all-to-all-start.11 = ((f32[16,40,256]{2,1,0:T(8,128)}), f32[16,40,256]{2,1,0:T(8,128)}, u32[]{:S(2)}, u32[]{:S(2)}) async-start(f32[16,40,256]{2,1,0:T(8,128)} %broadcast_in_dim.17), calls=%async_computation.12 | async-start | bytes 1310720 | tf_op jit(solution)/shard_map/all_to_all | solution.py:168
  272.3 1.6 copy-start.2
  273.9 3.0 copy-start.11
  293.7 9.2 %all-to-all-start.5 = ((bf16[4,128,256]{2,1,0:T(8,128)(2,1)}), bf16[4,128,256]{2,1,0:T(8,128)(2,1)S(1)}, u32[]{:S(2)}, u32[]{:S(2)}) async-start(bf16[4,128,256]{2,1,0:T(8,128)(2,1)} %bitcast.25), calls=%async_computation.6 | async-start | bytes 524288 | tf_op jit(solution)/shard_map/all_to_all | solution.py:168
  (8 other events, 6.8 us)
Sparse Core Ops, SparseCore 0:
  32.3 42.1 all-gather.1
  202.8 36.9 reduce-scatter.1

commit v2 on v1

--- a/solution.py
+++ b/solution.py
@@ -52,27 +52,42 @@
         out_ref[g] = lax.dot_general(hot, feat, TN, preferred_element_type=F32).astype(BF)
 
 
-def place(index_ref, count_ref, t, k):
+def band_of(index_ref, t, k):
     index = index_ref[t, k]
     band = lax.shift_right_logical(index, 1)
-    even = (band & (NZ - 1)) * NX + lax.shift_right_logical(band, 3)
-    slot = jnp.where((index & 1) == 0, even, HALF + band)
-    return jnp.where(k < count_ref[t], slot, 2 * HALF)
-
-
-def main_body(
-    index_ref, count_ref, even_ref, odd_ref, blocks_ref, outer_ref, pre_ref, w_ref, dout_ref,
-    out_ref, dpre_ref, dagg_ref, agg_ref, teven_ref, todd_ref,
-    tiles, acc, sems,
-):
-    slots = blocks_ref.shape[1]
+    return lax.shift_right_logical(band, 3), band & (NZ - 1), index & 1
+
+
+def tile_spot(index_ref, count_ref, my_x, t, k):
+    x, z, odd = band_of(index_ref, t, k)
+    spot = jnp.where(odd == 0, z * NX + x, HALF + ((x - my_x) & (NX - 1)) * NZ + z)
+    return jnp.where(k < count_ref[t], spot, 2 * HALF)
+
+
+def term_spot(index_ref, count_ref, t, k):
+    x, z, odd = band_of(index_ref, t, k)
+    return jnp.where(k < count_ref[t], (z * NX + x) * 2 + odd, 2 * HALF)
+
+
+def fetch_tiles(sources, tiles, sems):
+    starts = (0, HALF, HALF + NZ, HALF + 2 * NZ, HALF + 2 * NZ + NZ // 2, HALF + 3 * NZ)
     copies = [
-        pltpu.make_async_copy(even_ref, tiles.at[pl.ds(0, HALF)], sems.at[0]),
-        pltpu.make_async_copy(odd_ref, tiles.at[pl.ds(HALF, HALF)], sems.at[1]),
+        pltpu.make_async_copy(source, tiles.at[pl.ds(start, source.shape[0])], sems.at[i])
+        for i, (source, start) in enumerate(zip(sources, starts, strict=True))
     ]
     for copy in copies:
         copy.start()
     tiles[2 * HALF] = jnp.zeros(tiles.shape[1:], BF)
+    return copies
+
+
+def main_body(
+    index_ref, count_ref, x_ref, s0, s1, s2, s3, s4, s5, blocks_ref, outer_ref, pre_ref, w_ref, dout_ref,
+    out_ref, dpre_ref, dagg_ref, agg_ref, term_ref,
+    tiles, acc, sems,
+):
+    slots = blocks_ref.shape[1]
+    copies = fetch_tiles((s0, s1, s2, s3, s4, s5), tiles, sems)
 
     def clear(i, carry):
         acc[i] = jnp.zeros(acc.shape[1:], F32)
@@ -81,13 +96,14 @@
     lax.fori_loop(0, 2 * HALF, clear, 0)
     for copy in copies:
         copy.wait()
-    where = [[place(index_ref, count_ref, t, k) for k in range(slots)] for t in range(2)]
+    my_x = x_ref[0]
     for t in range(2):
+        where = [tile_spot(index_ref, count_ref, my_x, t, k) for k in range(slots)]
         rows = pl.ds(t * 128, 128)
         total = outer_ref[rows, :]
         for k in range(0, slots, 2):
             left = jnp.concatenate([blocks_ref[t, k], blocks_ref[t, k + 1]], axis=1)
-            right = jnp.concatenate([tiles[where[t][k]], tiles[where[t][k + 1]]], axis=0)
+            right = jnp.concatenate([tiles[where[k]], tiles[where[k + 1]]], axis=0)
             total = total + jnp.dot(left, right, preferred_element_type=F32)
         agg = total.astype(BF)
         agg_ref[rows, :] = agg
@@ -99,16 +115,15 @@
         d_agg = lax.dot_general(d_pre, w_ref[...], NT, preferred_element_type=F32).astype(BF)
         dagg_ref[rows, :] = d_agg
         for k in range(slots):
-            spot = where[t][k]
+            spot = term_spot(index_ref, count_ref, t, k)
             term = lax.dot_general(blocks_ref[t, k], d_agg, TN, preferred_element_type=F32)
             acc[spot] = acc[spot] + term
 
     def store(i, carry):
-        teven_ref[i] = acc[i].astype(BF)
-        todd_ref[i] = acc[HALF + i].astype(BF)
+        term_ref[i] = acc[i].astype(BF)
         return carry
 
-    lax.fori_loop(0, HALF, store, 0)
+    lax.fori_loop(0, 2 * HALF, store, 0)
 
 
 def third_body(
@@ -134,20 +149,17 @@
         ).astype(BF)
 
 
-def blocks_body(index_ref, count_ref, even_ref, odd_ref, dagg_ref, out_ref, tiles, sems):
-    copies = [
-        pltpu.make_async_copy(even_ref, tiles.at[pl.ds(0, HALF)], sems.at[0]),
-        pltpu.make_async_copy(odd_ref, tiles.at[pl.ds(HALF, HALF)], sems.at[1]),
-    ]
-    for copy in copies:
-        copy.start()
-    tiles[2 * HALF] = jnp.zeros(tiles.shape[1:], BF)
+def blocks_body(
+    index_ref, count_ref, x_ref, s0, s1, s2, s3, s4, s5, dagg_ref, out_ref, tiles, sems
+):
+    copies = fetch_tiles((s0, s1, s2, s3, s4, s5), tiles, sems)
+    my_x = x_ref[0]
     for copy in copies:
         copy.wait()
     for t in range(2):
         d_agg = dagg_ref[pl.ds(t * 128, 128), :]
         for k in range(out_ref.shape[1]):
-            tile = tiles[place(index_ref, count_ref, t, k)]
+            tile = tiles[tile_spot(index_ref, count_ref, my_x, t, k)]
             out_ref[t, k] = lax.dot_general(
                 d_agg, tile, NT, preferred_element_type=F32
             ).astype(BF)
@@ -172,6 +184,10 @@
     return a2a(jnp.broadcast_to(x[None], (n, *x.shape)), axis)
 
 
+def shift(x, axis, n, by):
+    return lax.ppermute(x, axis, [(i, (i + by) % n) for i in range(n)])
+
+
 def local(
     features, block_index, block_count, block_values, cut_weight, send_rows, send_count,
     w_self, w_neigh, bias, d_out,
@@ -184,8 +200,13 @@
 
     even = spread(features[:128], "x", NX)
     even = lax.all_gather(even, "z", axis=0, tiled=True)
-    odd = spread(features[128:], "z", NZ)
-    odd = spread(odd, "x", NX).reshape(HALF, 128, width)
+    own = lax.all_gather(features[128:], "z", axis=0)
+    left = shift(own, "x", NX, 1)
+    right = shift(own, "x", NX, -1)
+    far_low = shift(left[: NZ // 2], "x", NX, 1)
+    far_high = shift(right[NZ // 2 :], "x", NX, -1)
+    gathered = (even, own, right, far_low, far_high, left)
+    my_x = lax.axis_index("x").astype(jnp.int32).reshape(1)
 
     outgoing = call(
         pick_body, sds((NG, cut, width), BF), [SMEM, VMEM, VMEM], VMEM,
@@ -196,24 +217,19 @@
     own_pre = jnp.dot(features, w_self, preferred_element_type=F32) + bias
 
     node_bf = sds((nodes, width), BF)
-    half_bf = sds((HALF, 128, width), BF)
-    gathered = pltpu.VMEM((2 * HALF + 1, 128, width), BF)
-    output, d_pre, d_agg, aggregate, t_even, t_odd = call(
+    tile_scratch = pltpu.VMEM((2 * HALF + 1, 128, width), BF)
+    copy_sems = pltpu.SemaphoreType.DMA((6,))
+    output, d_pre, d_agg, aggregate, terms = call(
         main_body,
-        (node_bf, node_bf, node_bf, node_bf, half_bf, half_bf),
-        [SMEM, SMEM, HBM, HBM, VMEM, VMEM, VMEM, VMEM, VMEM],
-        (VMEM,) * 6,
-        [gathered, pltpu.VMEM((2 * HALF + 1, 128, width), F32), pltpu.SemaphoreType.DMA((2,))],
+        (node_bf, node_bf, node_bf, node_bf, sds((2 * HALF, 128, width), BF)),
+        [SMEM] * 3 + [HBM] * 6 + [VMEM] * 5,
+        (VMEM,) * 5,
+        [tile_scratch, pltpu.VMEM((2 * HALF + 1, 128, width), F32), copy_sems],
         flops=2 << 30, nbytes=16 << 20, vmem=40,
-    )(block_index, block_count, even, odd, block_values, outer, own_pre, w_neigh, d_out)
-
-    t_even = lax.psum_scatter(t_even.reshape(NZ, NX * 128, width), "z", scatter_dimension=0)
-    t_odd = a2a(t_odd.reshape(NX, NZ, 128, width), "x")
-    t_odd = jnp.sum(t_odd.astype(F32), axis=0).astype(BF)
-    t_odd = a2a(t_odd, "z")
-    t_odd = jnp.sum(t_odd.astype(F32), axis=0)
-    t_even = a2a(t_even.reshape(NX, 128, width), "x")
-    t_even = jnp.sum(t_even.astype(F32), axis=0)
+    )(block_index, block_count, my_x, *gathered, block_values, outer, own_pre, w_neigh, d_out)
+
+    terms = lax.psum_scatter(terms.reshape(NZ, NX * nodes, width), "z", scatter_dimension=0)
+    terms = a2a(terms.reshape(NX, nodes, width), "x")
 
     back, part, self_back = call(
         third_body,
@@ -225,18 +241,20 @@
         base_body, sds((nodes, width), F32), [SMEM, VMEM, VMEM, VMEM], VMEM,
         flops=2 * NG * cut * width * nodes, nbytes=2 << 20,
     )(send_count, rows2, returned, self_back)
-    d_features = (base + jnp.concatenate([t_even, t_odd], axis=0)).astype(BF)
-
-    part = jnp.sum(a2a(part.reshape(NG, GRAD_ROWS, width), ("y", "c")), axis=0)
-    part = jnp.sum(spread(part, "x", NX), axis=0)
-    part = jnp.sum(spread(part, "z", NZ), axis=0) * scale
-    grads = spread(part, ("y", "c"), NG).reshape(-1, width)
+    d_features = (base + jnp.sum(terms.astype(F32), axis=0)).astype(BF)
+
+    part = jnp.sum(a2a(part.reshape(NC, NY * GRAD_ROWS, width), "c"), axis=0)
+    part = jnp.sum(a2a(part.reshape(NY, GRAD_ROWS, width), "y"), axis=0)
+    part = jnp.sum(lax.all_gather(part, "x", axis=0), axis=0)
+    part = jnp.sum(lax.all_gather(part, "z", axis=0), axis=0) * scale
+    part = lax.all_gather(part, "y", axis=0, tiled=True)
+    grads = lax.all_gather(part, "c", axis=0, tiled=True)
 
     grad_blocks = call(
-        blocks_body, sds(block_values.shape, BF), [SMEM, SMEM, HBM, HBM, VMEM], VMEM,
-        [gathered, pltpu.SemaphoreType.DMA((2,))],
+        blocks_body, sds(block_values.shape, BF), [SMEM] * 3 + [HBM] * 6 + [VMEM], VMEM,
+        [tile_scratch, copy_sems],
         flops=2 * tiles_here * slots * 128 * 128 * width, nbytes=6 << 20,
-    )(block_index, block_count, even, odd, d_agg)
+    )(block_index, block_count, my_x, *gathered, d_agg)
 
     return (
         output,

time: 312 us -> 230 us (0.74)
  waiting for transfers between devices: 132 us -> 6.62 us
  blocking collectives: 81.4 us -> 134 us
  starting transfers between devices: 40.4 us -> 32.1 us
  other arithmetic: 5.79 us -> 1.84 us
    all_to_all x8 -> x3, waiting for transfers between devices: 131 us -> 0.01 us  [a2a(): return lax.all_to_all(x, axis, 0, 0, tiled=True)]
    all_gather x0 -> x5, blocking collectives: none -> 95 us  [the longest x1 27.8 us: local(): own = lax.all_gather(features[128:], 'z', axis=0)]
    all_to_all x4 -> x3, blocking collectives: 81.4 us -> 39.4 us  [a2a(): return lax.all_to_all(x, axis, 0, 0, tiled=True)]
    all_to_all x8 -> x3, starting transfers between devices: 40.3 us -> 18.9 us  [a2a(): return lax.all_to_all(x, axis, 0, 0, tiled=True)]
    ppermute x0 -> x4, starting transfers between devices: none -> 13.1 us  [shift(): return lax.ppermute(x, axis, [(i, (i + by) % n) for i in range(n)])]
    ppermute x0 -> x4, waiting for transfers between devices: none -> 6.58 us  [shift(): return lax.ppermute(x, axis, [(i, (i + by) % n) for i in range(n)])]
    broadcast_in_dim x6 -> x1, local copies, waits for them, and re-layouts: 4.06 us -> 0.02 us  [spread(): return a2a(jnp.broadcast_to(x[None], (n, *x.shape)), axis)]
    reduce_sum x6 -> x5, other arithmetic: 5.1 us -> 1.15 us  [the longest x1 1 us: local(): part = jnp.sum(a2a(part.reshape(NY, GRAD_ROWS, width), 'y'), axis=0)]
  transfers between devices with their start and end apart: 10 -> 9, of which waited for: 8 -> 2; matrix products, arithmetic and copies ran while one was open for 4% -> 3% of each run, Pallas kernels for 2% -> 3%
where the time goes in v2:
time: 230 us; the launch traced here: 227 us
  blocking collectives  134 us (58%)
  starting transfers between devices  32.1 us (14%)
  local copies, waits for them, and re-layouts  21.3 us (9%)
  between operations  14.4 us (6%)
  Pallas kernels  13.6 us (6%)
  waiting for transfers between devices  6.62 us (3%)
  matrix products  2.61 us (1%)
    all_to_all x3, blocking collectives, a2a(): return lax.all_to_all(x, axis, 0, 0, tiled=True)  39.4 us
    all_gather x1, blocking collectives, local(): own = lax.all_gather(features[128:], 'z', axis=0)  27.8 us
    all_gather x1, blocking collectives, local(): part = lax.all_gather(part, 'y', axis=0, tiled=True)  20.6 us
    all_gather x1, blocking collectives, local(): part = jnp.sum(lax.all_gather(part, 'z', axis=0), axis=0) * scale  19.9 us
    all_to_all x3, starting transfers between devices, a2a(): return lax.all_to_all(x, axis, 0, 0, tiled=True)  18.9 us
    unnamed x60, local copies, waits for them, and re-layouts  17.4 us
    all_gather x1, blocking collectives, local(): grads = lax.all_gather(part, 'c', axis=0, tiled=True)  15.5 us
    ppermute x4, starting transfers between devices, shift(): return lax.ppermute(x, axis, [(i, (i + by) % n) for i in range(n)])  13.1 us
  transfers between devices with their start and end apart: 9, of which 2 were waited for; matrix products, arithmetic and copies ran while one was open for 3% of the time, Pallas kernels for 3%

profile of v2, /device:TPU:1, one launch (start us, length us, event | category | flops | bytes accessed | tf_op | source)
XLA Modules:
  0.0 226.8 jit_solution(1225556512892885622)
XLA Ops:
  8.1 10.3 %all_to_all.30 = bf16[4,128,256]{2,1,0:T(8,128)(2,1)} all-to-all(bf16[4,128,256]{2,1,0:T(8,128)(2,1)S(1)} %broadcast_in_dim.2), channel_id=1, replica_groups=mesh['y'=8,'c'=2,'x'=4,'z'=8] {'x'}, dimensions={0} | all-to-all | bytes 524288 | tf_op jit(solution)/shard_map/all_to_all | solution.py:180
  20.7 2.0 shard_map.154
  22.7 10.6 %all-to-all-start.1 = ((bf16[16,128,256]{2,1,0:T(8,128)(2,1)}), bf16[16,128,256]{2,1,0:T(8,128)(2,1)}, u32[]{:S(2)}, u32[]{:S(2)}) async-start(bf16[16,128,256]{2,1,0:T(8,128)(2,1)} %shard_map.154), calls=%async_computation.1 | async-start | bytes 2097152 | tf_op jit(solution)/shard_map/all_to_all | solution.py:180
  33.3 27.8 %all-gather = bf16[1024,256]{1,0:T(8,128)(2,1)S(1)} all-gather(bf16[128,256]{1,0:T(8,128)(2,1)S(1)} %get-tuple-element.24), channel_id=2, replica_groups=mesh['y'=8,'c'=2,'x'=4,'z'=8] {'z'}, dimensions={0}, use_global_device_ids=true | all-gather | bytes 589824 | tf_op jit(solution)/shard_map/all_gather | solution.py:203
  61.2 2.2 collective-permute-start.1
  63.4 4.4 %collective-permute-start = (bf16[8,128,256]{2,1,0:T(8,128)(2,1)S(1)}, bf16[8,128,256]{2,1,0:T(8,128)(2,1)S(1)}, u32[]{:S(2)}, u32[]{:S(2)}) collective-permute-start(bf16[8,128,256]{2,1,0:T(8,128)(2,1)S(1)} %bitcast.20), channel_id=1, source_target_pairs={{0,24},{8,0},{16,8},{24,16},{1,25},{9,1},{17,9},{25,17},{2,26},{10... | collective-permute-start | bytes 1572872 | tf_op jit(solution)/shard_map/ppermute | solution.py:188
  68.8 5.4 %collective-permute-done.1.s5 = bf16[8,128,256]{2,1,0:T(8,128)(2,1)S(1)} collective-permute-done((bf16[8,128,256]{2,1,0:T(8,128)(2,1)S(1)}, bf16[8,128,256]{2,1,0:T(8,128)(2,1)S(1)}, u32[]{:S(2)}, u32[]{:S(2)}) %collective-permute-start.1) | collective-permute-done | bytes 524320 | tf_op jit(solution)/shard_map/ppermute | solution.py:188
  74.9 1.9 collective-permute-start.2
  77.6 4.6 %collective-permute-start.3 = (bf16[4,128,256]{2,1,0:T(8,128)(2,1)}, bf16[4,128,256]{2,1,0:T(8,128)(2,1)}, u32[]{:S(2)}, u32[]{:S(2)}) collective-permute-start(bf16[4,128,256]{2,1,0:T(8,128)(2,1)} %slice.29), channel_id=1, source_target_pairs={{0,24},{8,0},{16,8},{24,16},{1,25},{9,1},{17,9},{25,17},{2,26},{10... | collective-permute-start | bytes 786440 | tf_op jit(solution)/shard_map/ppermute | solution.py:188
  82.2 1.7 convolution_bitcast_fusion.outer_ref
  84.6 1.2 collective-permute-done.3.s4
  85.8 1.6 copy-done.2
  89.3 1.4 copy-done.26
  92.5 6.1 %shard_map.155 = (bf16[256,256]{1,0:T(8,128)(2,1)}, bf16[256,256]{1,0:T(8,128)(2,1)S(1)}, bf16[256,256]{1,0:T(8,128)(2,1)S(1)}, bf16[256,256]{1,0:T(8,128)(2,1)S(1)}, bf16[64,128,256]{2,1,0:T(8,128)(2,1)S(1)}) custom-call(s32[2,24]{1,0:T(2,128)S(1)} %copy-done.24, s32[2]{0:T(128)S(1)} %copy-done.25, s32[1]{0:T(128)} %bitcast.x_ref, ...), custom_call_target="tpu_custom_call" | custom-call | flops 2147483648 | bytes 16777216 | tf_op jit(solution)/shard_map/pallas_call | solution.py:222
  98.7 2.0 copy-done
  102.9 9.6 %all_to_all.31 = f32[2,320,256]{2,1,0:T(8,128)S(1)} all-to-all(f32[2,320,256]{2,1,0:T(8,128)S(1)} %bitcast.24), channel_id=1, replica_groups=mesh['y'=8,'c'=2,'x'=4,'z'=8] {'c'}, dimensions={0} | all-to-all | bytes 1310720 | tf_op jit(solution)/shard_map/all_to_all | solution.py:180
  112.6 19.5 %all_to_all.32 = f32[8,40,256]{2,1,0:T(8,128)} all-to-all(f32[8,40,256]{2,1,0:T(8,128)S(1)} %bitcast.27), channel_id=1, replica_groups=mesh['y'=8,'c'=2,'x'=4,'z'=8] {'y'}, dimensions={0} | all-to-all | bytes 655360 | tf_op jit(solution)/shard_map/all_to_all | solution.py:180
  132.1 4.9 %all-to-all-start.2 = ((bf16[16,128,256]{2,1,0:T(8,128)(2,1)}), bf16[16,128,256]{2,1,0:T(8,128)(2,1)S(1)}, u32[]{:S(2)}, u32[]{:S(2)}) async-start(bf16[16,128,256]{2,1,0:T(8,128)(2,1)} %bitcast.23), calls=%async_computation.2 | async-start | bytes 2097152 | tf_op jit(solution)/shard_map/all_to_all | solution.py:180
  141.1 3.9 %shard_map.158 = bf16[2,24,128,128]{3,2,1,0:T(8,128)(2,1)} custom-call(s32[2,24]{1,0:T(2,128)S(1)} %copy-done.24, s32[2]{0:T(128)S(1)} %copy-done.25, s32[1]{0:T(128)} %bitcast.x_ref, bf16[32,128,256]{2,1,0:T(8,128)(2,1)S(1)} %copy-done.3, bf16[8,128,256]{2,1,0:T(8,128)(2,1)S(1)} %bitcast.22, bf16[8,128,256]{2,1,0:T(8,128)(2,1)S(1)} %copy-done.11, ...), custom_call_target="tpu_custom_call" | custom-call | flops 402653184 | bytes 6291456 | tf_op jit(solution)/shard_map/pallas_call | solution.py:253
  146.0 11.1 %all-gather.1 = f32[160,256]{1,0:T(8,128)S(1)} all-gather(f32[40,256]{1,0:T(8,128)S(1)} %reduce_sum.47), channel_id=3, replica_groups=mesh['y'=8,'c'=2,'x'=4,'z'=8] {'x'}, dimensions={0}, use_global_device_ids=true | all-gather | bytes 204800 | tf_op jit(solution)/shard_map/all_gather | solution.py:248
  157.2 19.9 %all-gather.2 = f32[320,256]{1,0:T(8,128)S(1)} all-gather(f32[40,256]{1,0:T(8,128)S(1)} %reduce_sum.48), channel_id=4, replica_groups=mesh['y'=8,'c'=2,'x'=4,'z'=8] {'z'}, dimensions={0}, use_global_device_ids=true | all-gather | bytes 368640 | tf_op jit(solution)/shard_map/all_gather | solution.py:249
  177.2 20.6 %all_gather.34 = f32[320,256]{1,0:T(8,128)S(1)} all-gather(f32[40,256]{1,0:T(8,128)S(1)} %broadcast_multiply_fusion), channel_id=1, replica_groups=mesh['y'=8,'c'=2,'x'=4,'z'=8] {'y'}, dimensions={0}, use_global_device_ids=true | all-gather | bytes 368640 | tf_op jit(solution)/shard_map/all_gather | solution.py:250
  197.8 3.5 %all-to-all-start.3 = ((bf16[4,256,256]{2,1,0:T(8,128)(2,1)}), bf16[4,256,256]{2,1,0:T(8,128)(2,1)S(1)}, u32[]{:S(2)}, u32[]{:S(2)}) async-start(bf16[4,256,256]{2,1,0:T(8,128)(2,1)} %bitcast.30), calls=%async_computation.4 | async-start | bytes 1048576 | tf_op jit(solution)/shard_map/all_to_all | solution.py:180
  201.2 15.5 %all_gather.35 = f32[640,256]{1,0:T(8,128)S(1)} all-gather(f32[320,256]{1,0:T(8,128)S(1)} %all_gather.34), channel_id=1, replica_groups=mesh['y'=8,'c'=2,'x'=4,'z'=8] {'c'}, dimensions={0}, use_global_device_ids=true | all-gather | bytes 983040 | tf_op jit(solution)/shard_map/all_gather | solution.py:251
  (84 shorter events, 20.8 us)
Async XLA Ops:
  7.2 78.7 %all-gather.5.cloned.1.call-start = ((), (), s32[]{:S(2)}) async-start(), calls=%async_computation.7 | async-start | bytes 2359296 | tf_op jit(solution)/shard_map/all_gather | solution.py:202
  18.4 49.4 %copy-start.5 = (bf16[256,256]{1,0:T(8,128)(2,1)S(1)}, bf16[256,256]{1,0:T(8,128)(2,1)}, u32[]{:S(2)}) copy-start(bf16[256,256]{1,0:T(8,128)(2,1)} %feat_ref.3) | copy-start | bytes 393220
  18.4 49.4 %copy-start.13 = (bf16[256,256]{1,0:T(8,128)(2,1)S(1)}, bf16[256,256]{1,0:T(8,128)(2,1)}, u32[]{:S(2)}) copy-start(bf16[256,256]{1,0:T(8,128)(2,1)} %w_ref.3) | copy-start | bytes 393220
  18.4 49.4 %copy-start.29 = (f32[256]{0:T(256)S(1)}, f32[256]{0:T(256)}, u32[]{:S(2)}) copy-start(f32[256]{0:T(256)} %param.20) | copy-start | bytes 3076
  22.7 59.5 %copy-start.1 = (bf16[256,2048]{1,0:T(8,128)(2,1)S(1)}, bf16[256,2048]{1,0:T(8,128)(2,1)}, u32[]{:S(2)}) copy-start(bf16[256,2048]{1,0:T(8,128)(2,1)} %cut_ref.1) | copy-start | bytes 3145732
  22.7 59.5 %all-to-all-start.1 = ((bf16[16,128,256]{2,1,0:T(8,128)(2,1)}), bf16[16,128,256]{2,1,0:T(8,128)(2,1)}, u32[]{:S(2)}, u32[]{:S(2)}) async-start(bf16[16,128,256]{2,1,0:T(8,128)(2,1)} %shard_map.154), calls=%async_computation.1 | async-start | bytes 2097152 | tf_op jit(solution)/shard_map/all_to_all | solution.py:180
  33.3 164.5 %reduce-scatter.2.cloned.1.call-start = ((), (), s32[]{:S(2)}) async-start(), calls=%async_computation.8 | async-start | bytes 4718592 | tf_op jit(solution)/shard_map/reduce_scatter | solution.py:231
  61.2 37.5 %copy-start.6 = (bf16[1024,256]{1,0:T(8,128)(2,1)}, bf16[1024,256]{1,0:T(8,128)(2,1)S(1)}, u32[]{:S(2)}) copy-start(bf16[1024,256]{1,0:T(8,128)(2,1)S(1)} %all-gather) | copy-start | bytes 1572868
  61.2 24.7 %copy-start.24 = (s32[2,24]{1,0:T(2,128)S(1)}, s32[2,24]{1,0:T(2,128)}, u32[]{:S(2)}) copy-start(s32[2,24]{1,0:T(2,128)} %index_ref.3) | copy-start | bytes 580
  61.2 24.7 %copy-start.25 = (s32[2]{0:T(128)S(1)}, s32[2]{0:T(128)}, u32[]{:S(2)}) copy-start(s32[2]{0:T(128)} %count_ref.7) | copy-start | bytes 28
  61.2 13.0 %collective-permute-start.1 = (bf16[8,128,256]{2,1,0:T(8,128)(2,1)S(1)}, bf16[8,128,256]{2,1,0:T(8,128)(2,1)S(1)}, u32[]{:S(2)}, u32[]{:S(2)}) collective-permute-start(bf16[8,128,256]{2,1,0:T(8,128)(2,1)S(1)} %bitcast.19), channel_id=1, source_target_pairs={{0,8},{8,16},{16,24},{24,0},{1,9},{9,17},{17,25},{25,1},{2,10},{10... | collective-permute-start | bytes 1572872 | tf_op jit(solution)/shard_map/ppermute | solution.py:188
  63.4 13.5 %collective-permute-start = (bf16[8,128,256]{2,1,0:T(8,128)(2,1)S(1)}, bf16[8,128,256]{2,1,0:T(8,128)(2,1)S(1)}, u32[]{:S(2)}, u32[]{:S(2)}) collective-permute-start(bf16[8,128,256]{2,1,0:T(8,128)(2,1)S(1)} %bitcast.20), channel_id=1, source_target_pairs={{0,24},{8,0},{16,8},{24,16},{1,25},{9,1},{17,9},{25,17},{2,26},{10... | collective-permute-start | bytes 1572872 | tf_op jit(solution)/shard_map/ppermute | solution.py:188
  74.2 24.5 %copy-start.8 = (bf16[8,128,256]{2,1,0:T(8,128)(2,1)}, bf16[8,128,256]{2,1,0:T(8,128)(2,1)S(1)}, u32[]{:S(2)}) copy-start(bf16[8,128,256]{2,1,0:T(8,128)(2,1)S(1)} %collective-permute-done.1.s5) | copy-start | bytes 1572868
  74.9 9.0 %collective-permute-start.2 = (bf16[4,128,256]{2,1,0:T(8,128)(2,1)}, bf16[4,128,256]{2,1,0:T(8,128)(2,1)S(1)}, u32[]{:S(2)}, u32[]{:S(2)}) collective-permute-start(bf16[4,128,256]{2,1,0:T(8,128)(2,1)} %slice.28), channel_id=1, source_target_pairs={{0,8},{8,16},{16,24},{24,0},{1,9},{9,17},{17,25},{25,1},{2,10},{10... | collective-permute-start | bytes 786440 | tf_op jit(solution)/shard_map/ppermute | solution.py:188
  76.9 21.8 %copy-start.10 = (bf16[8,128,256]{2,1,0:T(8,128)(2,1)}, bf16[8,128,256]{2,1,0:T(8,128)(2,1)S(1)}, u32[]{:S(2)}) copy-start(bf16[8,128,256]{2,1,0:T(8,128)(2,1)S(1)} %collective-permute-done.s2) | copy-start | bytes 1572868
  77.6 8.2 %collective-permute-start.3 = (bf16[4,128,256]{2,1,0:T(8,128)(2,1)}, bf16[4,128,256]{2,1,0:T(8,128)(2,1)}, u32[]{:S(2)}, u32[]{:S(2)}) collective-permute-start(bf16[4,128,256]{2,1,0:T(8,128)(2,1)} %slice.29), channel_id=1, source_target_pairs={{0,24},{8,0},{16,8},{24,16},{1,25},{9,1},{17,9},{25,17},{2,26},{10... | collective-permute-start | bytes 786440 | tf_op jit(solution)/shard_map/ppermute | solution.py:188
  85.8 1.6 copy-start.2
  98.7 2.0 copy-start
  112.5 24.5 %copy-start.3 = (bf16[32,128,256]{2,1,0:T(8,128)(2,1)S(1)}, bf16[32,128,256]{2,1,0:T(8,128)(2,1)}, u32[]{:S(2)}) copy-start(bf16[32,128,256]{2,1,0:T(8,128)(2,1)} %all-gather.5.cloned.1.call-done.s0) | copy-start | bytes 6291460
  132.1 65.7 %all-to-all-start.2 = ((bf16[16,128,256]{2,1,0:T(8,128)(2,1)}), bf16[16,128,256]{2,1,0:T(8,128)(2,1)S(1)}, u32[]{:S(2)}, u32[]{:S(2)}) async-start(bf16[16,128,256]{2,1,0:T(8,128)(2,1)} %bitcast.23), calls=%async_computation.2 | async-start | bytes 2097152 | tf_op jit(solution)/shard_map/all_to_all | solution.py:180
  157.2 61.0 %copy-start.16 = (f32[256,256]{1,0:T(8,128)S(1)}, f32[256,256]{1,0:T(8,128)}, u32[]{:S(2)}) copy-start(f32[256,256]{1,0:T(8,128)} %copy-done.15) | copy-start | bytes 786436
  157.2 61.0 %copy-start.21 = (s32[1,16,128]{2,1,0:T(8,128)S(1)}, s32[1,16,128]{2,1,0:T(8,128)}, u32[]{:S(2)}) copy-start(s32[1,16,128]{2,1,0:T(8,128)} %param.16) | copy-start | bytes 24580
  157.2 61.0 %copy-start.23 = (s32[1,16]{1,0:T(1,128)S(1)}, s32[1,16]{1,0:T(1,128)}, u32[]{:S(2)}) copy-start(s32[1,16]{1,0:T(1,128)} %count_ref.6) | copy-start | bytes 196
  197.8 21.4 %all-to-all-start.3 = ((bf16[4,256,256]{2,1,0:T(8,128)(2,1)}), bf16[4,256,256]{2,1,0:T(8,128)(2,1)S(1)}, u32[]{:S(2)}, u32[]{:S(2)}) async-start(bf16[4,256,256]{2,1,0:T(8,128)(2,1)} %bitcast.30), calls=%async_computation.4 | async-start | bytes 1048576 | tf_op jit(solution)/shard_map/all_to_all | solution.py:180
  (15 other events, 13.9 us)
Sparse Core Ops, SparseCore 0:
  18.6 47.7 all-gather.4
  100.8 62.5 reduce-scatter.1

commit v3 on v2

v3 whole, which is shorter than its diff:
```python
import math

import jax
import jax.numpy as jnp
from jax import lax
from jax.experimental import pallas as pl
from jax.experimental.pallas import tpu as pltpu
from jax.sharding import Mesh, PartitionSpec as P

BF = jnp.bfloat16
F32 = jnp.float32
TN = (((0,), (0,)), ((), ()))
NT = (((1,), (1,)), ((), ()))
NX, NZ, NY, NC = 4, 8, 8, 2
NG = NY * NC
BANDS = NX * NZ
GRAD_ROWS = 40
STORE = 8
VMEM = pl.BlockSpec(memory_space=pltpu.VMEM)
SMEM = pl.BlockSpec(memory_space=pltpu.SMEM)
HBM = pl.BlockSpec(memory_space=pl.ANY)


def sds(shape, dtype):
    return jax.ShapeDtypeStruct(shape, dtype)


def call(body, scalars, arrays, outs, out_specs=None, scratch=(), extra=(), flops=0, vmem=24):
    count, first = len(arrays), len(scalars)

    def kernel(*refs):
        sources = refs[first : first + count]
        rest = refs[first + count + len(extra) :]
        outputs, rest = rest[: len(outs)], rest[len(outs) :]
        buffers, sems, rest = rest[:count], rest[count], rest[count + 1 :]
        copies = [
            pltpu.make_async_copy(source, buffer, sems.at[i])
            for i, (source, buffer) in enumerate(zip(sources, buffers, strict=True))
        ]
        for copy in copies:
            copy.start()
        body(refs[:first], buffers, copies, outputs, *rest)

    nbytes = sum(a.size * a.dtype.itemsize for a in (*arrays, *outs))
    return pl.pallas_call(
        kernel,
        out_shape=tuple(outs),
        in_specs=[SMEM] * first + [HBM] * (count + len(extra)),
        out_specs=tuple(out_specs or [VMEM] * len(outs)),
        scratch_shapes=[
            *(pltpu.VMEM(a.shape, a.dtype) for a in arrays),
            pltpu.SemaphoreType.DMA((count,)),
            *scratch,
        ],
        compiler_params=pltpu.CompilerParams(vmem_limit_bytes=vmem << 20),
        cost_estimate=pl.CostEstimate(flops=flops, bytes_accessed=nbytes, transcendentals=0),
    )(*scalars, *arrays, *extra)


def wait(copies):
    for copy in copies:
        copy.wait()


def hot_columns(rows_ref, count_ref, g, nodes):
    rows = rows_ref[g : g + 1, :]
    lane = lax.broadcasted_iota(jnp.int32, rows.shape, 1)
    rows = jnp.where(lane < count_ref[0, g], rows, -1)
    node = lax.broadcasted_iota(jnp.int32, (nodes, rows.shape[1]), 0)
    return jnp.where(node == rows, 1.0, 0.0).astype(BF)


def pick_body(scalars, arrays, copies, outs):
    (count_ref,), (rows_ref, feat_ref), (out_ref,) = scalars, arrays, outs
    wait(copies)
    feat = feat_ref[...]
    for g in range(out_ref.shape[0]):
        hot = hot_columns(rows_ref, count_ref, g, feat.shape[0])
        out_ref[g] = lax.dot_general(hot, feat, TN, preferred_element_type=F32).astype(BF)


def spot_of(index_ref, count_ref, t, k):
    index = index_ref[t, k]
    z, x = lax.shift_right_logical(index, 1) & (NZ - 1), lax.shift_right_logical(index, 4)
    return jnp.where(k < count_ref[t], (z * NX + x) * 2 + (index & 1), 2 * BANDS)


def main_body(scalars, arrays, copies, outs, tiles, acc, terms, tile_sem, term_sems):
    index_ref, count_ref = scalars
    blocks_ref, outer_ref, pre_ref, w_ref, dout_ref = arrays[:5]
    out_ref, dpre_ref, dagg_ref, agg_ref, term_ref = outs
    slots = blocks_ref.shape[1]
    spare = 2 * BANDS
    tiles[spare] = jnp.zeros(tiles.shape[1:], BF)

    def clear(i, carry):
        acc[i] = jnp.zeros(acc.shape[1:], F32)
        return carry

    lax.fori_loop(0, spare, clear, 0)
    wait(copies)
    for t in range(2):
        rows = pl.ds(t * 128, 128)
        spots = [spot_of(index_ref, count_ref, t, k) for k in range(slots)]
        total = outer_ref[rows, :]
        for k in range(0, slots, 2):
            left = jnp.concatenate([blocks_ref[t, k], blocks_ref[t, k + 1]], axis=1)
            right = jnp.concatenate([tiles[spots[k]], tiles[spots[k + 1]]], axis=0)
            total = total + jnp.dot(left, right, preferred_element_type=F32)
        agg = total.astype(BF)
        agg_ref[rows, :] = agg
        pre = pre_ref[rows, :] + jnp.dot(agg, w_ref[...], preferred_element_type=F32)
        sig = jax.nn.sigmoid(pre)
        out_ref[rows, :] = (pre * sig).astype(BF)
        d_pre = (dout_ref[rows, :].astype(F32) * sig * (1.0 + pre * (1.0 - sig))).astype(BF)
        dpre_ref[rows, :] = d_pre
        d_agg = lax.dot_general(d_pre, w_ref[...], NT, preferred_element_type=F32).astype(BF)
        dagg_ref[rows, :] = d_agg
        for k in range(slots):
            term = lax.dot_general(blocks_ref[t, k], d_agg, TN, preferred_element_type=F32)
            acc[spots[k]] = acc[spots[k]] + term
    stores = []
    for c in range(STORE):
        part = pl.ds(c * (spare // STORE), spare // STORE)

        def convert(i, carry):
            terms[i] = acc[i].astype(BF)
            return carry

        lax.fori_loop(part.start, part.start + part.size, convert, 0)
        store = pltpu.make_async_copy(terms.at[part], term_ref.at[part], term_sems.at[c])
        store.start()
        stores.append(store)
    wait(stores)


def main_kernel(scalars, arrays, gathered, outs):
    count = len(arrays)

    def kernel(*refs):
        scalar_refs, refs = refs[:2], refs[2:]
        sources, gathered_ref, refs = refs[:count], refs[count], refs[count + 1 :]
        outputs, refs = refs[: len(outs)], refs[len(outs) :]
        buffers, (sems, tiles, acc, terms, tile_sem, term_sems) = refs[:count], refs[count:]
        copies = [pltpu.make_async_copy(gathered_ref, tiles.at[pl.ds(0, 2 * BANDS)], tile_sem)] + [
            pltpu.make_async_copy(source, buffer, sems.at[i])
            for i, (source, buffer) in enumerate(zip(sources, buffers, strict=True))
        ]
        for copy in copies:
            copy.start()
        main_body(scalar_refs, buffers, copies, outputs, tiles, acc, terms, tile_sem, term_sems)

    shape = (2 * BANDS + 1, *gathered.shape[1:])
    return pl.pallas_call(
        kernel,
        out_shape=tuple(outs),
        in_specs=[SMEM] * 2 + [HBM] * (count + 1),
        out_specs=(VMEM,) * (len(outs) - 1) + (HBM,),
        scratch_shapes=[
            *(pltpu.VMEM(a.shape, a.dtype) for a in arrays),
            pltpu.SemaphoreType.DMA((count,)),
            pltpu.VMEM(shape, BF),
            pltpu.VMEM(shape, F32),
            pltpu.VMEM(gathered.shape, BF),
            pltpu.SemaphoreType.DMA,
            pltpu.SemaphoreType.DMA((STORE,)),
        ],
        compiler_params=pltpu.CompilerParams(vmem_limit_bytes=40 << 20),
        cost_estimate=pl.CostEstimate(flops=1 << 30, bytes_accessed=12 << 20, transcendentals=0),
    )(*scalars, *arrays, gathered)


def third_body(scalars, arrays, copies, outs):
    dpre_ref, agg_ref, feat_ref, w_ref = arrays
    part_ref, self_ref = outs
    wait(copies)
    d_pre = dpre_ref[...]
    width = d_pre.shape[1]
    part_ref[pl.ds(0, width), :] = lax.dot_general(
        feat_ref[...], d_pre, TN, preferred_element_type=F32
    )
    part_ref[pl.ds(width, width), :] = lax.dot_general(
        agg_ref[...], d_pre, TN, preferred_element_type=F32
    )
    rest = part_ref.shape[0] - 2 * width
    row = lax.broadcasted_iota(jnp.int32, (rest, width), 0)
    bias = jnp.sum(d_pre.astype(F32), axis=0, keepdims=True)
    part_ref[pl.ds(2 * width, rest), :] = jnp.where(row == 0, bias, 0.0)
    self_ref[...] = lax.dot_general(d_pre, w_ref[...], NT, preferred_element_type=F32)


def back_body(scalars, arrays, copies, outs):
    (cut_ref, dagg_ref), (back_ref,) = arrays, outs
    wait(copies)
    d_agg = dagg_ref[...]
    cut = back_ref.shape[1]
    for g in range(0, back_ref.shape[0], 2):
        rows = lax.dot_general(
            cut_ref[:, pl.ds(g * cut, 2 * cut)], d_agg, TN, preferred_element_type=F32
        ).astype(BF)
        back_ref[g] = rows[:cut]
        back_ref[g + 1] = rows[cut:]


def blocks_body(scalars, arrays, copies, outs):
    (index_ref, count_ref), (tiles, dagg_ref), (out_ref,) = scalars, arrays, outs
    wait(copies)
    for t in range(2):
        d_agg = dagg_ref[pl.ds(t * 128, 128), :]
        for k in range(out_ref.shape[1]):
            live = k < count_ref[t]
            spot = jnp.where(live, spot_of(index_ref, count_ref, t, k), 0)

            @pl.when(live)
            def _(t=t, k=k, spot=spot, d_agg=d_agg):
                out_ref[t, k] = lax.dot_general(
                    d_agg, tiles[spot], NT, preferred_element_type=F32
                ).astype(BF)

            @pl.when(jnp.logical_not(live))
            def _(t=t, k=k):
                out_ref[t, k] = jnp.zeros(out_ref.shape[2:], BF)


def base_body(scalars, arrays, copies, outs):
    (count_ref,), (rows_ref, back_ref, self_ref), (out_ref,) = scalars, arrays, outs
    wait(copies)
    total = self_ref[...]
    for g in range(0, back_ref.shape[0], 2):
        hot = jnp.concatenate(
            [hot_columns(rows_ref, count_ref, g + i, total.shape[0]) for i in range(2)], axis=1
        )
        rows = jnp.concatenate([back_ref[g], back_ref[g + 1]], axis=0)
        total = total + jnp.dot(hot, rows, preferred_element_type=F32)
    out_ref[...] = total


def a2a(x, axis):
    return lax.all_to_all(x, axis, 0, 0, tiled=True)


def spread(x, axis, n):
    return a2a(jnp.broadcast_to(x[None], (n, *x.shape)), axis)


def shift(x, axis, n, by):
    return lax.ppermute(x, axis, [(i, (i + by) % n) for i in range(n)])


def local(
    features, block_index, block_count, block_values, cut_weight, send_rows, send_count,
    w_self, w_neigh, bias, d_out,
):
    nodes, width = features.shape
    tiles_here, slots = block_index.shape
    scale = 1.0 / math.sqrt(nodes * NG * BANDS)
    rows2 = send_rows.reshape(NG, -1)
    cut = rows2.shape[1]
    node_bf, node_f32 = sds((nodes, width), BF), sds((nodes, width), F32)
    cut_bf = sds((NG, cut, width), BF)

    gathered = lax.all_gather(features, "x", axis=0, tiled=True)
    gathered = lax.all_gather(gathered, "z", axis=0, tiled=True).reshape(2 * BANDS, 128, width)

    (outgoing,) = call(
        pick_body, [send_count], [rows2, features], [cut_bf], flops=2 * NG * cut * width * nodes
    )
    arrived = a2a(outgoing, ("y", "c")).reshape(NG * cut, width)
    outer = jnp.dot(cut_weight, arrived, preferred_element_type=F32)
    own_pre = jnp.dot(features, w_self, preferred_element_type=F32) + bias

    output, d_pre, d_agg, aggregate, terms = main_kernel(
        [block_index, block_count],
        [block_values, outer, own_pre, w_neigh, d_out],
        gathered,
        [node_bf, node_bf, node_bf, node_bf, sds(gathered.shape, BF)],
    )

    terms = lax.psum_scatter(terms.reshape(NZ, NX * nodes, width), "z", scatter_dimension=0)
    terms = terms.reshape(NX, nodes, width)
    me = lax.axis_index("x")
    own_back = lax.dynamic_index_in_dim(terms, me, 0, keepdims=False).astype(F32)
    for by in range(1, NX):
        away = lax.dynamic_index_in_dim(terms, (me + by) & (NX - 1), 0, keepdims=False)
        own_back = own_back + shift(away, "x", NX, by).astype(F32)

    part, self_back = call(
        third_body, [], [d_pre, aggregate, features, w_self],
        [sds((NG * GRAD_ROWS, width), F32), node_f32], flops=100 << 20,
    )
    part = jnp.sum(a2a(part.reshape(NC, NY * GRAD_ROWS, width), "c"), axis=0)
    part = jnp.sum(a2a(part.reshape(NY, GRAD_ROWS, width), "y"), axis=0)
    part = jnp.sum(spread(part, "x", NX), axis=0)
    part = jnp.sum(spread(part, "z", NZ), axis=0) * scale

    (back,) = call(
        back_body, [], [cut_weight, d_agg], [cut_bf], extra=[part],
        flops=2 * NG * cut * width * nodes,
    )
    returned = a2a(back, ("y", "c"))
    part = lax.all_gather(part, "y", axis=0, tiled=True)
    grads = lax.all_gather(part, "c", axis=0, tiled=True)
    (base,) = call(
        base_body, [send_count], [rows2, returned, self_back], [node_f32],
        flops=2 * NG * cut * width * nodes,
    )
    d_features = (base + own_back).astype(BF)

    (grad_blocks,) = call(
        blocks_body, [block_index, block_count], [gathered, d_agg], [sds(block_values.shape, BF)],
        extra=[part], flops=2 * tiles_here * slots * 128 * 128 * width,
    )

    return (
        output,
        d_features,
        grad_blocks,
        grads[:width],
        grads[width : 2 * width],
        grads[2 * width],
    )


def solution(mesh):
    mesh = Mesh(mesh.devices.reshape(NY, NC, NX, NZ), ("y", "c", "x", "z"))
    rows = ("y", "c", "x", "z")
    split = [P(rows)] * 7 + [P()] * 3 + [P(rows)]
    return jax.shard_map(
        local,
        mesh=mesh,
        in_specs=tuple(split),
        out_specs=(P(rows), P(rows), P(rows), P(), P(), P()),
        check_vma=False,
    )
```

time: 230 us -> 242 us (1.052); the launches traced: 227 us -> 242 us
  waiting for transfers between devices: 6.62 us -> 45 us
  blocking collectives: 134 us -> 114 us
  Pallas kernels: 13.6 us -> 21.2 us
  local copies, waits for them, and re-layouts: 21.3 us -> 15.2 us
  starting transfers between devices: 32.1 us -> 27.7 us
    all_gather x3 -> x1, blocking collectives: 58.9 us -> 13.5 us  [local(): gathered = lax.all_gather(features, 'x', axis=0, tiled=True)]
    all_to_all x3 -> x2, waiting for transfers between devices: 0.01 us -> 26.9 us  [a2a(): return lax.all_to_all(x, axis, 0, 0, tiled=True)]
    all_gather x1, blocking collectives: 20.6 us -> 40.5 us  [local(): part = lax.all_gather(part, 'y', axis=0, tiled=True)]
    all_gather x1, waiting for transfers between devices: 0.01 us -> 18.1 us  [local(): lax.all_gather(gathered, 'z', axis=0, tiled=True)]
    all_to_all x3 -> x4, blocking collectives: 39.4 us -> 51.7 us  [a2a(): return lax.all_to_all(x, axis, 0, 0, tiled=True)]
    pallas_call x5 -> x6, Pallas kernels: 13.6 us -> 21.2 us  [the longest x5 14.7 us: call(): pl.pallas_call(kernel, out_shape=tuple(outs), in_specs=[SMEM] * first + [...]
    all_gather x1, blocking collectives: 15.5 us -> 8.06 us  [local(): grads = lax.all_gather(part, 'c', axis=0, tiled=True)]
    ppermute x4 -> x3, waiting for transfers between devices: 6.58 us -> 0.01 us  [shift(): return lax.ppermute(x, axis, [(i, (i + by) % n) for i in range(n)])]
  transfers between devices with their start and end apart: 9 -> 7, of which waited for: 2 -> 2; matrix products, arithmetic and copies ran while one was open for 3% -> 2% of each run, Pallas kernels for 3% -> 6%
where the time goes in v3:
time: 242 us
  blocking collectives  114 us (47%)
  waiting for transfers between devices  45 us (19%)
  starting transfers between devices  27.7 us (11%)
  Pallas kernels  21.2 us (9%)
  local copies, waits for them, and re-layouts  15.2 us (6%)
  between operations  14.3 us (6%)
  matrix products  2.77 us (1%)
    all_to_all x4, blocking collectives, a2a(): return lax.all_to_all(x, axis, 0, 0, tiled=True)  51.7 us
    all_gather x1, blocking collectives, local(): part = lax.all_gather(part, 'y', axis=0, tiled=True)  40.5 us
    all_to_all x2, waiting for transfers between devices, a2a(): return lax.all_to_all(x, axis, 0, 0, tiled=True)  26.9 us
    all_to_all x2, starting transfers between devices, a2a(): return lax.all_to_all(x, axis, 0, 0, tiled=True)  19.2 us
    all_gather x1, waiting for transfers between devices, local(): lax.all_gather(gathered, 'z', axis=0, tiled=True)  18.1 us
    pallas_call x5, Pallas kernels, call(): pl.pallas_call(kernel, out_shape=tuple(outs), in_specs=[SMEM] * first + [...  14.7 us
    all_gather x1, blocking collectives, local(): gathered = lax.all_gather(features, 'x', axis=0, tiled=True)  13.5 us
    unnamed x42, local copies, waits for them, and re-layouts  12.7 us
  transfers between devices with their start and end apart: 7, of which 2 were waited for; matrix products, arithmetic and copies ran while one was open for 2% of the time, Pallas kernels for 6%

profile of v3, /device:TPU:1, one launch (start us, length us, event | category | flops | bytes accessed | tf_op | source)
XLA Modules:
  0.0 241.6 jit_solution(89784552575721462)
XLA Ops:
  7.3 13.5 %all_gather.12 = bf16[1024,256]{1,0:T(8,128)(2,1)} all-gather(bf16[256,256]{1,0:T(8,128)(2,1)} %refs_2_.5), channel_id=1, replica_groups=mesh['y'=8,'c'=2,'x'=4,'z'=8] {'x'}, dimensions={0}, use_global_device_ids=true | all-gather | bytes 655360 | tf_op jit(solution)/shard_map/all_gather | solution.py:262
  23.0 2.2 shard_map.154
  25.2 11.7 %all-to-all-start = ((bf16[16,128,256]{2,1,0:T(8,128)(2,1)}), bf16[16,128,256]{2,1,0:T(8,128)(2,1)}, u32[]{:S(2)}, u32[]{:S(2)}) async-start(bf16[16,128,256]{2,1,0:T(8,128)(2,1)} %shard_map.154), calls=%async_computation | async-start | bytes 2097152 | tf_op jit(solution)/shard_map/all_to_all | solution.py:239
  38.1 26.9 %all-to-all-done = bf16[16,128,256]{2,1,0:T(8,128)(2,1)} async-done(((bf16[16,128,256]{2,1,0:T(8,128)(2,1)}), bf16[16,128,256]{2,1,0:T(8,128)(2,1)}, u32[]{:S(2)}, u32[]{:S(2)}) %all-to-all-start) | async-done | bytes 1048608 | tf_op jit(solution)/shard_map/all_to_all | solution.py:239
  65.0 1.7 convolution_bitcast_fusion.refs_3_
  66.7 18.1 %all-gather.2.cloned.1.call-done = bf16[8192,256]{1,0:T(8,128)(2,1)} async-done(((bf16[1024,256]{1,0:T(8,128)(2,1)}), bf16[8192,256]{1,0:T(8,128)(2,1)}) %all-gather.2.cloned.1.call-update) | async-done | bytes 4194320 | tf_op jit(solution)/shard_map/all_gather | solution.py:263
  84.8 2.2 copy-done
  88.8 6.6 %shard_map.155 = (bf16[256,256]{1,0:T(8,128)(2,1)}, bf16[256,256]{1,0:T(8,128)(2,1)S(1)}, bf16[256,256]{1,0:T(8,128)(2,1)S(1)}, bf16[256,256]{1,0:T(8,128)(2,1)S(1)}, bf16[64,128,256]{2,1,0:T(8,128)(2,1)S(1)}) custom-call(s32[2,24]{1,0:T(2,128)S(1)} %copy-done.16, s32[2]{0:T(128)S(1)} %copy-done.19, bf16[2,24,128,128]{3,2,1,0:T(8,128)(2,1)S(1)} %copy-done.6, ...), custom_call_target="tpu_custom_call" | custom-call | flops 1073741824 | bytes 12582912 | tf_op jit(solution)/shard_map/pallas_call | solution.py:154
  95.4 2.0 copy-done.2
  100.6 4.6 %all_to_all.30 = f32[2,320,256]{2,1,0:T(8,128)S(1)} all-to-all(f32[2,320,256]{2,1,0:T(8,128)S(1)} %bitcast.26), channel_id=1, replica_groups=mesh['y'=8,'c'=2,'x'=4,'z'=8] {'c'}, dimensions={0} | all-to-all | bytes 1310720 | tf_op jit(solution)/shard_map/all_to_all | solution.py:239
  105.2 19.0 %all_to_all.31 = f32[8,40,256]{2,1,0:T(8,128)S(1)} all-to-all(f32[8,40,256]{2,1,0:T(8,128)S(1)} %bitcast.29), channel_id=1, replica_groups=mesh['y'=8,'c'=2,'x'=4,'z'=8] {'y'}, dimensions={0} | all-to-all | bytes 655360 | tf_op jit(solution)/shard_map/all_to_all | solution.py:239
  124.3 8.8 %all_to_all.32 = f32[4,40,256]{2,1,0:T(8,128)S(1)} all-to-all(f32[4,40,256]{2,1,0:T(8,128)S(1)} %broadcast_in_dim.4), channel_id=1, replica_groups=mesh['y'=8,'c'=2,'x'=4,'z'=8] {'x'}, dimensions={0} | all-to-all | bytes 327680 | tf_op jit(solution)/shard_map/all_to_all | solution.py:239
  133.2 19.3 %all_to_all.33 = f32[8,40,256]{2,1,0:T(8,128)S(1)} all-to-all(f32[8,40,256]{2,1,0:T(8,128)S(1)} %broadcast_in_dim.5), channel_id=1, replica_groups=mesh['y'=8,'c'=2,'x'=4,'z'=8] {'z'}, dimensions={0} | all-to-all | bytes 655360 | tf_op jit(solution)/shard_map/all_to_all | solution.py:239
  152.5 1.8 shard_map.157
  154.3 7.4 %all-to-all-start.5 = ((bf16[16,128,256]{2,1,0:T(8,128)(2,1)}), bf16[16,128,256]{2,1,0:T(8,128)(2,1)S(1)}, u32[]{:S(2)}, u32[]{:S(2)}) async-start(bf16[16,128,256]{2,1,0:T(8,128)(2,1)} %shard_map.157), calls=%async_computation.5 | async-start | bytes 2097152 | tf_op jit(solution)/shard_map/all_to_all | solution.py:239
  161.8 40.5 %all_gather.14.refs_4_ = f32[320,256]{1,0:T(8,128)S(1)} all-gather(f32[40,256]{1,0:T(8,128)S(1)} %broadcast_multiply_fusion.refs_2_), channel_id=1, replica_groups=mesh['y'=8,'c'=2,'x'=4,'z'=8] {'y'}, dimensions={0}, use_global_device_ids=true | all-gather | bytes 368640 | tf_op jit(solution)/shard_map/all_gather | solution.py:301
  202.2 8.1 %all_gather.15 = f32[640,256]{1,0:T(8,128)S(1)} all-gather(f32[320,256]{1,0:T(8,128)S(1)} %all_gather.14.refs_4_), channel_id=1, replica_groups=mesh['y'=8,'c'=2,'x'=4,'z'=8] {'c'}, dimensions={0}, use_global_device_ids=true | all-gather | bytes 983040 | tf_op jit(solution)/shard_map/all_gather | solution.py:302
  211.4 2.3 collective-permute-start
  213.7 4.2 %collective-permute-start.2 = (bf16[256,256]{1,0:T(8,128)(2,1)S(1)}, bf16[256,256]{1,0:T(8,128)(2,1)S(1)}, u32[]{:S(2)}, u32[]{:S(2)}) collective-permute-start(bf16[256,256]{1,0:T(8,128)(2,1)S(1)} %get-tuple-element.23), channel_id=1, source_target_pairs={{0,24},{8,0},{16,8},{24,16},{1,25},{9,1},{17,9},{25,17},{2,26},{10... | collective-permute-start | bytes 393224 | tf_op jit(solution)/shard_map/ppermute | solution.py:247
  217.9 1.9 collective-permute-start.1
  221.2 2.2 copy-done.1
  223.4 8.5 %shard_map.159 = bf16[2,24,128,128]{3,2,1,0:T(8,128)(2,1)} custom-call(s32[2,24]{1,0:T(2,128)S(1)} %copy-done.16, s32[2]{0:T(128)S(1)} %copy-done.19, bf16[64,128,256]{2,1,0:T(8,128)(2,1)S(1)} %bitcast.24, bf16[256,256]{1,0:T(8,128)(2,1)S(1)} %get-tuple-element.14.refs_1_.refs_3_, f32[320,256]{1,0:T(8,128)S(1)} %all_gather.14.refs_4_), custom_call_target="tpu_custom_call" | custom-call | flops 402653184 | bytes 5898240 | tf_op jit(solution)/shard_map/pallas_call | solution.py:45
  232.0 1.1 shard_map.158
  233.1 1.7 fusion.3
  (60 shorter events, 11.1 us)
Async XLA Ops:
  7.2 29.8 %copy-start.5 = (bf16[256,256]{1,0:T(8,128)(2,1)S(1)}, bf16[256,256]{1,0:T(8,128)(2,1)}, u32[]{:S(2)}) copy-start(bf16[256,256]{1,0:T(8,128)(2,1)} %refs_2_.5) | copy-start | bytes 393220
  7.2 29.8 %copy-start.20 = (f32[256]{0:T(256)S(1)}, f32[256]{0:T(256)}, u32[]{:S(2)}) copy-start(f32[256]{0:T(256)} %param.20) | copy-start | bytes 3076
  7.2 57.9 %copy-start.3 = (bf16[256,2048]{1,0:T(8,128)(2,1)S(1)}, bf16[256,2048]{1,0:T(8,128)(2,1)}, u32[]{:S(2)}) copy-start(bf16[256,2048]{1,0:T(8,128)(2,1)} %refs_0_.7) | copy-start | bytes 3145732
  7.2 77.6 %copy-start.19 = (s32[2]{0:T(128)S(1)}, s32[2]{0:T(128)}, u32[]{:S(2)}) copy-start(s32[2]{0:T(128)} %refs_1_.3) | copy-start | bytes 28
  7.2 77.6 %copy-start.16 = (s32[2,24]{1,0:T(2,128)S(1)}, s32[2,24]{1,0:T(2,128)}, u32[]{:S(2)}) copy-start(s32[2,24]{1,0:T(2,128)} %refs_0_.9) | copy-start | bytes 580
  7.2 77.6 %all-gather.2.cloned.1.call-start = ((), (), s32[]{:S(2)}) async-start(), calls=%async_computation.7 | async-start | bytes 4718592 | tf_op jit(solution)/shard_map/all_gather | solution.py:263
  20.8 0.9 copy-start.4
  23.0 61.8 %copy-start.6 = (bf16[2,24,128,128]{3,2,1,0:T(8,128)(2,1)S(1)}, bf16[2,24,128,128]{3,2,1,0:T(8,128)(2,1)}, u32[]{:S(2)}) copy-start(bf16[2,24,128,128]{3,2,1,0:T(8,128)(2,1)} %refs_2_.4) | copy-start | bytes 4718596
  25.2 39.8 %all-to-all-start = ((bf16[16,128,256]{2,1,0:T(8,128)(2,1)}), bf16[16,128,256]{2,1,0:T(8,128)(2,1)}, u32[]{:S(2)}, u32[]{:S(2)}) async-start(bf16[16,128,256]{2,1,0:T(8,128)(2,1)} %shard_map.154), calls=%async_computation | async-start | bytes 2097152 | tf_op jit(solution)/shard_map/all_to_all | solution.py:239
  37.0 173.3 %reduce-scatter.2.cloned.1.call-start = ((), (), s32[]{:S(2)}) async-start(), calls=%async_computation.8 | async-start | bytes 4718592 | tf_op jit(solution)/shard_map/reduce_scatter | solution.py:279
  84.8 2.2 copy-start
  87.0 0.9 copy-start.8
  87.9 0.9 copy-start.9
  88.8 9.9 %copy-start.7 = (bf16[256,256]{1,0:T(8,128)(2,1)S(1)}, bf16[256,256]{1,0:T(8,128)(2,1)}, u32[]{:S(2)}) copy-start(bf16[256,256]{1,0:T(8,128)(2,1)} %refs_3_.1) | copy-start | bytes 393220
  95.4 2.0 copy-start.2
  98.7 0.9 copy-start.11
  98.7 1.0 copy-start.13
  154.3 77.6 %all-to-all-start.5 = ((bf16[16,128,256]{2,1,0:T(8,128)(2,1)}), bf16[16,128,256]{2,1,0:T(8,128)(2,1)S(1)}, u32[]{:S(2)}, u32[]{:S(2)}) async-start(bf16[16,128,256]{2,1,0:T(8,128)(2,1)} %shard_map.157), calls=%async_computation.5 | async-start | bytes 2097152 | tf_op jit(solution)/shard_map/all_to_all | solution.py:239
  210.3 21.7 %copy-start.15 = (s32[1,16,128]{2,1,0:T(8,128)S(1)}, s32[1,16,128]{2,1,0:T(8,128)}, u32[]{:S(2)}) copy-start(s32[1,16,128]{2,1,0:T(8,128)} %param.16) | copy-start | bytes 24580
  210.3 21.7 %copy-start.18 = (s32[1,16]{1,0:T(1,128)S(1)}, s32[1,16]{1,0:T(1,128)}, u32[]{:S(2)}) copy-start(s32[1,16]{1,0:T(1,128)} %refs_0_.8) | copy-start | bytes 196
  211.4 21.7 %collective-permute-start = (bf16[256,256]{1,0:T(8,128)(2,1)S(1)}, bf16[256,256]{1,0:T(8,128)(2,1)S(1)}, u32[]{:S(2)}, u32[]{:S(2)}) collective-permute-start(bf16[256,256]{1,0:T(8,128)(2,1)S(1)} %get-tuple-element.22), channel_id=1, source_target_pairs={{0,8},{8,16},{16,24},{24,0},{1,9},{9,17},{17,25},{25,1},{2,10},{10... | collective-permute-start | bytes 393224 | tf_op jit(solution)/shard_map/ppermute | solution.py:247
  213.7 19.4 %collective-permute-start.2 = (bf16[256,256]{1,0:T(8,128)(2,1)S(1)}, bf16[256,256]{1,0:T(8,128)(2,1)S(1)}, u32[]{:S(2)}, u32[]{:S(2)}) collective-permute-start(bf16[256,256]{1,0:T(8,128)(2,1)S(1)} %get-tuple-element.23), channel_id=1, source_target_pairs={{0,24},{8,0},{16,8},{24,16},{1,25},{9,1},{17,9},{25,17},{2,26},{10... | collective-permute-start | bytes 393224 | tf_op jit(solution)/shard_map/ppermute | solution.py:247
  217.9 15.2 %collective-permute-start.1 = (bf16[256,256]{1,0:T(8,128)(2,1)S(1)}, bf16[256,256]{1,0:T(8,128)(2,1)S(1)}, u32[]{:S(2)}, u32[]{:S(2)}) collective-permute-start(bf16[256,256]{1,0:T(8,128)(2,1)S(1)} %get-tuple-element.24), channel_id=1, source_target_pairs={{0,16},{8,24},{16,0},{24,8},{1,17},{9,25},{17,1},{25,9},{2,18},{10... | collective-permute-start | bytes 393224 | tf_op jit(solution)/shard_map/ppermute | solution.py:247
  221.2 2.2 copy-start.1
  (4 other events, 2.7 us)
Sparse Core Ops, SparseCore 0:
  20.9 63.8 all-gather.1
  98.8 63.8 reduce-scatter.1

commit v4 on v3

--- a/solution.py
+++ b/solution.py
@@ -14,18 +14,18 @@
 NX, NZ, NY, NC = 4, 8, 8, 2
 NG = NY * NC
 BANDS = NX * NZ
-GRAD_ROWS = 40
+GRAD_ROWS = 48
 STORE = 8
 VMEM = pl.BlockSpec(memory_space=pltpu.VMEM)
 SMEM = pl.BlockSpec(memory_space=pltpu.SMEM)
-HBM = pl.BlockSpec(memory_space=pl.ANY)
+HBM = pl.BlockSpec(memory_space=pltpu.HBM)
 
 
 def sds(shape, dtype):
     return jax.ShapeDtypeStruct(shape, dtype)
 
 
-def call(body, scalars, arrays, outs, out_specs=None, scratch=(), extra=(), flops=0, vmem=24):
+def call(body, scalars, arrays, outs, out_specs=None, scratch=(), extra=(), flops=0, vmem=60):
     count, first = len(arrays), len(scalars)
 
     def kernel(*refs):
@@ -79,10 +79,10 @@
         out_ref[g] = lax.dot_general(hot, feat, TN, preferred_element_type=F32).astype(BF)
 
 
-def spot_of(index_ref, count_ref, t, k):
+def spot_of(index_ref, t, k):
     index = index_ref[t, k]
     z, x = lax.shift_right_logical(index, 1) & (NZ - 1), lax.shift_right_logical(index, 4)
-    return jnp.where(k < count_ref[t], (z * NX + x) * 2 + (index & 1), 2 * BANDS)
+    return (z * NX + x) * 2 + (index & 1)
 
 
 def main_body(scalars, arrays, copies, outs, tiles, acc, terms, tile_sem, term_sems):
@@ -101,7 +101,9 @@
     wait(copies)
     for t in range(2):
         rows = pl.ds(t * 128, 128)
-        spots = [spot_of(index_ref, count_ref, t, k) for k in range(slots)]
+        spots = [
+            jnp.where(k < count_ref[t], spot_of(index_ref, t, k), spare) for k in range(slots)
+        ]
         total = outer_ref[rows, :]
         for k in range(0, slots, 2):
             left = jnp.concatenate([blocks_ref[t, k], blocks_ref[t, k + 1]], axis=1)
@@ -165,7 +167,7 @@
             pltpu.SemaphoreType.DMA,
             pltpu.SemaphoreType.DMA((STORE,)),
         ],
-        compiler_params=pltpu.CompilerParams(vmem_limit_bytes=40 << 20),
+        compiler_params=pltpu.CompilerParams(vmem_limit_bytes=60 << 20),
         cost_estimate=pl.CostEstimate(flops=1 << 30, bytes_accessed=12 << 20, transcendentals=0),
     )(*scalars, *arrays, gathered)
 
@@ -176,16 +178,18 @@
     wait(copies)
     d_pre = dpre_ref[...]
     width = d_pre.shape[1]
-    part_ref[pl.ds(0, width), :] = lax.dot_general(
-        feat_ref[...], d_pre, TN, preferred_element_type=F32
-    )
-    part_ref[pl.ds(width, width), :] = lax.dot_general(
-        agg_ref[...], d_pre, TN, preferred_element_type=F32
-    )
-    rest = part_ref.shape[0] - 2 * width
+    groups, rows, _ = part_ref.shape
+    share = 2 * width // groups
+    for i, ref in enumerate((feat_ref, agg_ref)):
+        grad = lax.dot_general(ref[...], d_pre, TN, preferred_element_type=F32).astype(BF)
+        for g in range(groups // 2):
+            part_ref[i * groups // 2 + g, pl.ds(0, share), :] = grad[g * share : (g + 1) * share]
+    bias = jnp.sum(d_pre.astype(F32), axis=0, keepdims=True)
+    rest = rows - share
     row = lax.broadcasted_iota(jnp.int32, (rest, width), 0)
-    bias = jnp.sum(d_pre.astype(F32), axis=0, keepdims=True)
-    part_ref[pl.ds(2 * width, rest), :] = jnp.where(row == 0, bias, 0.0)
+    part_ref[0, pl.ds(share, rest), :] = jnp.where(row == 0, bias, 0.0).astype(BF)
+    for g in range(1, groups):
+        part_ref[g, pl.ds(share, rest), :] = jnp.zeros((rest, width), BF)
     self_ref[...] = lax.dot_general(d_pre, w_ref[...], NT, preferred_element_type=F32)
 
 
@@ -208,18 +212,10 @@
     for t in range(2):
         d_agg = dagg_ref[pl.ds(t * 128, 128), :]
         for k in range(out_ref.shape[1]):
-            live = k < count_ref[t]
-            spot = jnp.where(live, spot_of(index_ref, count_ref, t, k), 0)
-
-            @pl.when(live)
-            def _(t=t, k=k, spot=spot, d_agg=d_agg):
-                out_ref[t, k] = lax.dot_general(
-                    d_agg, tiles[spot], NT, preferred_element_type=F32
-                ).astype(BF)
-
-            @pl.when(jnp.logical_not(live))
-            def _(t=t, k=k):
-                out_ref[t, k] = jnp.zeros(out_ref.shape[2:], BF)
+            live = jnp.where(k < count_ref[t], 1.0, 0.0)
+            tile = tiles[spot_of(index_ref, t, k)]
+            grad = lax.dot_general(d_agg, tile, NT, preferred_element_type=F32)
+            out_ref[t, k] = (grad * live).astype(BF)
 
 
 def base_body(scalars, arrays, copies, outs):
@@ -235,12 +231,18 @@
     out_ref[...] = total
 
 
+def sum_body(scalars, arrays, copies, outs):
+    (parts_ref,), (out_ref,) = arrays, outs
+    wait(copies)
+    total = parts_ref[0].astype(F32)
+    for i in range(1, parts_ref.shape[0]):
+        total = total + parts_ref[i].astype(F32)
+    for i in range(out_ref.shape[0]):
+        out_ref[i] = total.astype(BF)
+
+
 def a2a(x, axis):
     return lax.all_to_all(x, axis, 0, 0, tiled=True)
-
-
-def spread(x, axis, n):
-    return a2a(jnp.broadcast_to(x[None], (n, *x.shape)), axis)
 
 
 def shift(x, axis, n, by):
@@ -286,20 +288,22 @@
 
     part, self_back = call(
         third_body, [], [d_pre, aggregate, features, w_self],
-        [sds((NG * GRAD_ROWS, width), F32), node_f32], flops=100 << 20,
-    )
-    part = jnp.sum(a2a(part.reshape(NC, NY * GRAD_ROWS, width), "c"), axis=0)
-    part = jnp.sum(a2a(part.reshape(NY, GRAD_ROWS, width), "y"), axis=0)
-    part = jnp.sum(spread(part, "x", NX), axis=0)
-    part = jnp.sum(spread(part, "z", NZ), axis=0) * scale
-
+        [sds((NG, GRAD_ROWS, width), BF), node_f32], flops=100 << 20,
+    )
+    part = jnp.sum(a2a(part, ("y", "c")).astype(F32), axis=0).astype(BF)
     (back,) = call(
         back_body, [], [cut_weight, d_agg], [cut_bf], extra=[part],
         flops=2 * NG * cut * width * nodes,
     )
     returned = a2a(back, ("y", "c"))
-    part = lax.all_gather(part, "y", axis=0, tiled=True)
-    grads = lax.all_gather(part, "c", axis=0, tiled=True)
+    part = jnp.sum(lax.all_gather(part, "x", axis=0).astype(F32), axis=0).astype(BF)
+    part = lax.all_gather(part, "z", axis=0)
+    (part,) = call(sum_body, [], [part], [sds((NY, GRAD_ROWS, width), BF)], extra=[returned])
+    part = a2a(part, "y")
+    grads = lax.all_gather(part, "c", axis=1).reshape(NG, GRAD_ROWS, width)
+    grads = grads.astype(F32) * scale
+    share = 2 * width // NG
+    weight_grads = grads[:, :share].reshape(2, width, width)
     (base,) = call(
         base_body, [send_count], [rows2, returned, self_back], [node_f32],
         flops=2 * NG * cut * width * nodes,
@@ -308,16 +312,16 @@
 
     (grad_blocks,) = call(
         blocks_body, [block_index, block_count], [gathered, d_agg], [sds(block_values.shape, BF)],
-        extra=[part], flops=2 * tiles_here * slots * 128 * 128 * width,
+        extra=[grads], flops=2 * tiles_here * slots * 128 * 128 * width,
     )
 
     return (
         output,
         d_features,
         grad_blocks,
-        grads[:width],
-        grads[width : 2 * width],
-        grads[2 * width],
+        weight_grads[0],
+        weight_grads[1],
+        grads[0, share],
     )
 
 

time: 242 us -> 212 us (0.88)
  blocking collectives: 114 us -> 78.9 us
  local copies, waits for them, and re-layouts: 15.2 us -> 3.75 us
  waiting for transfers between devices: 45 us -> 53.3 us
  Pallas kernels: 21.2 us -> 27.2 us
    all_to_all x4 -> x1, blocking collectives: 51.7 us -> 22 us  [a2a(): return lax.all_to_all(x, axis, 0, 0, tiled=True)]
    unnamed x42 -> x16, local copies, waits for them, and re-layouts: 12.7 us -> 1.01 us
    all_to_all x2 -> x3, waiting for transfers between devices: 26.9 us -> 32.5 us  [a2a(): return lax.all_to_all(x, axis, 0, 0, tiled=True)]
    all_gather x2 -> x3, blocking collectives: 48.5 us -> 43.4 us  [the longest x1 22.5 us: local(): part = lax.all_gather(part, 'z', axis=0)]
    pallas_call x5 -> x6, Pallas kernels: 14.7 us -> 17.8 us  [call(): pl.pallas_call(kernel, out_shape=tuple(outs), in_specs=[SMEM] * first + [...]
    pallas_call x1, Pallas kernels: 6.56 us -> 9.39 us  [main_kernel(): pl.pallas_call(kernel, out_shape=tuple(outs), in_specs=[SMEM] * 2 + [HBM]...]
    all_gather x1, waiting for transfers between devices: 18.1 us -> 20.7 us  [local(): lax.all_gather(gathered, 'z', axis=0, tiled=True)]
    all_to_all x2 -> x3, starting transfers between devices: 19.2 us -> 20.4 us  [a2a(): return lax.all_to_all(x, axis, 0, 0, tiled=True)]
  transfers between devices with their start and end apart: 7 -> 8, of which waited for: 2 -> 3; matrix products, arithmetic and copies ran while one was open for 2% -> 2% of each run, Pallas kernels for 6% -> 8%
where the time goes in v4:
time: 212 us; the launch traced here: 211 us
  blocking collectives  78.9 us (37%)
  waiting for transfers between devices  53.3 us (25%)
  starting transfers between devices  29.6 us (14%)
  Pallas kernels  27.2 us (13%)
  between operations  14.3 us (7%)
  local copies, waits for them, and re-layouts  3.75 us (2%)
  other arithmetic  2.4 us (1%)
    all_to_all x3, waiting for transfers between devices, a2a(): return lax.all_to_all(x, axis, 0, 0, tiled=True)  32.5 us
    all_gather x1, blocking collectives, local(): part = lax.all_gather(part, 'z', axis=0)  22.5 us
    all_to_all x1, blocking collectives, a2a(): return lax.all_to_all(x, axis, 0, 0, tiled=True)  22 us
    all_gather x1, waiting for transfers between devices, local(): lax.all_gather(gathered, 'z', axis=0, tiled=True)  20.7 us
    all_to_all x3, starting transfers between devices, a2a(): return lax.all_to_all(x, axis, 0, 0, tiled=True)  20.4 us
    pallas_call x6, Pallas kernels, call(): pl.pallas_call(kernel, out_shape=tuple(outs), in_specs=[SMEM] * first + [...  17.8 us
    all_gather x1, blocking collectives, local(): gathered = lax.all_gather(features, 'x', axis=0, tiled=True)  13.5 us
    all_gather x1, blocking collectives, local(): lax.all_gather(part, 'x', axis=0).astype(F32)  10.6 us
  transfers between devices with their start and end apart: 8, of which 3 were waited for; matrix products, arithmetic and copies ran while one was open for 2% of the time, Pallas kernels for 8%

profile of v4, /device:TPU:1, one launch (start us, length us, event | category | flops | bytes accessed | tf_op | source)
XLA Modules:
  0.0 211.4 jit_solution(2713580489834940315)
XLA Ops:
  7.3 13.5 %all_gather.24 = bf16[1024,256]{1,0:T(8,128)(2,1)} all-gather(bf16[256,256]{1,0:T(8,128)(2,1)} %refs_2_.5), channel_id=1, replica_groups=mesh['y'=8,'c'=2,'x'=4,'z'=8] {'x'}, dimensions={0}, use_global_device_ids=true | all-gather | bytes 655360 | tf_op jit(solution)/shard_map/all_gather | solution.py:264
  20.7 3.1 %shard_map.154 = bf16[16,128,256]{2,1,0:T(8,128)(2,1)} custom-call(s32[1,16]{1,0:T(1,128)} %refs_0_.8, s32[16,128]{1,0:T(8,128)} %bitcast.39, bf16[256,256]{1,0:T(8,128)(2,1)} %refs_2_.5), custom_call_target="tpu_custom_call" | custom-call | flops 268435456 | bytes 1187840 | tf_op jit(solution)/shard_map/pallas_call | solution.py:45
  23.8 11.1 %all-to-all-start = ((bf16[16,128,256]{2,1,0:T(8,128)(2,1)}), bf16[16,128,256]{2,1,0:T(8,128)(2,1)S(1)}, u32[]{:S(2)}, u32[]{:S(2)}) async-start(bf16[16,128,256]{2,1,0:T(8,128)(2,1)} %shard_map.154), calls=%async_computation | async-start | bytes 2097152 | tf_op jit(solution)/shard_map/all_to_all | solution.py:245
  35.9 27.0 %all-to-all-done = bf16[16,128,256]{2,1,0:T(8,128)(2,1)S(1)} async-done(((bf16[16,128,256]{2,1,0:T(8,128)(2,1)}), bf16[16,128,256]{2,1,0:T(8,128)(2,1)S(1)}, u32[]{:S(2)}, u32[]{:S(2)}) %all-to-all-start) | async-done | bytes 1048608 | tf_op jit(solution)/shard_map/all_to_all | solution.py:245
  62.9 1.1 convolution_bitcast_fusion.refs_3_
  64.0 20.7 %all-gather.5.cloned.1.call-done = bf16[8192,256]{1,0:T(8,128)(2,1)} async-done(((bf16[1024,256]{1,0:T(8,128)(2,1)}), bf16[8192,256]{1,0:T(8,128)(2,1)}) %all-gather.5.cloned.1.call-update) | async-done | bytes 4194320 | tf_op jit(solution)/shard_map/all_gather | solution.py:265
  84.8 9.4 %shard_map.155 = (bf16[256,256]{1,0:T(8,128)(2,1)}, bf16[256,256]{1,0:T(8,128)(2,1)}, bf16[256,256]{1,0:T(8,128)(2,1)}, bf16[256,256]{1,0:T(8,128)(2,1)}, bf16[64,128,256]{2,1,0:T(8,128)(2,1)}) custom-call(s32[2,24]{1,0:T(2,128)} %refs_0_.9, s32[2]{0:T(128)} %refs_1_.3, bf16[2,24,128,128]{3,2,1,0:T(8,128)(2,1)} %refs_2_.4, ...), custom_call_target="tpu_custom_call" | custom-call | flops 1073741824 | bytes 12582912 | tf_op jit(solution)/shard_map/pallas_call | solution.py:156
  94.2 2.2 %shard_map.156 = (bf16[16,48,256]{2,1,0:T(8,128)(2,1)}, f32[256,256]{1,0:T(8,128)}) custom-call(bf16[256,256]{1,0:T(8,128)(2,1)} %get-tuple-element.15.refs_0_, bf16[256,256]{1,0:T(8,128)(2,1)} %get-tuple-element.16.refs_1_, bf16[256,256]{1,0:T(8,128)(2,1)} %refs_2_.5, bf16[256,256]{1,0:T(8,128)(2,1)} %refs_3_.1), custom_call_target="tpu_custom_call" | custom-call | flops 104857600 | bytes 1179648 | tf_op jit(solution)/shard_map/pallas_call | solution.py:45
  96.4 22.0 %all_to_all.20 = bf16[16,48,256]{2,1,0:T(8,128)(2,1)S(1)} all-to-all(bf16[16,48,256]{2,1,0:T(8,128)(2,1)} %get-tuple-element.17), channel_id=1, replica_groups=mesh['y'=8,'c'=2,'x'=4,'z'=8] {'y','c'}, dimensions={0} | all-to-all | bytes 786432 | tf_op jit(solution)/shard_map/all_to_all | solution.py:245
  119.1 2.7 %shard_map.157 = bf16[16,128,256]{2,1,0:T(8,128)(2,1)} custom-call(bf16[256,2048]{1,0:T(8,128)(2,1)} %refs_0_.7, bf16[256,256]{1,0:T(8,128)(2,1)} %get-tuple-element.14.refs_1_.refs_3_, bf16[48,256]{1,0:T(8,128)(2,1)} %reduce_sum.24.refs_2_), custom_call_target="tpu_custom_call" | custom-call | flops 268435456 | bytes 2228224 | tf_op jit(solution)/shard_map/pallas_call | solution.py:45
  121.8 3.6 %all-to-all-start.2 = ((bf16[16,128,256]{2,1,0:T(8,128)(2,1)}), bf16[16,128,256]{2,1,0:T(8,128)(2,1)S(1)}, u32[]{:S(2)}, u32[]{:S(2)}) async-start(bf16[16,128,256]{2,1,0:T(8,128)(2,1)} %shard_map.157), calls=%async_computation.2 | async-start | bytes 2097152 | tf_op jit(solution)/shard_map/all_to_all | solution.py:245
  125.4 10.6 %all-gather = bf16[192,256]{1,0:T(8,128)(2,1)S(1)} all-gather(bf16[48,256]{1,0:T(8,128)(2,1)S(1)} %copy-done.6), channel_id=2, replica_groups=mesh['y'=8,'c'=2,'x'=4,'z'=8] {'x'}, dimensions={0}, use_global_device_ids=true | all-gather | bytes 122880 | tf_op jit(solution)/shard_map/all_gather | solution.py:299
  136.0 22.5 %all-gather.1 = bf16[384,256]{1,0:T(8,128)(2,1)} all-gather(bf16[48,256]{1,0:T(8,128)(2,1)S(1)} %reduce_sum.25), channel_id=3, replica_groups=mesh['y'=8,'c'=2,'x'=4,'z'=8] {'z'}, dimensions={0}, use_global_device_ids=true | all-gather | bytes 221184 | tf_op jit(solution)/shard_map/all_gather | solution.py:300
  159.5 1.6 shard_map.159
  161.1 5.8 %all-to-all-start.3 = ((bf16[8,48,256]{2,1,0:T(8,128)(2,1)}), bf16[8,48,256]{2,1,0:T(8,128)(2,1)S(1)}, u32[]{:S(2)}, u32[]{:S(2)}) async-start(bf16[8,48,256]{2,1,0:T(8,128)(2,1)} %shard_map.159), calls=%async_computation.4 | async-start | bytes 393216 | tf_op jit(solution)/shard_map/all_to_all | solution.py:245
  166.9 3.1 %shard_map.158 = f32[256,256]{1,0:T(8,128)} custom-call(s32[1,16]{1,0:T(1,128)} %refs_0_.8, s32[16,128]{1,0:T(8,128)} %bitcast.40, bf16[16,128,256]{2,1,0:T(8,128)(2,1)} %copy-done, f32[256,256]{1,0:T(8,128)} %get-tuple-element.18.refs_3_), custom_call_target="tpu_custom_call" | custom-call | flops 268435456 | bytes 1581056 | tf_op jit(solution)/shard_map/pallas_call | solution.py:45
  170.0 5.5 %all-to-all-done.3 = bf16[8,48,256]{2,1,0:T(8,128)(2,1)S(1)} async-done(((bf16[8,48,256]{2,1,0:T(8,128)(2,1)}), bf16[8,48,256]{2,1,0:T(8,128)(2,1)S(1)}, u32[]{:S(2)}, u32[]{:S(2)}) %all-to-all-start.3) | async-done | bytes 196640 | tf_op jit(solution)/shard_map/all_to_all | solution.py:245
  175.5 10.4 %all-gather.2 = bf16[8,96,256]{2,1,0:T(8,128)(2,1)S(1)} all-gather(bf16[8,48,256]{2,1,0:T(8,128)(2,1)S(1)} %all-to-all-done.3), channel_id=4, replica_groups=mesh['y'=8,'c'=2,'x'=4,'z'=8] {'c'}, dimensions={1}, use_global_device_ids=true | all-gather | bytes 589824 | tf_op jit(solution)/shard_map/all_gather | solution.py:303
  186.0 1.4 dynamic-slice_bitcast_fusion.2
  187.4 2.8 %collective-permute-start = (bf16[256,256]{1,0:T(8,128)(2,1)S(1)}, bf16[256,256]{1,0:T(8,128)(2,1)S(1)}, u32[]{:S(2)}, u32[]{:S(2)}) collective-permute-start(bf16[256,256]{1,0:T(8,128)(2,1)S(1)} %get-tuple-element.22), channel_id=1, source_target_pairs={{0,8},{8,16},{16,24},{24,0},{1,9},{9,17},{17,25},{25,1},{2,10},{10... | collective-permute-start | bytes 393224 | tf_op jit(solution)/shard_map/ppermute | solution.py:249
  190.2 3.7 %collective-permute-start.2 = (bf16[256,256]{1,0:T(8,128)(2,1)S(1)}, bf16[256,256]{1,0:T(8,128)(2,1)S(1)}, u32[]{:S(2)}, u32[]{:S(2)}) collective-permute-start(bf16[256,256]{1,0:T(8,128)(2,1)S(1)} %get-tuple-element.23), channel_id=1, source_target_pairs={{0,24},{8,0},{16,8},{24,16},{1,25},{9,1},{17,9},{25,17},{2,26},{10... | collective-permute-start | bytes 393224 | tf_op jit(solution)/shard_map/ppermute | solution.py:249
  193.9 2.6 %collective-permute-start.1 = (bf16[256,256]{1,0:T(8,128)(2,1)S(1)}, bf16[256,256]{1,0:T(8,128)(2,1)S(1)}, u32[]{:S(2)}, u32[]{:S(2)}) collective-permute-start(bf16[256,256]{1,0:T(8,128)(2,1)S(1)} %get-tuple-element.24), channel_id=1, source_target_pairs={{0,16},{8,24},{16,0},{24,8},{1,17},{9,25},{17,1},{25,9},{2,18},{10... | collective-permute-start | bytes 393224 | tf_op jit(solution)/shard_map/ppermute | solution.py:249
  197.9 5.0 %shard_map.160 = bf16[2,24,128,128]{3,2,1,0:T(8,128)(2,1)} custom-call(s32[2,24]{1,0:T(2,128)} %refs_0_.9, s32[2]{0:T(128)} %refs_1_.3, bf16[64,128,256]{2,1,0:T(8,128)(2,1)} %bitcast.27, bf16[256,256]{1,0:T(8,128)(2,1)} %get-tuple-element.14.refs_1_.refs_3_, f32[16,48,256]{2,1,0:T(8,128)} %bitcast.30), custom_call_target="tpu_custom_call" | custom-call | flops 402653184 | bytes 5898240 | tf_op jit(solution)/shard_map/pallas_call | solution.py:45
  202.9 1.6 fusion.3
  (31 shorter events, 4.2 us)
Async XLA Ops:
  7.2 27.8 %copy-start.3 = (bf16[256,256]{1,0:T(8,128)(2,1)S(1)}, bf16[256,256]{1,0:T(8,128)(2,1)}, u32[]{:S(2)}) copy-start(bf16[256,256]{1,0:T(8,128)(2,1)} %refs_2_.5) | copy-start | bytes 393220
  7.2 27.8 %copy-start.5 = (bf16[256,256]{1,0:T(8,128)(2,1)S(1)}, bf16[256,256]{1,0:T(8,128)(2,1)}, u32[]{:S(2)}) copy-start(bf16[256,256]{1,0:T(8,128)(2,1)} %refs_3_.1) | copy-start | bytes 393220
  7.2 27.8 %copy-start.7 = (f32[256]{0:T(256)S(1)}, f32[256]{0:T(256)}, u32[]{:S(2)}) copy-start(f32[256]{0:T(256)} %param.20) | copy-start | bytes 3076
  7.2 55.7 %copy-start.2 = (bf16[256,2048]{1,0:T(8,128)(2,1)S(1)}, bf16[256,2048]{1,0:T(8,128)(2,1)}, u32[]{:S(2)}) copy-start(bf16[256,2048]{1,0:T(8,128)(2,1)} %refs_0_.7) | copy-start | bytes 3145732
  7.2 77.6 %all-gather.5.cloned.1.call-start = ((), (), s32[]{:S(2)}) async-start(), calls=%async_computation.5 | async-start | bytes 4718592 | tf_op jit(solution)/shard_map/all_gather | solution.py:265
  23.8 39.1 %all-to-all-start = ((bf16[16,128,256]{2,1,0:T(8,128)(2,1)}), bf16[16,128,256]{2,1,0:T(8,128)(2,1)S(1)}, u32[]{:S(2)}, u32[]{:S(2)}) async-start(bf16[16,128,256]{2,1,0:T(8,128)(2,1)} %shard_map.154), calls=%async_computation | async-start | bytes 2097152 | tf_op jit(solution)/shard_map/all_to_all | solution.py:245
  34.9 151.1 %reduce-scatter.2.cloned.1.call-start = ((), (), s32[]{:S(2)}) async-start(), calls=%async_computation.6 | async-start | bytes 4718592 | tf_op jit(solution)/shard_map/reduce_scatter | solution.py:281
  119.1 6.3 %copy-start.6 = (bf16[48,256]{1,0:T(8,128)(2,1)S(1)}, bf16[48,256]{1,0:T(8,128)(2,1)}, u32[]{:S(2)}) copy-start(bf16[48,256]{1,0:T(8,128)(2,1)} %reduce_sum.24.refs_2_) | copy-start | bytes 73732
  121.8 36.7 %all-to-all-start.2 = ((bf16[16,128,256]{2,1,0:T(8,128)(2,1)}), bf16[16,128,256]{2,1,0:T(8,128)(2,1)S(1)}, u32[]{:S(2)}, u32[]{:S(2)}) async-start(bf16[16,128,256]{2,1,0:T(8,128)(2,1)} %shard_map.157), calls=%async_computation.2 | async-start | bytes 2097152 | tf_op jit(solution)/shard_map/all_to_all | solution.py:245
  158.5 1.0 copy-start
  161.1 14.4 %all-to-all-start.3 = ((bf16[8,48,256]{2,1,0:T(8,128)(2,1)}), bf16[8,48,256]{2,1,0:T(8,128)(2,1)S(1)}, u32[]{:S(2)}, u32[]{:S(2)}) async-start(bf16[8,48,256]{2,1,0:T(8,128)(2,1)} %shard_map.159), calls=%async_computation.4 | async-start | bytes 393216 | tf_op jit(solution)/shard_map/all_to_all | solution.py:245
  186.0 11.9 %copy-start.1 = (f32[8,96,256]{2,1,0:T(8,128)}, f32[8,96,256]{2,1,0:T(8,128)S(1)}, u32[]{:S(2)}) copy-start(f32[8,96,256]{2,1,0:T(8,128)S(1)} %convert_multiply_fusion) | copy-start | bytes 2359300
  186.0 16.9 %copy-start.4 = (f32[256,256]{1,0:T(8,128)S(1)}, f32[256,256]{1,0:T(8,128)}, u32[]{:S(2)}) copy-start(f32[256,256]{1,0:T(8,128)} %shard_map.158) | copy-start | bytes 786436
  187.4 15.5 %collective-permute-start = (bf16[256,256]{1,0:T(8,128)(2,1)S(1)}, bf16[256,256]{1,0:T(8,128)(2,1)S(1)}, u32[]{:S(2)}, u32[]{:S(2)}) collective-permute-start(bf16[256,256]{1,0:T(8,128)(2,1)S(1)} %get-tuple-element.22), channel_id=1, source_target_pairs={{0,8},{8,16},{16,24},{24,0},{1,9},{9,17},{17,25},{25,1},{2,10},{10... | collective-permute-start | bytes 393224 | tf_op jit(solution)/shard_map/ppermute | solution.py:249
  190.2 12.7 %collective-permute-start.2 = (bf16[256,256]{1,0:T(8,128)(2,1)S(1)}, bf16[256,256]{1,0:T(8,128)(2,1)S(1)}, u32[]{:S(2)}, u32[]{:S(2)}) collective-permute-start(bf16[256,256]{1,0:T(8,128)(2,1)S(1)} %get-tuple-element.23), channel_id=1, source_target_pairs={{0,24},{8,0},{16,8},{24,16},{1,25},{9,1},{17,9},{25,17},{2,26},{10... | collective-permute-start | bytes 393224 | tf_op jit(solution)/shard_map/ppermute | solution.py:249
  193.9 9.0 %collective-permute-start.1 = (bf16[256,256]{1,0:T(8,128)(2,1)S(1)}, bf16[256,256]{1,0:T(8,128)(2,1)S(1)}, u32[]{:S(2)}, u32[]{:S(2)}) collective-permute-start(bf16[256,256]{1,0:T(8,128)(2,1)S(1)} %get-tuple-element.24), channel_id=1, source_target_pairs={{0,16},{8,24},{16,0},{24,8},{1,17},{9,25},{17,1},{25,9},{2,18},{10... | collective-permute-start | bytes 393224 | tf_op jit(solution)/shard_map/ppermute | solution.py:249
Sparse Core Ops, SparseCore 0:
  20.9 63.8 all-gather.4
  94.3 57.7 reduce-scatter.1

commit v5 on v4

v5 whole, which is shorter than its diff:
```python
import math

import jax
import jax.numpy as jnp
from jax import lax
from jax.experimental import pallas as pl
from jax.experimental.pallas import tpu as pltpu
from jax.sharding import Mesh, PartitionSpec as P

BF = jnp.bfloat16
F32 = jnp.float32
TN = (((0,), (0,)), ((), ()))
NT = (((1,), (1,)), ((), ()))
NX, NZ, NY, NC = 4, 8, 8, 2
NG = NY * NC
BANDS = NX * NZ
GRAD_ROWS = 48
STORE = 8
VMEM = pl.BlockSpec(memory_space=pltpu.VMEM)
SMEM = pl.BlockSpec(memory_space=pltpu.SMEM)
HBM = pl.BlockSpec(memory_space=pltpu.HBM)


def sds(shape, dtype):
    return jax.ShapeDtypeStruct(shape, dtype)


def call(
    body, scalars, arrays, outs, out_specs=None, scratch=(), direct=(), extra=(), flops=0, vmem=60
):
    count, first = len(arrays), len(scalars)

    def kernel(*refs):
        sources = refs[first : first + count]
        rest = refs[first + count :]
        given, rest = rest[: len(direct)], rest[len(direct) + len(extra) :]
        outputs, rest = rest[: len(outs)], rest[len(outs) :]
        buffers, sems, rest = rest[:count], rest[count], rest[count + 1 :]
        copies = [
            pltpu.make_async_copy(source, buffer, sems.at[i])
            for i, (source, buffer) in enumerate(zip(sources, buffers, strict=True))
        ]
        for copy in copies:
            copy.start()
        body(refs[:first], buffers, copies, outputs, *([given] if direct else []), *rest)

    nbytes = sum(a.size * a.dtype.itemsize for a in (*arrays, *outs, *direct))
    return pl.pallas_call(
        kernel,
        out_shape=tuple(outs),
        in_specs=[SMEM] * first + [HBM] * (count + len(direct) + len(extra)),
        out_specs=tuple(out_specs or [VMEM] * len(outs)),
        scratch_shapes=[
            *(pltpu.VMEM(a.shape, a.dtype) for a in arrays),
            pltpu.SemaphoreType.DMA((count,)),
            *scratch,
        ],
        compiler_params=pltpu.CompilerParams(vmem_limit_bytes=vmem << 20),
        cost_estimate=pl.CostEstimate(flops=flops, bytes_accessed=nbytes, transcendentals=0),
    )(*scalars, *arrays, *direct, *extra)


def wait(copies):
    for copy in copies:
        copy.wait()


def hot_columns(rows_ref, count_ref, g, nodes):
    rows = rows_ref[g : g + 1, :]
    lane = lax.broadcasted_iota(jnp.int32, rows.shape, 1)
    rows = jnp.where(lane < count_ref[0, g], rows, -1)
    node = lax.broadcasted_iota(jnp.int32, (nodes, rows.shape[1]), 0)
    return jnp.where(node == rows, 1.0, 0.0).astype(BF)


def pick_body(scalars, arrays, copies, outs):
    (count_ref,), (rows_ref, feat_ref), (out_ref,) = scalars, arrays, outs
    wait(copies)
    feat = feat_ref[...]
    for g in range(out_ref.shape[0]):
        hot = hot_columns(rows_ref, count_ref, g, feat.shape[0])
        out_ref[g] = lax.dot_general(hot, feat, TN, preferred_element_type=F32).astype(BF)


def band_of(index_ref, t, k):
    index = index_ref[t, k]
    return lax.shift_right_logical(index, 4), lax.shift_right_logical(index, 1) & (NZ - 1), index & 1


def tile_spot(index_ref, x_ref, t, k):
    x, z, odd = band_of(index_ref, t, k)
    even_spot = z * NX + ((x_ref[0] - x) & (NX - 1))
    odd_spot = BANDS + ((x - x_ref[0]) & (NX - 1)) * NZ + z
    return jnp.where(odd == 0, even_spot, odd_spot)


def term_spot(index_ref, t, k):
    x, z, odd = band_of(index_ref, t, k)
    return (z * NX + x) * 2 + odd


def fetch_tiles(sources, tiles, sems):
    starts = (0, BANDS, BANDS + NZ, BANDS + 2 * NZ, BANDS + 2 * NZ + NZ // 2, BANDS + 3 * NZ)
    copies = [
        pltpu.make_async_copy(source, tiles.at[pl.ds(start, source.shape[0])], sems.at[i])
        for i, (source, start) in enumerate(zip(sources, starts, strict=True))
    ]
    for copy in copies:
        copy.start()
    return copies


def forward_body(scalars, arrays, copies, outs, sources, tiles, tile_sems):
    index_ref, count_ref, x_ref = scalars
    blocks_ref, outer_ref, pre_ref, w_ref, dout_ref, feat_ref, wself_ref, cut_ref = arrays
    out_ref, dagg_ref, back_ref, self_ref = outs
    tile_copies = fetch_tiles(sources, tiles, tile_sems)
    slots = blocks_ref.shape[1]
    spare = 2 * BANDS
    tiles[spare] = jnp.zeros(tiles.shape[1:], BF)
    wait(copies)
    wait(tile_copies)
    aggs, d_pres, d_aggs = [], [], []
    for t in range(2):
        rows = pl.ds(t * 128, 128)
        spots = [
            jnp.where(k < count_ref[t], tile_spot(index_ref, x_ref, t, k), spare)
            for k in range(slots)
        ]
        total = outer_ref[rows, :]
        for k in range(0, slots, 2):
            left = jnp.concatenate([blocks_ref[t, k], blocks_ref[t, k + 1]], axis=1)
            right = jnp.concatenate([tiles[spots[k]], tiles[spots[k + 1]]], axis=0)
            total = total + jnp.dot(left, right, preferred_element_type=F32)
        agg = total.astype(BF)
        pre = pre_ref[rows, :] + jnp.dot(agg, w_ref[...], preferred_element_type=F32)
        sig = jax.nn.sigmoid(pre)
        out_ref[rows, :] = (pre * sig).astype(BF)
        d_pre = (dout_ref[rows, :].astype(F32) * sig * (1.0 + pre * (1.0 - sig))).astype(BF)
        d_agg = lax.dot_general(d_pre, w_ref[...], NT, preferred_element_type=F32).astype(BF)
        dagg_ref[rows, :] = d_agg
        d_aggs.append(d_agg)
        aggs.append(agg)
        d_pres.append(d_pre)
    agg, d_pre = jnp.concatenate(aggs, axis=0), jnp.concatenate(d_pres, axis=0)
    width = d_pre.shape[1]
    groups = back_ref.shape[0]
    cut = cut_ref.shape[1] // groups
    share = 2 * width // groups
    rest = back_ref.shape[1] - cut - share
    for i, left in enumerate((feat_ref[...], agg)):
        grad = lax.dot_general(left, d_pre, TN, preferred_element_type=F32).astype(BF)
        for g in range(groups // 2):
            spot = i * groups // 2 + g
            back_ref[spot, pl.ds(cut, share), :] = grad[g * share : (g + 1) * share]
    bias = jnp.sum(d_pre.astype(F32), axis=0, keepdims=True)
    row = lax.broadcasted_iota(jnp.int32, (rest, width), 0)
    back_ref[0, pl.ds(cut + share, rest), :] = jnp.where(row == 0, bias, 0.0).astype(BF)
    for g in range(1, groups):
        back_ref[g, pl.ds(cut + share, rest), :] = jnp.zeros((rest, width), BF)
    d_agg = jnp.concatenate(d_aggs, axis=0)
    for g in range(0, groups, 2):
        rows = lax.dot_general(
            cut_ref[:, pl.ds(g * cut, 2 * cut)], d_agg, TN, preferred_element_type=F32
        ).astype(BF)
        back_ref[g, pl.ds(0, cut), :] = rows[:cut]
        back_ref[g + 1, pl.ds(0, cut), :] = rows[cut:]
    self_ref[...] = lax.dot_general(d_pre, wself_ref[...], NT, preferred_element_type=F32)


def terms_body(scalars, arrays, copies, outs, acc, terms, sems):
    (index_ref, count_ref), (blocks_ref, dagg_ref), (term_ref,) = scalars, arrays, outs
    slots = blocks_ref.shape[1]
    spare = 2 * BANDS

    def clear(i, carry):
        acc[i] = jnp.zeros(acc.shape[1:], F32)
        return carry

    lax.fori_loop(0, spare, clear, 0)
    wait(copies)
    for t in range(2):
        d_agg = dagg_ref[pl.ds(t * 128, 128), :]
        for k in range(slots):
            spot = jnp.where(k < count_ref[t], term_spot(index_ref, t, k), spare)
            term = lax.dot_general(blocks_ref[t, k], d_agg, TN, preferred_element_type=F32)
            acc[spot] = acc[spot] + term
    stores = []
    for c in range(STORE):
        part = pl.ds(c * (spare // STORE), spare // STORE)

        def convert(i, carry):
            terms[i] = acc[i].astype(BF)
            return carry

        lax.fori_loop(part.start, part.start + part.size, convert, 0)
        store = pltpu.make_async_copy(terms.at[part], term_ref.at[part], sems.at[c])
        store.start()
        stores.append(store)
    wait(stores)


def blocks_body(scalars, arrays, copies, outs, sources, tiles, tile_sems):
    (index_ref, count_ref, x_ref), (dagg_ref,), (out_ref,) = scalars, arrays, outs
    tile_copies = fetch_tiles(sources, tiles, tile_sems)
    wait(copies)
    wait(tile_copies)
    for t in range(2):
        d_agg = dagg_ref[pl.ds(t * 128, 128), :]
        for k in range(out_ref.shape[1]):
            live = jnp.where(k < count_ref[t], 1.0, 0.0)
            tile = tiles[tile_spot(index_ref, x_ref, t, k)]
            grad = lax.dot_general(d_agg, tile, NT, preferred_element_type=F32)
            out_ref[t, k] = (grad * live).astype(BF)


def base_body(scalars, arrays, copies, outs):
    (count_ref,), (rows_ref, back_ref, self_ref), (out_ref,) = scalars, arrays, outs
    cut = rows_ref.shape[1]
    wait(copies)
    total = self_ref[...]
    for g in range(0, back_ref.shape[0], 2):
        hot = jnp.concatenate(
            [hot_columns(rows_ref, count_ref, g + i, total.shape[0]) for i in range(2)], axis=1
        )
        rows = jnp.concatenate([back_ref[g + i, pl.ds(0, cut), :] for i in range(2)], axis=0)
        total = total + jnp.dot(hot, rows, preferred_element_type=F32)
    out_ref[...] = total


def sum_body(scalars, arrays, copies, outs):
    (parts_ref,), (out_ref,) = arrays, outs
    wait(copies)
    total = parts_ref[0].astype(F32)
    for i in range(1, parts_ref.shape[0]):
        total = total + parts_ref[i].astype(F32)
    for i in range(out_ref.shape[0]):
        out_ref[i] = total.astype(BF)


def a2a(x, axis):
    return lax.all_to_all(x, axis, 0, 0, tiled=True)


def shift(x, axis, n, by):
    return lax.ppermute(x, axis, [(i, (i + by) % n) for i in range(n)])


def local(
    features, block_index, block_count, block_values, cut_weight, send_rows, send_count,
    w_self, w_neigh, bias, d_out,
):
    nodes, width = features.shape
    tiles_here, slots = block_index.shape
    scale = 1.0 / math.sqrt(nodes * NG * BANDS)
    rows2 = send_rows.reshape(NG, -1)
    cut = rows2.shape[1]
    node_bf, node_f32 = sds((nodes, width), BF), sds((nodes, width), F32)
    cut_bf = sds((NG, cut, width), BF)

    even, odd = features[:128], features[128:]
    own = a2a(jnp.broadcast_to(odd[None], (NZ, *odd.shape)), "z")
    even = jnp.stack([even] + [shift(even, "x", NX, by) for by in range(1, NX)])
    even = lax.all_gather(even, "z", axis=0, tiled=True)
    left, right = shift(own, "x", NX, 1), shift(own, "x", NX, -1)
    far_low = shift(left[: NZ // 2], "x", NX, 1)
    far_high = shift(right[NZ // 2 :], "x", NX, -1)
    gathered = (even, own, right, far_low, far_high, left)
    me = lax.axis_index("x")
    my_x = me.astype(jnp.int32).reshape(1)

    (outgoing,) = call(
        pick_body, [send_count], [rows2, features], [cut_bf], flops=2 * NG * cut * width * nodes,
    )
    arrived = a2a(outgoing, ("y", "c")).reshape(NG * cut, width)
    outer = jnp.dot(cut_weight, arrived, preferred_element_type=F32)
    own_pre = jnp.dot(features, w_self, preferred_element_type=F32) + bias

    tiles = pltpu.VMEM((2 * BANDS + 1, 128, width), BF)
    output, d_agg, back, self_back = call(
        forward_body,
        [block_index, block_count, my_x],
        [block_values, outer, own_pre, w_neigh, d_out, features, w_self, cut_weight],
        [node_bf, node_bf, sds((NG, cut + GRAD_ROWS, width), BF), node_f32],
        scratch=[tiles, pltpu.SemaphoreType.DMA((6,))],
        direct=gathered,
        flops=1 << 29,
    )
    (terms,) = call(
        terms_body,
        [block_index, block_count],
        [block_values, d_agg],
        [sds((2 * BANDS, 128, width), BF)],
        out_specs=[HBM],
        scratch=[
            pltpu.VMEM((2 * BANDS + 1, 128, width), F32),
            pltpu.VMEM((2 * BANDS, 128, width), BF),
            pltpu.SemaphoreType.DMA((STORE,)),
        ],
        flops=1 << 29,
    )

    terms = lax.psum_scatter(terms.reshape(NZ, NX * nodes, width), "z", scatter_dimension=0)
    terms = terms.reshape(NX, nodes, width)
    own_back = lax.dynamic_index_in_dim(terms, me, 0, keepdims=False).astype(F32)
    for by in range(1, NX):
        away = lax.dynamic_index_in_dim(terms, (me + by) & (NX - 1), 0, keepdims=False)
        own_back = own_back + shift(away, "x", NX, by).astype(F32)

    returned = a2a(back, ("y", "c"))
    part = jnp.sum(returned[:, cut:].astype(F32), axis=0).astype(BF)
    part = a2a(jnp.broadcast_to(part[None], (NX, *part.shape)), "x")
    part = jnp.sum(part.astype(F32), axis=0).astype(BF)
    part = a2a(jnp.broadcast_to(part[None], (NZ, *part.shape)), "z")
    (part,) = call(sum_body, [], [part], [sds((NY, GRAD_ROWS, width), BF)], extra=[terms])
    part = a2a(part, "y")
    grads = lax.all_gather(part, "c", axis=1).reshape(NG, GRAD_ROWS, width)
    grads = grads.astype(F32) * scale
    share = 2 * width // NG
    weight_grads = grads[:, :share].reshape(2, width, width)

    (grad_blocks,) = call(
        blocks_body, [block_index, block_count, my_x], [d_agg], [sds(block_values.shape, BF)],
        scratch=[tiles, pltpu.SemaphoreType.DMA((6,))], direct=gathered,
        flops=2 * tiles_here * slots * 128 * 128 * width,
    )
    (base,) = call(
        base_body, [send_count], [rows2, returned, self_back], [node_f32],
        flops=2 * NG * cut * width * nodes,
    )
    d_features = (base + own_back).astype(BF)

    return (
        output,
        d_features,
        grad_blocks,
        weight_grads[0],
        weight_grads[1],
        grads[0, share],
    )


def solution(mesh):
    mesh = Mesh(mesh.devices.reshape(NY, NC, NX, NZ), ("y", "c", "x", "z"))
    rows = ("y", "c", "x", "z")
    split = [P(rows)] * 7 + [P()] * 3 + [P(rows)]
    return jax.shard_map(
        local,
        mesh=mesh,
        in_specs=tuple(split),
        out_specs=(P(rows), P(rows), P(rows), P(), P(), P()),
        check_vma=False,
    )
```

time: 212 us -> 204 us (0.962)
  starting transfers between devices: 29.6 us -> 64.2 us
  waiting for transfers between devices: 53.3 us -> 26.3 us
  blocking collectives: 78.9 us -> 58.6 us
  local copies, waits for them, and re-layouts: 3.75 us -> 9.38 us
    all_gather x3 -> x0, blocking collectives: 46.5 us -> none  [the longest x1 22.5 us: local(): part = lax.all_gather(part, 'z', axis=0)]
    all_to_all x1 -> x2, blocking collectives: 22 us -> 55.2 us  [a2a(): return lax.all_to_all(x, axis, 0, 0, tiled=True)]
    ppermute x3 -> x10, starting transfers between devices: 9.05 us -> 34.7 us  [shift(): return lax.ppermute(x, axis, [(i, (i + by) % n) for i in range(n)])]
    all_gather x1, waiting for transfers between devices: 20.7 us -> 0.01 us  [local(): even = lax.all_gather(even, 'z', axis=0, tiled=True)]
    all_to_all x3 -> x4, waiting for transfers between devices: 32.5 us -> 13.7 us  [a2a(): return lax.all_to_all(x, axis, 0, 0, tiled=True)]
    ppermute x3 -> x10, waiting for transfers between devices: 0.01 us -> 12.6 us  [shift(): return lax.ppermute(x, axis, [(i, (i + by) % n) for i in range(n)])]
    pallas_call x1 -> x0, Pallas kernels: 9.39 us -> none  [main_kernel(): pl.pallas_call(kernel, out_shape=tuple(outs), in_specs=[SMEM] * 2 + [HBM]...]
    all_to_all x3 -> x4, starting transfers between devices: 20.4 us -> 29.3 us  [a2a(): return lax.all_to_all(x, axis, 0, 0, tiled=True)]
  transfers between devices with their start and end apart: 8 -> 16, of which waited for: 3 -> 7; matrix products, arithmetic and copies ran while one was open for 2% -> 4% of each run, Pallas kernels for 8% -> 6%
where the time goes in v5:
time: 204 us; the launch traced here: 203 us
  starting transfers between devices  64.2 us (31%)
  blocking collectives  58.6 us (29%)
  waiting for transfers between devices  26.3 us (13%)
  Pallas kernels  25.6 us (13%)
  between operations  14.4 us (7%)
  local copies, waits for them, and re-layouts  9.38 us (5%)
  other arithmetic  2.6 us (1%)
    all_to_all x2, blocking collectives, a2a(): return lax.all_to_all(x, axis, 0, 0, tiled=True)  55.2 us
    ppermute x10, starting transfers between devices, shift(): return lax.ppermute(x, axis, [(i, (i + by) % n) for i in range(n)])  34.7 us
    all_to_all x4, starting transfers between devices, a2a(): return lax.all_to_all(x, axis, 0, 0, tiled=True)  29.3 us
    pallas_call x6, Pallas kernels, call(): pl.pallas_call(kernel, out_shape=tuple(outs), in_specs=[SMEM] * first + [...  25.6 us
    all_to_all x4, waiting for transfers between devices, a2a(): return lax.all_to_all(x, axis, 0, 0, tiled=True)  13.7 us
    ppermute x10, waiting for transfers between devices, shift(): return lax.ppermute(x, axis, [(i, (i + by) % n) for i in range(n)])  12.6 us
  transfers between devices with their start and end apart: 16, of which 7 were waited for; matrix products, arithmetic and copies ran while one was open for 4% of the time, Pallas kernels for 6%

profile of v5, /device:TPU:1, one launch (start us, length us, event | category | flops | bytes accessed | tf_op | source)
XLA Modules:
  0.0 203.1 jit_solution(9705998198763221314)
XLA Ops:
  8.1 5.5 %collective-permute-start.1 = (bf16[128,256]{1,0:T(8,128)(2,1)S(1)}, bf16[128,256]{1,0:T(8,128)(2,1)S(1)}, u32[]{:S(2)}, u32[]{:S(2)}) collective-permute-start(bf16[128,256]{1,0:T(8,128)(2,1)S(1)} %get-tuple-element.21), channel_id=1, source_target_pairs={{0,16},{8,24},{16,0},{24,8},{1,17},{9,25},{17,1},{25,9},{2,18},{10... | collective-permute-start | bytes 196616 | tf_op jit(solution)/shard_map/ppermute | solution.py:246
  13.6 2.2 %collective-permute-start = (bf16[128,256]{1,0:T(8,128)(2,1)S(1)}, bf16[128,256]{1,0:T(8,128)(2,1)S(1)}, u32[]{:S(2)}, u32[]{:S(2)}) collective-permute-start(bf16[128,256]{1,0:T(8,128)(2,1)S(1)} %get-tuple-element.21), channel_id=1, source_target_pairs={{0,8},{8,16},{16,24},{24,0},{1,9},{9,17},{17,25},{25,1},{2,10},{10... | collective-permute-start | bytes 196616 | tf_op jit(solution)/shard_map/ppermute | solution.py:246
  15.8 4.3 %collective-permute-start.2 = (bf16[128,256]{1,0:T(8,128)(2,1)S(1)}, bf16[128,256]{1,0:T(8,128)(2,1)S(1)}, u32[]{:S(2)}, u32[]{:S(2)}) collective-permute-start(bf16[128,256]{1,0:T(8,128)(2,1)S(1)} %get-tuple-element.21), channel_id=1, source_target_pairs={{0,24},{8,0},{16,8},{24,16},{1,25},{9,1},{17,9},{25,17},{2,26},{10... | collective-permute-start | bytes 196616 | tf_op jit(solution)/shard_map/ppermute | solution.py:246
  23.0 10.0 %all-to-all-start.1 = ((bf16[8,128,256]{2,1,0:T(8,128)(2,1)}), bf16[8,128,256]{2,1,0:T(8,128)(2,1)S(1)}, u32[]{:S(2)}, u32[]{:S(2)}) async-start(bf16[8,128,256]{2,1,0:T(8,128)(2,1)} %broadcast_in_dim.6), calls=%async_computation.1 | async-start | bytes 1048576 | tf_op jit(solution)/shard_map/all_to_all | solution.py:242
  33.1 3.2 %shard_map.154 = bf16[16,128,256]{2,1,0:T(8,128)(2,1)} custom-call(s32[1,16]{1,0:T(1,128)} %refs_0_.7, s32[16,128]{1,0:T(8,128)} %bitcast.41, bf16[256,256]{1,0:T(8,128)(2,1)} %refs_8_.1), custom_call_target="tpu_custom_call" | custom-call | flops 268435456 | bytes 1187840 | tf_op jit(solution)/shard_map/pallas_call | solution.py:48
  36.3 11.9 %all-to-all-done.1.refs_12_.refs_5_ = bf16[8,128,256]{2,1,0:T(8,128)(2,1)S(1)} async-done(((bf16[8,128,256]{2,1,0:T(8,128)(2,1)}), bf16[8,128,256]{2,1,0:T(8,128)(2,1)S(1)}, u32[]{:S(2)}, u32[]{:S(2)}) %all-to-all-start.1) | async-done | bytes 524320 | tf_op jit(solution)/shard_map/all_to_all | solution.py:242
  48.2 12.5 %all-to-all-start = ((bf16[16,128,256]{2,1,0:T(8,128)(2,1)}), bf16[16,128,256]{2,1,0:T(8,128)(2,1)S(1)}, u32[]{:S(2)}, u32[]{:S(2)}) async-start(bf16[16,128,256]{2,1,0:T(8,128)(2,1)} %shard_map.154), calls=%async_computation | async-start | bytes 2097152 | tf_op jit(solution)/shard_map/all_to_all | solution.py:242
  60.7 1.9 collective-permute-start.4
  62.7 5.9 %collective-permute-start.3 = (bf16[8,128,256]{2,1,0:T(8,128)(2,1)S(1)}, bf16[8,128,256]{2,1,0:T(8,128)(2,1)}, u32[]{:S(2)}, u32[]{:S(2)}) collective-permute-start(bf16[8,128,256]{2,1,0:T(8,128)(2,1)S(1)} %all-to-all-done.1.refs_12_.refs_5_), channel_id=1, source_target_pairs={{0,24},{8,0},{16,8},{24,16},{1,25},{9,1},{17,9},{25,17},{2,26},{10... | collective-permute-start | bytes 1572872 | tf_op jit(solution)/shard_map/ppermute | solution.py:246
  69.6 9.3 %collective-permute-done.4.refs_16_.refs_9_ = bf16[8,128,256]{2,1,0:T(8,128)(2,1)S(1)} collective-permute-done((bf16[8,128,256]{2,1,0:T(8,128)(2,1)S(1)}, bf16[8,128,256]{2,1,0:T(8,128)(2,1)S(1)}, u32[]{:S(2)}, u32[]{:S(2)}) %collective-permute-start.4) | collective-permute-done | bytes 524320 | tf_op jit(solution)/shard_map/ppermute | solution.py:246
  79.6 1.9 collective-permute-start.5
  82.5 4.6 %collective-permute-start.6 = (bf16[4,128,256]{2,1,0:T(8,128)(2,1)S(1)}, bf16[4,128,256]{2,1,0:T(8,128)(2,1)S(1)}, u32[]{:S(2)}, u32[]{:S(2)}) collective-permute-start(bf16[4,128,256]{2,1,0:T(8,128)(2,1)S(1)} %slice.38), channel_id=1, source_target_pairs={{0,24},{8,0},{16,8},{24,16},{1,25},{9,1},{17,9},{25,17},{2,26},{10... | collective-permute-start | bytes 786440 | tf_op jit(solution)/shard_map/ppermute | solution.py:246
  92.4 7.2 %shard_map.155 = (bf16[256,256]{1,0:T(8,128)(2,1)}, bf16[256,256]{1,0:T(8,128)(2,1)}, bf16[16,176,256]{2,1,0:T(8,128)(2,1)}, f32[256,256]{1,0:T(8,128)}) custom-call(s32[2,24]{1,0:T(2,128)} %refs_0_.9, s32[2]{0:T(128)} %refs_1_.5, s32[1]{0:T(128)} %bitcast.refs_2_, bf16[2,24,128,128]{3,2,1,0:T(8,128)(2,1)} %refs_2_.3, ...), custom_call_target="tpu_custom_call" | custom-call | flops 536870912 | bytes 9830400 | tf_op jit(solution)/shard_map/pallas_call | solution.py:48
  99.6 5.3 %shard_map.157 = bf16[64,128,256]{2,1,0:T(8,128)(2,1)} custom-call(s32[2,24]{1,0:T(2,128)} %refs_0_.9, s32[2]{0:T(128)} %refs_1_.5, bf16[2,24,128,128]{3,2,1,0:T(8,128)(2,1)} %refs_2_.3, bf16[256,256]{1,0:T(8,128)(2,1)} %get-tuple-element.13.refs_3_), custom_call_target="tpu_custom_call" | custom-call | flops 536870912 | bytes 5898240 | tf_op jit(solution)/shard_map/pallas_call | solution.py:48
  106.3 45.3 %all_to_all.30.refs_2_ = bf16[16,176,256]{2,1,0:T(8,128)(2,1)S(1)} all-to-all(bf16[16,176,256]{2,1,0:T(8,128)(2,1)S(1)} %copy-done.5), channel_id=1, replica_groups=mesh['y'=8,'c'=2,'x'=4,'z'=8] {'y','c'}, dimensions={0} | all-to-all | bytes 2883584 | tf_op jit(solution)/shard_map/all_to_all | solution.py:242
  151.6 9.9 %all_to_all.31 = bf16[4,48,256]{2,1,0:T(8,128)(2,1)S(1)} all-to-all(bf16[4,48,256]{2,1,0:T(8,128)(2,1)S(1)} %broadcast_in_dim.7), channel_id=1, replica_groups=mesh['y'=8,'c'=2,'x'=4,'z'=8] {'x'}, dimensions={0} | all-to-all | bytes 196608 | tf_op jit(solution)/shard_map/all_to_all | solution.py:242
  162.3 3.4 %all-to-all-start.4 = ((bf16[8,48,256]{2,1,0:T(8,128)(2,1)}), bf16[8,48,256]{2,1,0:T(8,128)(2,1)S(1)}, u32[]{:S(2)}, u32[]{:S(2)}) async-start(bf16[8,48,256]{2,1,0:T(8,128)(2,1)} %broadcast_in_dim.8), calls=%async_computation.5 | async-start | bytes 393216 | tf_op jit(solution)/shard_map/all_to_all | solution.py:242
  166.8 2.2 %collective-permute-start.7 = (bf16[256,256]{1,0:T(8,128)(2,1)S(1)}, bf16[256,256]{1,0:T(8,128)(2,1)S(1)}, u32[]{:S(2)}, u32[]{:S(2)}) collective-permute-start(bf16[256,256]{1,0:T(8,128)(2,1)S(1)} %get-tuple-element.16), channel_id=1, source_target_pairs={{0,8},{8,16},{16,24},{24,0},{1,9},{9,17},{17,25},{25,1},{2,10},{10... | collective-permute-start | bytes 393224 | tf_op jit(solution)/shard_map/ppermute | solution.py:246
  169.0 4.3 %collective-permute-start.9 = (bf16[256,256]{1,0:T(8,128)(2,1)S(1)}, bf16[256,256]{1,0:T(8,128)(2,1)S(1)}, u32[]{:S(2)}, u32[]{:S(2)}) collective-permute-start(bf16[256,256]{1,0:T(8,128)(2,1)S(1)} %get-tuple-element.17), channel_id=1, source_target_pairs={{0,24},{8,0},{16,8},{24,16},{1,25},{9,1},{17,9},{25,17},{2,26},{10... | collective-permute-start | bytes 393224 | tf_op jit(solution)/shard_map/ppermute | solution.py:246
  173.3 1.9 collective-permute-start.8
  177.9 3.4 %all-to-all-start.5 = ((bf16[8,48,256]{2,1,0:T(8,128)(2,1)}), bf16[8,48,256]{2,1,0:T(8,128)(2,1)S(1)}, u32[]{:S(2)}, u32[]{:S(2)}) async-start(bf16[8,48,256]{2,1,0:T(8,128)(2,1)} %shard_map.159), calls=%async_computation.6 | async-start | bytes 393216 | tf_op jit(solution)/shard_map/all_to_all | solution.py:242
  181.3 5.1 %shard_map.158 = bf16[2,24,128,128]{3,2,1,0:T(8,128)(2,1)} custom-call(s32[2,24]{1,0:T(2,128)} %refs_0_.9, s32[2]{0:T(128)} %refs_1_.5, s32[1]{0:T(128)} %bitcast.refs_2_, bf16[256,256]{1,0:T(8,128)(2,1)} %get-tuple-element.13.refs_3_, bf16[32,128,256]{2,1,0:T(8,128)(2,1)} %all-gather.3.cloned.1.call-done.refs_11_.refs_4_, bf16[8,128,256]{2,1,0:T(8,128)(2,1)} %copy-done.1, ...), custom_call_target="tpu_custom_call" | custom-call | flops 402653184 | bytes 5898240 | tf_op jit(solution)/shard_map/pallas_call | solution.py:48
  186.4 3.2 %shard_map.156 = f32[256,256]{1,0:T(8,128)} custom-call(s32[1,16]{1,0:T(1,128)} %refs_0_.7, s32[16,128]{1,0:T(8,128)} %bitcast.42, bf16[16,176,256]{2,1,0:T(8,128)(2,1)} %copy-done, f32[256,256]{1,0:T(8,128)} %get-tuple-element.12.refs_3_), custom_call_target="tpu_custom_call" | custom-call | flops 268435456 | bytes 1974272 | tf_op jit(solution)/shard_map/pallas_call | solution.py:48
  191.4 3.4 %all-gather = bf16[8,96,256]{2,1,0:T(8,128)(2,1)S(1)} all-gather(bf16[8,48,256]{2,1,0:T(8,128)(2,1)S(1)} %all-to-all-done.5), channel_id=2, replica_groups=mesh['y'=8,'c'=2,'x'=4,'z'=8] {'c'}, dimensions={1}, use_global_device_ids=true | all-gather | bytes 589824 | tf_op jit(solution)/shard_map/all_gather | solution.py:317
  (57 shorter events, 20.9 us)
Async XLA Ops:
  7.2 84.6 %all-gather.3.cloned.1.call-start = ((), (), s32[]{:S(2)}) async-start(), calls=%async_computation.7 | async-start | bytes 2359296 | tf_op jit(solution)/shard_map/all_gather | solution.py:264
  8.1 12.0 %collective-permute-start.1 = (bf16[128,256]{1,0:T(8,128)(2,1)S(1)}, bf16[128,256]{1,0:T(8,128)(2,1)S(1)}, u32[]{:S(2)}, u32[]{:S(2)}) collective-permute-start(bf16[128,256]{1,0:T(8,128)(2,1)S(1)} %get-tuple-element.21), channel_id=1, source_target_pairs={{0,16},{8,24},{16,0},{24,8},{1,17},{9,25},{17,1},{25,9},{2,18},{10... | collective-permute-start | bytes 196616 | tf_op jit(solution)/shard_map/ppermute | solution.py:246
  13.6 6.5 %collective-permute-start = (bf16[128,256]{1,0:T(8,128)(2,1)S(1)}, bf16[128,256]{1,0:T(8,128)(2,1)S(1)}, u32[]{:S(2)}, u32[]{:S(2)}) collective-permute-start(bf16[128,256]{1,0:T(8,128)(2,1)S(1)} %get-tuple-element.21), channel_id=1, source_target_pairs={{0,8},{8,16},{16,24},{24,0},{1,9},{9,17},{17,25},{25,1},{2,10},{10... | collective-permute-start | bytes 196616 | tf_op jit(solution)/shard_map/ppermute | solution.py:246
  15.8 5.6 %collective-permute-start.2 = (bf16[128,256]{1,0:T(8,128)(2,1)S(1)}, bf16[128,256]{1,0:T(8,128)(2,1)S(1)}, u32[]{:S(2)}, u32[]{:S(2)}) collective-permute-start(bf16[128,256]{1,0:T(8,128)(2,1)S(1)} %get-tuple-element.21), channel_id=1, source_target_pairs={{0,24},{8,0},{16,8},{24,16},{1,25},{9,1},{17,9},{25,17},{2,26},{10... | collective-permute-start | bytes 196616 | tf_op jit(solution)/shard_map/ppermute | solution.py:246
  23.0 25.2 %all-to-all-start.1 = ((bf16[8,128,256]{2,1,0:T(8,128)(2,1)}), bf16[8,128,256]{2,1,0:T(8,128)(2,1)S(1)}, u32[]{:S(2)}, u32[]{:S(2)}) async-start(bf16[8,128,256]{2,1,0:T(8,128)(2,1)} %broadcast_in_dim.6), calls=%async_computation.1 | async-start | bytes 1048576 | tf_op jit(solution)/shard_map/all_to_all | solution.py:242
  33.1 35.6 %copy-start.4 = (bf16[256,256]{1,0:T(8,128)(2,1)S(1)}, bf16[256,256]{1,0:T(8,128)(2,1)}, u32[]{:S(2)}) copy-start(bf16[256,256]{1,0:T(8,128)(2,1)} %refs_8_.1) | copy-start | bytes 393220
  33.1 35.6 %copy-start.9 = (bf16[256,256]{1,0:T(8,128)(2,1)S(1)}, bf16[256,256]{1,0:T(8,128)(2,1)}, u32[]{:S(2)}) copy-start(bf16[256,256]{1,0:T(8,128)(2,1)} %refs_9_.1) | copy-start | bytes 393220
  33.1 35.6 %copy-start.10 = (f32[256]{0:T(256)S(1)}, f32[256]{0:T(256)}, u32[]{:S(2)}) copy-start(f32[256]{0:T(256)} %param.20) | copy-start | bytes 3076
  36.3 52.3 %copy-start.2 = (bf16[256,2048]{1,0:T(8,128)(2,1)S(1)}, bf16[256,2048]{1,0:T(8,128)(2,1)}, u32[]{:S(2)}) copy-start(bf16[256,2048]{1,0:T(8,128)(2,1)} %refs_10_.1) | copy-start | bytes 3145732
  48.2 31.4 %copy-start.1 = (bf16[8,128,256]{2,1,0:T(8,128)(2,1)}, bf16[8,128,256]{2,1,0:T(8,128)(2,1)S(1)}, u32[]{:S(2)}) copy-start(bf16[8,128,256]{2,1,0:T(8,128)(2,1)S(1)} %all-to-all-done.1.refs_12_.refs_5_) | copy-start | bytes 1572868
  48.2 40.4 %all-to-all-start = ((bf16[16,128,256]{2,1,0:T(8,128)(2,1)}), bf16[16,128,256]{2,1,0:T(8,128)(2,1)S(1)}, u32[]{:S(2)}, u32[]{:S(2)}) async-start(bf16[16,128,256]{2,1,0:T(8,128)(2,1)} %shard_map.154), calls=%async_computation | async-start | bytes 2097152 | tf_op jit(solution)/shard_map/all_to_all | solution.py:242
  60.7 105.0 %reduce-scatter.2.cloned.1.call-start = ((), (), s32[]{:S(2)}) async-start(), calls=%async_computation.8 | async-start | bytes 4718592 | tf_op jit(solution)/shard_map/reduce_scatter | solution.py:303
  60.7 18.1 %collective-permute-start.4 = (bf16[8,128,256]{2,1,0:T(8,128)(2,1)S(1)}, bf16[8,128,256]{2,1,0:T(8,128)(2,1)S(1)}, u32[]{:S(2)}, u32[]{:S(2)}) collective-permute-start(bf16[8,128,256]{2,1,0:T(8,128)(2,1)S(1)} %all-to-all-done.1.refs_12_.refs_5_), channel_id=1, source_target_pairs={{0,8},{8,16},{16,24},{24,0},{1,9},{9,17},{17,25},{25,1},{2,10},{10... | collective-permute-start | bytes 1572872 | tf_op jit(solution)/shard_map/ppermute | solution.py:246
  62.7 18.9 %collective-permute-start.3 = (bf16[8,128,256]{2,1,0:T(8,128)(2,1)S(1)}, bf16[8,128,256]{2,1,0:T(8,128)(2,1)}, u32[]{:S(2)}, u32[]{:S(2)}) collective-permute-start(bf16[8,128,256]{2,1,0:T(8,128)(2,1)S(1)} %all-to-all-done.1.refs_12_.refs_5_), channel_id=1, source_target_pairs={{0,24},{8,0},{16,8},{24,16},{1,25},{9,1},{17,9},{25,17},{2,26},{10... | collective-permute-start | bytes 1572872 | tf_op jit(solution)/shard_map/ppermute | solution.py:246
  78.9 10.9 %copy-start.3 = (bf16[8,128,256]{2,1,0:T(8,128)(2,1)}, bf16[8,128,256]{2,1,0:T(8,128)(2,1)S(1)}, u32[]{:S(2)}) copy-start(bf16[8,128,256]{2,1,0:T(8,128)(2,1)S(1)} %collective-permute-done.4.refs_16_.refs_9_) | copy-start | bytes 1572868
  79.6 10.5 %collective-permute-start.5 = (bf16[4,128,256]{2,1,0:T(8,128)(2,1)}, bf16[4,128,256]{2,1,0:T(8,128)(2,1)S(1)}, u32[]{:S(2)}, u32[]{:S(2)}) collective-permute-start(bf16[4,128,256]{2,1,0:T(8,128)(2,1)} %slice.37), channel_id=1, source_target_pairs={{0,8},{8,16},{16,24},{24,0},{1,9},{9,17},{17,25},{25,1},{2,10},{10... | collective-permute-start | bytes 786440 | tf_op jit(solution)/shard_map/ppermute | solution.py:246
  82.5 9.2 %collective-permute-start.6 = (bf16[4,128,256]{2,1,0:T(8,128)(2,1)S(1)}, bf16[4,128,256]{2,1,0:T(8,128)(2,1)S(1)}, u32[]{:S(2)}, u32[]{:S(2)}) collective-permute-start(bf16[4,128,256]{2,1,0:T(8,128)(2,1)S(1)} %slice.38), channel_id=1, source_target_pairs={{0,24},{8,0},{16,8},{24,16},{1,25},{9,1},{17,9},{25,17},{2,26},{10... | collective-permute-start | bytes 786440 | tf_op jit(solution)/shard_map/ppermute | solution.py:246
  90.1 1.6 copy-start.6
  151.6 26.3 %copy-start = (bf16[16,176,256]{2,1,0:T(8,128)(2,1)}, bf16[16,176,256]{2,1,0:T(8,128)(2,1)S(1)}, u32[]{:S(2)}) copy-start(bf16[16,176,256]{2,1,0:T(8,128)(2,1)S(1)} %all_to_all.30.refs_2_) | copy-start | bytes 4325380
  162.3 13.3 %all-to-all-start.4 = ((bf16[8,48,256]{2,1,0:T(8,128)(2,1)}), bf16[8,48,256]{2,1,0:T(8,128)(2,1)S(1)}, u32[]{:S(2)}, u32[]{:S(2)}) async-start(bf16[8,48,256]{2,1,0:T(8,128)(2,1)} %broadcast_in_dim.8), calls=%async_computation.5 | async-start | bytes 393216 | tf_op jit(solution)/shard_map/all_to_all | solution.py:242
  166.8 22.9 %collective-permute-start.7 = (bf16[256,256]{1,0:T(8,128)(2,1)S(1)}, bf16[256,256]{1,0:T(8,128)(2,1)S(1)}, u32[]{:S(2)}, u32[]{:S(2)}) collective-permute-start(bf16[256,256]{1,0:T(8,128)(2,1)S(1)} %get-tuple-element.16), channel_id=1, source_target_pairs={{0,8},{8,16},{16,24},{24,0},{1,9},{9,17},{17,25},{25,1},{2,10},{10... | collective-permute-start | bytes 393224 | tf_op jit(solution)/shard_map/ppermute | solution.py:246
  169.0 20.7 %collective-permute-start.9 = (bf16[256,256]{1,0:T(8,128)(2,1)S(1)}, bf16[256,256]{1,0:T(8,128)(2,1)S(1)}, u32[]{:S(2)}, u32[]{:S(2)}) collective-permute-start(bf16[256,256]{1,0:T(8,128)(2,1)S(1)} %get-tuple-element.17), channel_id=1, source_target_pairs={{0,24},{8,0},{16,8},{24,16},{1,25},{9,1},{17,9},{25,17},{2,26},{10... | collective-permute-start | bytes 393224 | tf_op jit(solution)/shard_map/ppermute | solution.py:246
  173.3 16.4 %collective-permute-start.8 = (bf16[256,256]{1,0:T(8,128)(2,1)S(1)}, bf16[256,256]{1,0:T(8,128)(2,1)S(1)}, u32[]{:S(2)}, u32[]{:S(2)}) collective-permute-start(bf16[256,256]{1,0:T(8,128)(2,1)S(1)} %get-tuple-element.18), channel_id=1, source_target_pairs={{0,16},{8,24},{16,0},{24,8},{1,17},{9,25},{17,1},{25,9},{2,18},{10... | collective-permute-start | bytes 393224 | tf_op jit(solution)/shard_map/ppermute | solution.py:246
  177.9 13.5 %all-to-all-start.5 = ((bf16[8,48,256]{2,1,0:T(8,128)(2,1)}), bf16[8,48,256]{2,1,0:T(8,128)(2,1)S(1)}, u32[]{:S(2)}, u32[]{:S(2)}) async-start(bf16[8,48,256]{2,1,0:T(8,128)(2,1)} %shard_map.159), calls=%async_computation.6 | async-start | bytes 393216 | tf_op jit(solution)/shard_map/all_to_all | solution.py:242
  (3 other events, 2.7 us)
Sparse Core Ops, SparseCore 0:
  22.3 48.6 all-gather.2
  105.1 56.3 reduce-scatter.1

commit v6 on v5

--- a/solution.py
+++ b/solution.py
@@ -14,7 +14,7 @@
 NX, NZ, NY, NC = 4, 8, 8, 2
 NG = NY * NC
 BANDS = NX * NZ
-GRAD_ROWS = 48
+SPARE_ROWS = 16
 STORE = 8
 VMEM = pl.BlockSpec(memory_space=pltpu.VMEM)
 SMEM = pl.BlockSpec(memory_space=pltpu.SMEM)
@@ -82,49 +82,28 @@
         out_ref[g] = lax.dot_general(hot, feat, TN, preferred_element_type=F32).astype(BF)
 
 
-def band_of(index_ref, t, k):
+def spot_of(index_ref, t, k):
     index = index_ref[t, k]
-    return lax.shift_right_logical(index, 4), lax.shift_right_logical(index, 1) & (NZ - 1), index & 1
-
-
-def tile_spot(index_ref, x_ref, t, k):
-    x, z, odd = band_of(index_ref, t, k)
-    even_spot = z * NX + ((x_ref[0] - x) & (NX - 1))
-    odd_spot = BANDS + ((x - x_ref[0]) & (NX - 1)) * NZ + z
-    return jnp.where(odd == 0, even_spot, odd_spot)
-
-
-def term_spot(index_ref, t, k):
-    x, z, odd = band_of(index_ref, t, k)
-    return (z * NX + x) * 2 + odd
-
-
-def fetch_tiles(sources, tiles, sems):
-    starts = (0, BANDS, BANDS + NZ, BANDS + 2 * NZ, BANDS + 2 * NZ + NZ // 2, BANDS + 3 * NZ)
-    copies = [
-        pltpu.make_async_copy(source, tiles.at[pl.ds(start, source.shape[0])], sems.at[i])
-        for i, (source, start) in enumerate(zip(sources, starts, strict=True))
-    ]
-    for copy in copies:
-        copy.start()
-    return copies
-
-
-def forward_body(scalars, arrays, copies, outs, sources, tiles, tile_sems):
-    index_ref, count_ref, x_ref = scalars
+    z, x = lax.shift_right_logical(index, 1) & (NZ - 1), lax.shift_right_logical(index, 4)
+    return (z * NX + x) * 2 + (index & 1)
+
+
+def forward_body(scalars, arrays, copies, outs, gathered, tiles, tile_sem):
+    index_ref, count_ref = scalars
     blocks_ref, outer_ref, pre_ref, w_ref, dout_ref, feat_ref, wself_ref, cut_ref = arrays
-    out_ref, dagg_ref, back_ref, self_ref = outs
-    tile_copies = fetch_tiles(sources, tiles, tile_sems)
+    out_ref, dagg_ref, back_ref, part_ref, self_ref = outs
+    tile_copy = pltpu.make_async_copy(gathered[0], tiles.at[pl.ds(0, 2 * BANDS)], tile_sem)
+    tile_copy.start()
     slots = blocks_ref.shape[1]
     spare = 2 * BANDS
     tiles[spare] = jnp.zeros(tiles.shape[1:], BF)
     wait(copies)
-    wait(tile_copies)
+    tile_copy.wait()
     aggs, d_pres, d_aggs = [], [], []
     for t in range(2):
         rows = pl.ds(t * 128, 128)
         spots = [
-            jnp.where(k < count_ref[t], tile_spot(index_ref, x_ref, t, k), spare)
+            jnp.where(k < count_ref[t], spot_of(index_ref, t, k), spare)
             for k in range(slots)
         ]
         total = outer_ref[rows, :]
@@ -146,18 +125,18 @@
     width = d_pre.shape[1]
     groups = back_ref.shape[0]
     cut = cut_ref.shape[1] // groups
-    share = 2 * width // groups
-    rest = back_ref.shape[1] - cut - share
-    for i, left in enumerate((feat_ref[...], agg)):
-        grad = lax.dot_general(left, d_pre, TN, preferred_element_type=F32).astype(BF)
-        for g in range(groups // 2):
-            spot = i * groups // 2 + g
-            back_ref[spot, pl.ds(cut, share), :] = grad[g * share : (g + 1) * share]
+    share = part_ref.shape[1] - SPARE_ROWS
+    grads = [
+        lax.dot_general(left, d_pre, TN, preferred_element_type=F32).astype(BF)
+        for left in (feat_ref[...], agg)
+    ]
     bias = jnp.sum(d_pre.astype(F32), axis=0, keepdims=True)
-    row = lax.broadcasted_iota(jnp.int32, (rest, width), 0)
-    back_ref[0, pl.ds(cut + share, rest), :] = jnp.where(row == 0, bias, 0.0).astype(BF)
-    for g in range(1, groups):
-        back_ref[g, pl.ds(cut + share, rest), :] = jnp.zeros((rest, width), BF)
+    row = lax.broadcasted_iota(jnp.int32, (SPARE_ROWS, width), 0)
+    bias = jnp.where(row == 0, bias, 0.0).astype(BF)
+    for x in range(NX):
+        grad, at = grads[2 * x // NX], x % 2 * share
+        part_ref[x, pl.ds(0, share), :] = grad[at : at + share]
+        part_ref[x, pl.ds(share, SPARE_ROWS), :] = bias
     d_agg = jnp.concatenate(d_aggs, axis=0)
     for g in range(0, groups, 2):
         rows = lax.dot_general(
@@ -182,7 +161,7 @@
     for t in range(2):
         d_agg = dagg_ref[pl.ds(t * 128, 128), :]
         for k in range(slots):
-            spot = jnp.where(k < count_ref[t], term_spot(index_ref, t, k), spare)
+            spot = jnp.where(k < count_ref[t], spot_of(index_ref, t, k), spare)
             term = lax.dot_general(blocks_ref[t, k], d_agg, TN, preferred_element_type=F32)
             acc[spot] = acc[spot] + term
     stores = []
@@ -200,42 +179,56 @@
     wait(stores)
 
 
-def blocks_body(scalars, arrays, copies, outs, sources, tiles, tile_sems):
-    (index_ref, count_ref, x_ref), (dagg_ref,), (out_ref,) = scalars, arrays, outs
-    tile_copies = fetch_tiles(sources, tiles, tile_sems)
-    wait(copies)
-    wait(tile_copies)
+def blocks_body(scalars, arrays, copies, outs):
+    (index_ref, count_ref), (dagg_ref, tiles), (out_ref,) = scalars, arrays, outs
+    wait(copies)
     for t in range(2):
         d_agg = dagg_ref[pl.ds(t * 128, 128), :]
         for k in range(out_ref.shape[1]):
             live = jnp.where(k < count_ref[t], 1.0, 0.0)
-            tile = tiles[tile_spot(index_ref, x_ref, t, k)]
+            tile = tiles[spot_of(index_ref, t, k)]
             grad = lax.dot_general(d_agg, tile, NT, preferred_element_type=F32)
             out_ref[t, k] = (grad * live).astype(BF)
 
 
 def base_body(scalars, arrays, copies, outs):
-    (count_ref,), (rows_ref, back_ref, self_ref), (out_ref,) = scalars, arrays, outs
-    cut = rows_ref.shape[1]
+    (count_ref,), (rows_ref, back_ref, self_ref, *term_refs), (out_ref,) = scalars, arrays, outs
     wait(copies)
     total = self_ref[...]
+    for term_ref in term_refs:
+        total = total + term_ref[...].astype(F32)
     for g in range(0, back_ref.shape[0], 2):
         hot = jnp.concatenate(
             [hot_columns(rows_ref, count_ref, g + i, total.shape[0]) for i in range(2)], axis=1
         )
-        rows = jnp.concatenate([back_ref[g + i, pl.ds(0, cut), :] for i in range(2)], axis=0)
+        rows = jnp.concatenate([back_ref[g], back_ref[g + 1]], axis=0)
         total = total + jnp.dot(hot, rows, preferred_element_type=F32)
-    out_ref[...] = total
-
-
-def sum_body(scalars, arrays, copies, outs):
+    out_ref[...] = total.astype(BF)
+
+
+def share_body(scalars, arrays, copies, outs):
     (parts_ref,), (out_ref,) = arrays, outs
     wait(copies)
     total = parts_ref[0].astype(F32)
     for i in range(1, parts_ref.shape[0]):
         total = total + parts_ref[i].astype(F32)
+    total = total.astype(BF)
+    share = out_ref.shape[1] - SPARE_ROWS
+    last = total.shape[0] - SPARE_ROWS
     for i in range(out_ref.shape[0]):
-        out_ref[i] = total.astype(BF)
+        out_ref[i, pl.ds(0, share), :] = total[i * share : (i + 1) * share]
+        out_ref[i, pl.ds(share, SPARE_ROWS), :] = total[last:]
+
+
+def gate(x, after):
+    return pl.pallas_call(
+        lambda x_ref, after_ref, out_ref: None,
+        out_shape=sds(x.shape, x.dtype),
+        in_specs=[HBM, HBM],
+        out_specs=HBM,
+        input_output_aliases={0: 0},
+        compiler_params=pltpu.CompilerParams(vmem_limit_bytes=60 << 20),
+    )(x, after)
 
 
 def a2a(x, axis):
@@ -258,16 +251,8 @@
     node_bf, node_f32 = sds((nodes, width), BF), sds((nodes, width), F32)
     cut_bf = sds((NG, cut, width), BF)
 
-    even, odd = features[:128], features[128:]
-    own = a2a(jnp.broadcast_to(odd[None], (NZ, *odd.shape)), "z")
-    even = jnp.stack([even] + [shift(even, "x", NX, by) for by in range(1, NX)])
-    even = lax.all_gather(even, "z", axis=0, tiled=True)
-    left, right = shift(own, "x", NX, 1), shift(own, "x", NX, -1)
-    far_low = shift(left[: NZ // 2], "x", NX, 1)
-    far_high = shift(right[NZ // 2 :], "x", NX, -1)
-    gathered = (even, own, right, far_low, far_high, left)
-    me = lax.axis_index("x")
-    my_x = me.astype(jnp.int32).reshape(1)
+    gathered = lax.all_gather(features, "x", axis=0, tiled=True)
+    gathered = lax.all_gather(gathered, "z", axis=0, tiled=True).reshape(2 * BANDS, 128, width)
 
     (outgoing,) = call(
         pick_body, [send_count], [rows2, features], [cut_bf], flops=2 * NG * cut * width * nodes,
@@ -276,14 +261,13 @@
     outer = jnp.dot(cut_weight, arrived, preferred_element_type=F32)
     own_pre = jnp.dot(features, w_self, preferred_element_type=F32) + bias
 
-    tiles = pltpu.VMEM((2 * BANDS + 1, 128, width), BF)
-    output, d_agg, back, self_back = call(
+    output, d_agg, back, part, self_back = call(
         forward_body,
-        [block_index, block_count, my_x],
+        [block_index, block_count],
         [block_values, outer, own_pre, w_neigh, d_out, features, w_self, cut_weight],
-        [node_bf, node_bf, sds((NG, cut + GRAD_ROWS, width), BF), node_f32],
-        scratch=[tiles, pltpu.SemaphoreType.DMA((6,))],
-        direct=gathered,
+        [node_bf, node_bf, cut_bf, sds((NX, 2 * width // NX + SPARE_ROWS, width), BF), node_f32],
+        scratch=[pltpu.VMEM((2 * BANDS + 1, 128, width), BF), pltpu.SemaphoreType.DMA],
+        direct=[gathered],
         flops=1 << 29,
     )
     (terms,) = call(
@@ -302,33 +286,33 @@
 
     terms = lax.psum_scatter(terms.reshape(NZ, NX * nodes, width), "z", scatter_dimension=0)
     terms = terms.reshape(NX, nodes, width)
-    own_back = lax.dynamic_index_in_dim(terms, me, 0, keepdims=False).astype(F32)
+    me = lax.axis_index("x")
+    own_terms = [lax.dynamic_index_in_dim(terms, me, 0, keepdims=False)]
     for by in range(1, NX):
         away = lax.dynamic_index_in_dim(terms, (me + by) & (NX - 1), 0, keepdims=False)
-        own_back = own_back + shift(away, "x", NX, by).astype(F32)
-
-    returned = a2a(back, ("y", "c"))
-    part = jnp.sum(returned[:, cut:].astype(F32), axis=0).astype(BF)
-    part = a2a(jnp.broadcast_to(part[None], (NX, *part.shape)), "x")
+        own_terms.append(shift(away, "x", NX, by))
+
+    part = a2a(part, "x")
+    (part,) = call(
+        share_body, [], [part], [sds((NZ, 2 * width // BANDS + SPARE_ROWS, width), BF)]
+    )
+    part = jnp.sum(a2a(part, "z").astype(F32), axis=0).astype(BF)
+    part = a2a(jnp.broadcast_to(part[None], (NG, *part.shape)), ("y", "c"))
     part = jnp.sum(part.astype(F32), axis=0).astype(BF)
-    part = a2a(jnp.broadcast_to(part[None], (NZ, *part.shape)), "z")
-    (part,) = call(sum_body, [], [part], [sds((NY, GRAD_ROWS, width), BF)], extra=[terms])
-    part = a2a(part, "y")
-    grads = lax.all_gather(part, "c", axis=1).reshape(NG, GRAD_ROWS, width)
-    grads = grads.astype(F32) * scale
-    share = 2 * width // NG
-    weight_grads = grads[:, :share].reshape(2, width, width)
+    returned = a2a(gate(back, part), ("y", "c"))
+    part = gate(lax.all_gather(part, "x", axis=0), terms)
+    part = lax.all_gather(part, "z", axis=1).astype(F32) * scale
+    share = 2 * width // BANDS
+    weight_grads = part[:, :, :share].reshape(2, width, width)
 
     (grad_blocks,) = call(
-        blocks_body, [block_index, block_count, my_x], [d_agg], [sds(block_values.shape, BF)],
-        scratch=[tiles, pltpu.SemaphoreType.DMA((6,))], direct=gathered,
+        blocks_body, [block_index, block_count], [d_agg, gathered], [sds(block_values.shape, BF)],
         flops=2 * tiles_here * slots * 128 * 128 * width,
     )
-    (base,) = call(
-        base_body, [send_count], [rows2, returned, self_back], [node_f32],
+    (d_features,) = call(
+        base_body, [send_count], [rows2, returned, self_back, *own_terms], [node_bf],
         flops=2 * NG * cut * width * nodes,
     )
-    d_features = (base + own_back).astype(BF)
 
     return (
         output,
@@ -336,7 +320,7 @@
         grad_blocks,
         weight_grads[0],
         weight_grads[1],
-        grads[0, share],
+        part[0, 0, share],
     )
 
 

time: 204 us -> 214 us (1.049)
  the two profiles are of different devices: /device:TPU:1 before, /device:TPU:10 now
where the time goes in v6:
time: 214 us; the launch traced here: 213 us
  blocking collectives  93.3 us (44%)
  waiting for transfers between devices  48.9 us (23%)
  Pallas kernels  25.6 us (12%)
  starting transfers between devices  24.2 us (11%)
  between operations  14.3 us (7%)
  local copies, waits for them, and re-layouts  4.28 us (2%)
    all_to_all x3, blocking collectives, a2a(): return lax.all_to_all(x, axis, 0, 0, tiled=True)  41.6 us
    all_gather x1, blocking collectives, local(): part = lax.all_gather(part, 'z', axis=1).astype(F32) * scale  25.7 us
    pallas_call x6, Pallas kernels, call(): pl.pallas_call(kernel, out_shape=tuple(outs), in_specs=[SMEM] * first + [...  25.6 us
    all_gather x1, waiting for transfers between devices, local(): lax.all_gather(gathered, 'z', axis=0, tiled=True)  25.1 us
    all_to_all x2, waiting for transfers between devices, a2a(): return lax.all_to_all(x, axis, 0, 0, tiled=True)  23.8 us
    all_gather x1, blocking collectives, local(): gathered = lax.all_gather(features, 'x', axis=0, tiled=True)  13.9 us
    all_to_all x2, starting transfers between devices, a2a(): return lax.all_to_all(x, axis, 0, 0, tiled=True)  13.8 us
    all_gather x1, blocking collectives, local(): part = gate(lax.all_gather(part, 'x', axis=0), terms)  12 us
  transfers between devices with their start and end apart: 7, of which 2 were waited for; matrix products, arithmetic and copies ran while one was open for 3% of the time, Pallas kernels for 5%

profile of v6, /device:TPU:10, one launch (start us, length us, event | category | flops | bytes accessed | tf_op | source)
XLA Modules:
  0.0 213.3 jit_solution(7152248357799269192)
XLA Ops:
  7.3 13.9 %all_gather.18 = bf16[1024,256]{1,0:T(8,128)(2,1)} all-gather(bf16[256,256]{1,0:T(8,128)(2,1)} %refs_7_.1), channel_id=1, replica_groups=mesh['y'=8,'c'=2,'x'=4,'z'=8] {'x'}, dimensions={0}, use_global_device_ids=true | all-gather | bytes 655360 | tf_op jit(solution)/shard_map/all_gather | solution.py:254
  21.2 3.1 %shard_map.154 = bf16[16,128,256]{2,1,0:T(8,128)(2,1)} custom-call(s32[1,16]{1,0:T(1,128)} %refs_0_.8, s32[16,128]{1,0:T(8,128)} %bitcast.35, bf16[256,256]{1,0:T(8,128)(2,1)} %refs_7_.1), custom_call_target="tpu_custom_call" | custom-call | flops 268435456 | bytes 1187840 | tf_op jit(solution)/shard_map/pallas_call | solution.py:48
  24.3 8.6 %all-to-all-start = ((bf16[16,128,256]{2,1,0:T(8,128)(2,1)}), bf16[16,128,256]{2,1,0:T(8,128)(2,1)S(1)}, u32[]{:S(2)}, u32[]{:S(2)}) async-start(bf16[16,128,256]{2,1,0:T(8,128)(2,1)} %shard_map.154), calls=%async_computation | async-start | bytes 2097152 | tf_op jit(solution)/shard_map/all_to_all | solution.py:235
  32.9 0.9 convolution_add_fusion.refs_4_
  33.8 23.8 %all-to-all-done = bf16[16,128,256]{2,1,0:T(8,128)(2,1)S(1)} async-done(((bf16[16,128,256]{2,1,0:T(8,128)(2,1)}), bf16[16,128,256]{2,1,0:T(8,128)(2,1)S(1)}, u32[]{:S(2)}, u32[]{:S(2)}) %all-to-all-start) | async-done | bytes 1048608 | tf_op jit(solution)/shard_map/all_to_all | solution.py:235
  57.6 1.1 convolution_bitcast_fusion.refs_3_
  58.7 25.1 %all-gather.4.cloned.1.call-done = bf16[8192,256]{1,0:T(8,128)(2,1)} async-done(((bf16[1024,256]{1,0:T(8,128)(2,1)}), bf16[8192,256]{1,0:T(8,128)(2,1)}) %all-gather.4.cloned.1.call-update) | async-done | bytes 4194320 | tf_op jit(solution)/shard_map/all_gather | solution.py:255
  83.8 7.0 %shard_map.155 = (bf16[256,256]{1,0:T(8,128)(2,1)}, bf16[256,256]{1,0:T(8,128)(2,1)}, bf16[16,128,256]{2,1,0:T(8,128)(2,1)}, bf16[4,144,256]{2,1,0:T(8,128)(2,1)}, f32[256,256]{1,0:T(8,128)}) custom-call(s32[2,24]{1,0:T(2,128)} %refs_0_.9, s32[2]{0:T(128)} %refs_1_.5, bf16[2,24,128,128]{3,2,1,0:T(8,128)(2,1)} %refs_2_.5, ...), custom_call_target="tpu_custom_call" | custom-call | flops 536870912 | bytes 9732096 | tf_op jit(solution)/shard_map/pallas_call | solution.py:48
  90.9 5.4 %shard_map.158 = bf16[64,128,256]{2,1,0:T(8,128)(2,1)} custom-call(s32[2,24]{1,0:T(2,128)} %refs_0_.9, s32[2]{0:T(128)} %refs_1_.5, bf16[2,24,128,128]{3,2,1,0:T(8,128)(2,1)} %refs_2_.5, bf16[256,256]{1,0:T(8,128)(2,1)} %get-tuple-element.15.refs_3_.refs_2_), custom_call_target="tpu_custom_call" | custom-call | flops 536870912 | bytes 5898240 | tf_op jit(solution)/shard_map/pallas_call | solution.py:48
  96.3 10.3 %all_to_all.25.refs_0_ = bf16[4,144,256]{2,1,0:T(8,128)(2,1)} all-to-all(bf16[4,144,256]{2,1,0:T(8,128)(2,1)S(1)} %copy-done.4), channel_id=1, replica_groups=mesh['y'=8,'c'=2,'x'=4,'z'=8] {'x'}, dimensions={0} | all-to-all | bytes 589824 | tf_op jit(solution)/shard_map/all_to_all | solution.py:235
  106.6 1.7 shard_map.156
  108.3 14.6 %all_to_all.26 = bf16[8,32,256]{2,1,0:T(8,128)(2,1)S(1)} all-to-all(bf16[8,32,256]{2,1,0:T(8,128)(2,1)} %shard_map.156), channel_id=1, replica_groups=mesh['y'=8,'c'=2,'x'=4,'z'=8] {'z'}, dimensions={0} | all-to-all | bytes 262144 | tf_op jit(solution)/shard_map/all_to_all | solution.py:235
  122.9 16.7 %all_to_all.27 = bf16[16,32,256]{2,1,0:T(8,128)(2,1)S(1)} all-to-all(bf16[16,32,256]{2,1,0:T(8,128)(2,1)S(1)} %broadcast_in_dim.2), channel_id=1, replica_groups=mesh['y'=8,'c'=2,'x'=4,'z'=8] {'y','c'}, dimensions={0} | all-to-all | bytes 524288 | tf_op jit(solution)/shard_map/all_to_all | solution.py:235
  140.3 5.2 %all-to-all-start.4 = ((bf16[16,128,256]{2,1,0:T(8,128)(2,1)}), bf16[16,128,256]{2,1,0:T(8,128)(2,1)S(1)}, u32[]{:S(2)}, u32[]{:S(2)}) async-start(bf16[16,128,256]{2,1,0:T(8,128)(2,1)} %shard_map.157), calls=%async_computation.4 | async-start | bytes 2097152 | tf_op jit(solution)/shard_map/all_to_all | solution.py:235
  145.5 5.2 %shard_map.160 = bf16[2,24,128,128]{3,2,1,0:T(8,128)(2,1)} custom-call(s32[2,24]{1,0:T(2,128)} %refs_0_.9, s32[2]{0:T(128)} %refs_1_.5, bf16[256,256]{1,0:T(8,128)(2,1)} %get-tuple-element.15.refs_3_.refs_2_, bf16[64,128,256]{2,1,0:T(8,128)(2,1)} %bitcast.25), custom_call_target="tpu_custom_call" | custom-call | flops 402653184 | bytes 5898240 | tf_op jit(solution)/shard_map/pallas_call | solution.py:48
  150.7 12.0 %all-gather = bf16[128,256]{1,0:T(8,128)(2,1)} all-gather(bf16[32,256]{1,0:T(8,128)(2,1)S(1)} %copy-done.5), channel_id=2, replica_groups=mesh['y'=8,'c'=2,'x'=4,'z'=8] {'x'}, dimensions={0}, use_global_device_ids=true | all-gather | bytes 81920 | tf_op jit(solution)/shard_map/all_gather | solution.py:303
  162.7 1.8 dynamic-slice_bitcast_fusion
  164.5 4.0 %collective-permute-start.2 = (bf16[256,256]{1,0:T(8,128)(2,1)S(1)}, bf16[256,256]{1,0:T(8,128)(2,1)S(1)}, u32[]{:S(2)}, u32[]{:S(2)}) collective-permute-start(bf16[256,256]{1,0:T(8,128)(2,1)S(1)} %get-tuple-element.18), channel_id=1, source_target_pairs={{0,24},{8,0},{16,8},{24,16},{1,25},{9,1},{17,9},{25,17},{2,26},{10... | collective-permute-start | bytes 393224 | tf_op jit(solution)/shard_map/ppermute | solution.py:239
  168.4 2.8 %collective-permute-start.1 = (bf16[256,256]{1,0:T(8,128)(2,1)S(1)}, bf16[256,256]{1,0:T(8,128)(2,1)S(1)}, u32[]{:S(2)}, u32[]{:S(2)}) collective-permute-start(bf16[256,256]{1,0:T(8,128)(2,1)S(1)} %get-tuple-element.19), channel_id=1, source_target_pairs={{0,16},{8,24},{16,0},{24,8},{1,17},{9,25},{17,1},{25,9},{2,18},{10... | collective-permute-start | bytes 393224 | tf_op jit(solution)/shard_map/ppermute | solution.py:239
  171.2 3.7 %collective-permute-start = (bf16[256,256]{1,0:T(8,128)(2,1)S(1)}, bf16[256,256]{1,0:T(8,128)(2,1)S(1)}, u32[]{:S(2)}, u32[]{:S(2)}) collective-permute-start(bf16[256,256]{1,0:T(8,128)(2,1)S(1)} %get-tuple-element.20), channel_id=1, source_target_pairs={{0,8},{8,16},{16,24},{24,0},{1,9},{9,17},{17,25},{25,1},{2,10},{10... | collective-permute-start | bytes 393224 | tf_op jit(solution)/shard_map/ppermute | solution.py:239
  174.9 25.7 %all-gather.1 = bf16[4,256,256]{2,1,0:T(8,128)(2,1)S(1)} all-gather(bf16[4,32,256]{2,1,0:T(8,128)(2,1)} %shard_map.161), channel_id=3, replica_groups=mesh['y'=8,'c'=2,'x'=4,'z'=8] {'z'}, dimensions={1}, use_global_device_ids=true | all-gather | bytes 589824 | tf_op jit(solution)/shard_map/all_gather | solution.py:304
  201.3 0.8 fusion
  202.2 0.9 copy-done.1
  203.2 3.3 %shard_map.159 = bf16[256,256]{1,0:T(8,128)(2,1)} custom-call(s32[1,16]{1,0:T(1,128)} %refs_0_.8, s32[16,128]{1,0:T(8,128)} %bitcast.36, bf16[16,128,256]{2,1,0:T(8,128)(2,1)} %copy-done.1, f32[256,256]{1,0:T(8,128)} %get-tuple-element.14.refs_3_, bf16[256,256]{1,0:T(8,128)(2,1)} %get-tuple-element.21.refs_4_, bf16[256,256]{1,0:T(8,128)(2,1)} %copy-done.8, ...), custom_call_target="tpu_custom_call" | custom-call | flops 268435456 | bytes 1974272 | tf_op jit(solution)/shard_map/pallas_call | solution.py:48
  (35 shorter events, 1.6 us)
Async XLA Ops:
  7.2 25.7 %copy-start.2 = (bf16[256,256]{1,0:T(8,128)(2,1)S(1)}, bf16[256,256]{1,0:T(8,128)(2,1)}, u32[]{:S(2)}) copy-start(bf16[256,256]{1,0:T(8,128)(2,1)} %refs_7_.1) | copy-start | bytes 393220
  7.2 25.7 %copy-start.3 = (bf16[256,256]{1,0:T(8,128)(2,1)S(1)}, bf16[256,256]{1,0:T(8,128)(2,1)}, u32[]{:S(2)}) copy-start(bf16[256,256]{1,0:T(8,128)(2,1)} %refs_8_.1) | copy-start | bytes 393220
  7.2 25.7 %copy-start.9 = (f32[256]{0:T(256)S(1)}, f32[256]{0:T(256)}, u32[]{:S(2)}) copy-start(f32[256]{0:T(256)} %param.20) | copy-start | bytes 3076
  7.2 50.4 %copy-start = (bf16[256,2048]{1,0:T(8,128)(2,1)S(1)}, bf16[256,2048]{1,0:T(8,128)(2,1)}, u32[]{:S(2)}) copy-start(bf16[256,2048]{1,0:T(8,128)(2,1)} %refs_9_.1) | copy-start | bytes 3145732
  7.2 76.6 %all-gather.4.cloned.1.call-start = ((), (), s32[]{:S(2)}) async-start(), calls=%async_computation.6 | async-start | bytes 4718592 | tf_op jit(solution)/shard_map/all_gather | solution.py:255
  24.3 33.3 %all-to-all-start = ((bf16[16,128,256]{2,1,0:T(8,128)(2,1)}), bf16[16,128,256]{2,1,0:T(8,128)(2,1)S(1)}, u32[]{:S(2)}, u32[]{:S(2)}) async-start(bf16[16,128,256]{2,1,0:T(8,128)(2,1)} %shard_map.154), calls=%async_computation | async-start | bytes 2097152 | tf_op jit(solution)/shard_map/all_to_all | solution.py:235
  32.8 129.8 %reduce-scatter.2.cloned.1.call-start = ((), (), s32[]{:S(2)}) async-start(), calls=%async_computation.7 | async-start | bytes 4718592 | tf_op jit(solution)/shard_map/reduce_scatter | solution.py:287
  90.8 5.5 %copy-start.4 = (bf16[4,144,256]{2,1,0:T(8,128)(2,1)S(1)}, bf16[4,144,256]{2,1,0:T(8,128)(2,1)}, u32[]{:S(2)}) copy-start(bf16[4,144,256]{2,1,0:T(8,128)(2,1)} %get-tuple-element.13) | copy-start | bytes 884740
  140.3 10.4 %copy-start.5 = (bf16[32,256]{1,0:T(8,128)(2,1)S(1)}, bf16[32,256]{1,0:T(8,128)(2,1)}, u32[]{:S(2)}) copy-start(bf16[32,256]{1,0:T(8,128)(2,1)} %reduce_sum.25.after_ref) | copy-start | bytes 49156
  140.3 61.8 %all-to-all-start.4 = ((bf16[16,128,256]{2,1,0:T(8,128)(2,1)}), bf16[16,128,256]{2,1,0:T(8,128)(2,1)S(1)}, u32[]{:S(2)}, u32[]{:S(2)}) async-start(bf16[16,128,256]{2,1,0:T(8,128)(2,1)} %shard_map.157), calls=%async_computation.4 | async-start | bytes 2097152 | tf_op jit(solution)/shard_map/all_to_all | solution.py:235
  164.5 37.7 %collective-permute-start.2 = (bf16[256,256]{1,0:T(8,128)(2,1)S(1)}, bf16[256,256]{1,0:T(8,128)(2,1)S(1)}, u32[]{:S(2)}, u32[]{:S(2)}) collective-permute-start(bf16[256,256]{1,0:T(8,128)(2,1)S(1)} %get-tuple-element.18), channel_id=1, source_target_pairs={{0,24},{8,0},{16,8},{24,16},{1,25},{9,1},{17,9},{25,17},{2,26},{10... | collective-permute-start | bytes 393224 | tf_op jit(solution)/shard_map/ppermute | solution.py:239
  168.4 33.7 %collective-permute-start.1 = (bf16[256,256]{1,0:T(8,128)(2,1)S(1)}, bf16[256,256]{1,0:T(8,128)(2,1)S(1)}, u32[]{:S(2)}, u32[]{:S(2)}) collective-permute-start(bf16[256,256]{1,0:T(8,128)(2,1)S(1)} %get-tuple-element.19), channel_id=1, source_target_pairs={{0,16},{8,24},{16,0},{24,8},{1,17},{9,25},{17,1},{25,9},{2,18},{10... | collective-permute-start | bytes 393224 | tf_op jit(solution)/shard_map/ppermute | solution.py:239
  171.2 31.0 %collective-permute-start = (bf16[256,256]{1,0:T(8,128)(2,1)S(1)}, bf16[256,256]{1,0:T(8,128)(2,1)S(1)}, u32[]{:S(2)}, u32[]{:S(2)}) collective-permute-start(bf16[256,256]{1,0:T(8,128)(2,1)S(1)} %get-tuple-element.20), channel_id=1, source_target_pairs={{0,8},{8,16},{16,24},{24,0},{1,9},{9,17},{17,25},{25,1},{2,10},{10... | collective-permute-start | bytes 393224 | tf_op jit(solution)/shard_map/ppermute | solution.py:239
  202.1 1.0 copy-start.1
  202.1 1.0 copy-start.6
  202.2 1.1 copy-start.7
  202.2 1.1 copy-start.8
Sparse Core Ops, SparseCore 0:
  21.3 62.4 all-gather.3
  96.4 59.6 reduce-scatter.1

commit v7 on v6

--- a/solution.py
+++ b/solution.py
@@ -1,3 +1,4 @@
+import functools
 import math
 
 import jax
@@ -88,15 +89,23 @@
     return (z * NX + x) * 2 + (index & 1)
 
 
-def forward_body(scalars, arrays, copies, outs, gathered, tiles, tile_sem):
+def main_body(
+    scalars, arrays, copies, outs, gathered, tiles, acc, terms, tile_sem, term_sems
+):
     index_ref, count_ref = scalars
     blocks_ref, outer_ref, pre_ref, w_ref, dout_ref, feat_ref, wself_ref, cut_ref = arrays
-    out_ref, dagg_ref, back_ref, part_ref, self_ref = outs
+    out_ref, dagg_ref, back_ref, part_ref, self_ref, term_ref = outs
     tile_copy = pltpu.make_async_copy(gathered[0], tiles.at[pl.ds(0, 2 * BANDS)], tile_sem)
     tile_copy.start()
     slots = blocks_ref.shape[1]
     spare = 2 * BANDS
     tiles[spare] = jnp.zeros(tiles.shape[1:], BF)
+
+    def clear(i, carry):
+        acc[i] = jnp.zeros(acc.shape[1:], F32)
+        return carry
+
+    lax.fori_loop(0, spare, clear, 0)
     wait(copies)
     tile_copy.wait()
     aggs, d_pres, d_aggs = [], [], []
@@ -118,9 +127,24 @@
         d_pre = (dout_ref[rows, :].astype(F32) * sig * (1.0 + pre * (1.0 - sig))).astype(BF)
         d_agg = lax.dot_general(d_pre, w_ref[...], NT, preferred_element_type=F32).astype(BF)
         dagg_ref[rows, :] = d_agg
+        for k in range(slots):
+            term = lax.dot_general(blocks_ref[t, k], d_agg, TN, preferred_element_type=F32)
+            acc[spots[k]] = acc[spots[k]] + term
         d_aggs.append(d_agg)
         aggs.append(agg)
         d_pres.append(d_pre)
+    stores = []
+    for c in range(STORE):
+        part = pl.ds(c * (spare // STORE), spare // STORE)
+
+        def convert(i, carry):
+            terms[i] = acc[i].astype(BF)
+            return carry
+
+        lax.fori_loop(part.start, part.start + part.size, convert, 0)
+        store = pltpu.make_async_copy(terms.at[part], term_ref.at[part], term_sems.at[c])
+        store.start()
+        stores.append(store)
     agg, d_pre = jnp.concatenate(aggs, axis=0), jnp.concatenate(d_pres, axis=0)
     width = d_pre.shape[1]
     groups = back_ref.shape[0]
@@ -145,37 +169,6 @@
         back_ref[g, pl.ds(0, cut), :] = rows[:cut]
         back_ref[g + 1, pl.ds(0, cut), :] = rows[cut:]
     self_ref[...] = lax.dot_general(d_pre, wself_ref[...], NT, preferred_element_type=F32)
-
-
-def terms_body(scalars, arrays, copies, outs, acc, terms, sems):
-    (index_ref, count_ref), (blocks_ref, dagg_ref), (term_ref,) = scalars, arrays, outs
-    slots = blocks_ref.shape[1]
-    spare = 2 * BANDS
-
-    def clear(i, carry):
-        acc[i] = jnp.zeros(acc.shape[1:], F32)
-        return carry
-
-    lax.fori_loop(0, spare, clear, 0)
-    wait(copies)
-    for t in range(2):
-        d_agg = dagg_ref[pl.ds(t * 128, 128), :]
-        for k in range(slots):
-            spot = jnp.where(k < count_ref[t], spot_of(index_ref, t, k), spare)
-            term = lax.dot_general(blocks_ref[t, k], d_agg, TN, preferred_element_type=F32)
-            acc[spot] = acc[spot] + term
-    stores = []
-    for c in range(STORE):
-        part = pl.ds(c * (spare // STORE), spare // STORE)
-
-        def convert(i, carry):
-            terms[i] = acc[i].astype(BF)
-            return carry
-
-        lax.fori_loop(part.start, part.start + part.size, convert, 0)
-        store = pltpu.make_async_copy(terms.at[part], term_ref.at[part], sems.at[c])
-        store.start()
-        stores.append(store)
     wait(stores)
 
 
@@ -196,7 +189,7 @@
     wait(copies)
     total = self_ref[...]
     for term_ref in term_refs:
-        total = total + term_ref[...].astype(F32)
+        total = total + term_ref[pl.ds(0, total.shape[0]), :].astype(F32)
     for g in range(0, back_ref.shape[0], 2):
         hot = jnp.concatenate(
             [hot_columns(rows_ref, count_ref, g + i, total.shape[0]) for i in range(2)], axis=1
@@ -204,6 +197,21 @@
         rows = jnp.concatenate([back_ref[g], back_ref[g + 1]], axis=0)
         total = total + jnp.dot(hot, rows, preferred_element_type=F32)
     out_ref[...] = total.astype(BF)
+
+
+def grads_body(scale, scalars, arrays, copies, outs):
+    (x_ref,) = scalars
+    wait(copies)
+    share = sum(out_ref.shape[0] for out_ref in outs) // len(arrays)
+    for by, rows_ref in enumerate(arrays):
+        x = (x_ref[0] - by) & (NX - 1)
+        grads = rows_ref[pl.ds(rows_ref.shape[0] - share, share), :].astype(F32) * scale
+        for i, out_ref in enumerate(outs):
+            held = out_ref.shape[0] // share
+
+            @pl.when(lax.div(x, held) == i)
+            def _(out_ref=out_ref, grads=grads, spot=(x & (held - 1)) * share):
+                out_ref[pl.ds(pl.multiple_of(spot, share), share), :] = grads
 
 
 def share_body(scalars, arrays, copies, outs):
@@ -261,56 +269,56 @@
     outer = jnp.dot(cut_weight, arrived, preferred_element_type=F32)
     own_pre = jnp.dot(features, w_self, preferred_element_type=F32) + bias
 
-    output, d_agg, back, part, self_back = call(
-        forward_body,
+    outs = [
+        node_bf, node_bf, cut_bf, sds((NX, 2 * width // NX + SPARE_ROWS, width), BF), node_f32,
+        sds(gathered.shape, BF),
+    ]
+    spared = (2 * BANDS + 1, 128, width)
+    output, d_agg, back, part, self_back, terms = call(
+        main_body,
         [block_index, block_count],
         [block_values, outer, own_pre, w_neigh, d_out, features, w_self, cut_weight],
-        [node_bf, node_bf, cut_bf, sds((NX, 2 * width // NX + SPARE_ROWS, width), BF), node_f32],
-        scratch=[pltpu.VMEM((2 * BANDS + 1, 128, width), BF), pltpu.SemaphoreType.DMA],
-        direct=[gathered],
-        flops=1 << 29,
-    )
-    (terms,) = call(
-        terms_body,
-        [block_index, block_count],
-        [block_values, d_agg],
-        [sds((2 * BANDS, 128, width), BF)],
-        out_specs=[HBM],
+        outs,
+        out_specs=[VMEM] * (len(outs) - 1) + [HBM],
         scratch=[
-            pltpu.VMEM((2 * BANDS + 1, 128, width), F32),
-            pltpu.VMEM((2 * BANDS, 128, width), BF),
+            pltpu.VMEM(spared, BF),
+            pltpu.VMEM(spared, F32),
+            pltpu.VMEM(gathered.shape, BF),
+            pltpu.SemaphoreType.DMA,
             pltpu.SemaphoreType.DMA((STORE,)),
         ],
-        flops=1 << 29,
+        direct=[gathered],
+        flops=1 << 30,
     )
 
     terms = lax.psum_scatter(terms.reshape(NZ, NX * nodes, width), "z", scatter_dimension=0)
     terms = terms.reshape(NX, nodes, width)
     me = lax.axis_index("x")
-    own_terms = [lax.dynamic_index_in_dim(terms, me, 0, keepdims=False)]
-    for by in range(1, NX):
-        away = lax.dynamic_index_in_dim(terms, (me + by) & (NX - 1), 0, keepdims=False)
-        own_terms.append(shift(away, "x", NX, by))
-
+
+    share = 2 * width // BANDS
     part = a2a(part, "x")
-    (part,) = call(
-        share_body, [], [part], [sds((NZ, 2 * width // BANDS + SPARE_ROWS, width), BF)]
-    )
+    (part,) = call(share_body, [], [part], [sds((NZ, share + SPARE_ROWS, width), BF)])
     part = jnp.sum(a2a(part, "z").astype(F32), axis=0).astype(BF)
     part = a2a(jnp.broadcast_to(part[None], (NG, *part.shape)), ("y", "c"))
     part = jnp.sum(part.astype(F32), axis=0).astype(BF)
     returned = a2a(gate(back, part), ("y", "c"))
-    part = gate(lax.all_gather(part, "x", axis=0), terms)
-    part = lax.all_gather(part, "z", axis=1).astype(F32) * scale
-    share = 2 * width // BANDS
-    weight_grads = part[:, :, :share].reshape(2, width, width)
+    grads = lax.all_gather(part[:share], "z", axis=0, tiled=True)
+    moved = []
+    for by in range(NX):
+        rows = lax.dynamic_index_in_dim(terms, (me + by) & (NX - 1), 0, keepdims=False)
+        rows = jnp.concatenate([rows, grads], axis=0)
+        moved.append(shift(rows, "x", NX, by) if by else rows)
+    grad_self, grad_neigh = call(
+        functools.partial(grads_body, scale), [me.astype(jnp.int32).reshape(1)], moved,
+        [sds((width, width), F32)] * 2,
+    )
 
     (grad_blocks,) = call(
         blocks_body, [block_index, block_count], [d_agg, gathered], [sds(block_values.shape, BF)],
-        flops=2 * tiles_here * slots * 128 * 128 * width,
+        extra=[moved[0]], flops=2 * tiles_here * slots * 128 * 128 * width,
     )
     (d_features,) = call(
-        base_body, [send_count], [rows2, returned, self_back, *own_terms], [node_bf],
+        base_body, [send_count], [rows2, returned, self_back, *moved], [node_bf],
         flops=2 * NG * cut * width * nodes,
     )
 
@@ -318,9 +326,9 @@
         output,
         d_features,
         grad_blocks,
-        weight_grads[0],
-        weight_grads[1],
-        part[0, 0, share],
+        grad_self,
+        grad_neigh,
+        part[share].astype(F32) * scale,
     )
 
 

time: 214 us -> 202 us (0.944)
  blocking collectives: 93.3 us -> 80.3 us
    all_gather x2 -> x1, blocking collectives: 37.7 us -> 24.8 us  [local(): grads = lax.all_gather(part[:share], 'z', axis=0, tiled=True)]
  transfers between devices with their start and end apart: 7 -> 7, of which waited for: 2 -> 2; matrix products, arithmetic and copies ran while one was open for 3% -> 3% of each run, Pallas kernels for 5% -> 6%
where the time goes in v7:
time: 202 us; the launch traced here: 201 us
  blocking collectives  80.3 us (40%)
  waiting for transfers between devices  48.9 us (24%)
  Pallas kernels  25.5 us (13%)
  starting transfers between devices  24.3 us (12%)
  between operations  14.3 us (7%)
  local copies, waits for them, and re-layouts  3.87 us (2%)
  matrix products  2.03 us (1%)
    all_to_all x3, blocking collectives, a2a(): return lax.all_to_all(x, axis, 0, 0, tiled=True)  41.6 us
    pallas_call x6, Pallas kernels, call(): pl.pallas_call(kernel, out_shape=tuple(outs), in_specs=[SMEM] * first + [...  25.5 us
    all_gather x1, waiting for transfers between devices, local(): lax.all_gather(gathered, 'z', axis=0, tiled=True)  25.1 us
    all_gather x1, blocking collectives, local(): grads = lax.all_gather(part[:share], 'z', axis=0, tiled=True)  24.8 us
    all_to_all x2, waiting for transfers between devices, a2a(): return lax.all_to_all(x, axis, 0, 0, tiled=True)  23.8 us
    all_gather x1, blocking collectives, local(): gathered = lax.all_gather(features, 'x', axis=0, tiled=True)  13.9 us
    all_to_all x2, starting transfers between devices, a2a(): return lax.all_to_all(x, axis, 0, 0, tiled=True)  13.8 us
    ppermute x3, starting transfers between devices, shift(): return lax.ppermute(x, axis, [(i, (i + by) % n) for i in range(n)])  10.4 us
  transfers between devices with their start and end apart: 7, of which 2 were waited for; matrix products, arithmetic and copies ran while one was open for 3% of the time, Pallas kernels for 6%

profile of v7, /device:TPU:10, one launch (start us, length us, event | category | flops | bytes accessed | tf_op | source)
XLA Modules:
  0.0 201.2 jit_solution(4017418515455897431)
XLA Ops:
  7.3 13.9 %all_gather.9 = bf16[1024,256]{1,0:T(8,128)(2,1)} all-gather(bf16[256,256]{1,0:T(8,128)(2,1)} %refs_7_.1), channel_id=1, replica_groups=mesh['y'=8,'c'=2,'x'=4,'z'=8] {'x'}, dimensions={0}, use_global_device_ids=true | all-gather | bytes 655360 | tf_op jit(solution)/shard_map/all_gather | solution.py:262
  21.2 3.1 %shard_map.154 = bf16[16,128,256]{2,1,0:T(8,128)(2,1)} custom-call(s32[1,16]{1,0:T(1,128)} %refs_0_.6, s32[16,128]{1,0:T(8,128)} %bitcast.26, bf16[256,256]{1,0:T(8,128)(2,1)} %refs_7_.1), custom_call_target="tpu_custom_call" | custom-call | flops 268435456 | bytes 1187840 | tf_op jit(solution)/shard_map/pallas_call | solution.py:49
  24.3 8.6 %all-to-all-start = ((bf16[16,128,256]{2,1,0:T(8,128)(2,1)}), bf16[16,128,256]{2,1,0:T(8,128)(2,1)S(1)}, u32[]{:S(2)}, u32[]{:S(2)}) async-start(bf16[16,128,256]{2,1,0:T(8,128)(2,1)} %shard_map.154), calls=%async_computation | async-start | bytes 2097152 | tf_op jit(solution)/shard_map/all_to_all | solution.py:243
  32.9 0.9 convolution_add_fusion.refs_4_
  33.8 23.8 %all-to-all-done = bf16[16,128,256]{2,1,0:T(8,128)(2,1)S(1)} async-done(((bf16[16,128,256]{2,1,0:T(8,128)(2,1)}), bf16[16,128,256]{2,1,0:T(8,128)(2,1)S(1)}, u32[]{:S(2)}, u32[]{:S(2)}) %all-to-all-start) | async-done | bytes 1048608 | tf_op jit(solution)/shard_map/all_to_all | solution.py:243
  57.6 1.1 convolution_bitcast_fusion.refs_3_
  58.8 25.1 %all-gather.2.cloned.1.call-done = bf16[8192,256]{1,0:T(8,128)(2,1)} async-done(((bf16[1024,256]{1,0:T(8,128)(2,1)}), bf16[8192,256]{1,0:T(8,128)(2,1)}) %all-gather.2.cloned.1.call-update) | async-done | bytes 4194320 | tf_op jit(solution)/shard_map/all_gather | solution.py:263
  83.8 10.2 %shard_map.155 = (bf16[256,256]{1,0:T(8,128)(2,1)}, bf16[256,256]{1,0:T(8,128)(2,1)}, bf16[16,128,256]{2,1,0:T(8,128)(2,1)}, bf16[4,144,256]{2,1,0:T(8,128)(2,1)...) custom-call(s32[2,24]{1,0:T(2,128)} %refs_0_.7, s32[2]{0:T(128)} %refs_1_.3, bf16[2,24,128,128]{3,2,1,0:T(8,128)(2,1)} %refs_2_.3, ...), custom_call_target="tpu_custom_call" | custom-call | flops 1073741824 | bytes 13926400 | tf_op jit(solution)/shard_map/pallas_call | solution.py:49
  94.1 0.9 copy-done.7
  95.0 10.3 %all_to_all.25.refs_0_ = bf16[4,144,256]{2,1,0:T(8,128)(2,1)} all-to-all(bf16[4,144,256]{2,1,0:T(8,128)(2,1)S(1)} %copy-done.7), channel_id=1, replica_groups=mesh['y'=8,'c'=2,'x'=4,'z'=8] {'x'}, dimensions={0} | all-to-all | bytes 589824 | tf_op jit(solution)/shard_map/all_to_all | solution.py:243
  105.3 1.7 shard_map.156
  107.0 14.6 %all_to_all.26 = bf16[8,32,256]{2,1,0:T(8,128)(2,1)S(1)} all-to-all(bf16[8,32,256]{2,1,0:T(8,128)(2,1)} %shard_map.156), channel_id=1, replica_groups=mesh['y'=8,'c'=2,'x'=4,'z'=8] {'z'}, dimensions={0} | all-to-all | bytes 262144 | tf_op jit(solution)/shard_map/all_to_all | solution.py:243
  121.6 16.7 %all_to_all.27 = bf16[16,32,256]{2,1,0:T(8,128)(2,1)S(1)} all-to-all(bf16[16,32,256]{2,1,0:T(8,128)(2,1)S(1)} %broadcast_in_dim.2), channel_id=1, replica_groups=mesh['y'=8,'c'=2,'x'=4,'z'=8] {'y','c'}, dimensions={0} | all-to-all | bytes 524288 | tf_op jit(solution)/shard_map/all_to_all | solution.py:243
  139.0 5.2 %all-to-all-start.4 = ((bf16[16,128,256]{2,1,0:T(8,128)(2,1)}), bf16[16,128,256]{2,1,0:T(8,128)(2,1)S(1)}, u32[]{:S(2)}, u32[]{:S(2)}) async-start(bf16[16,128,256]{2,1,0:T(8,128)(2,1)} %shard_map.157), calls=%async_computation.4 | async-start | bytes 2097152 | tf_op jit(solution)/shard_map/all_to_all | solution.py:243
  144.2 24.8 %all_gather.11 = bf16[128,256]{1,0:T(8,128)(2,1)S(1)} all-gather(bf16[16,256]{1,0:T(8,128)(2,1)S(1)} %slice-done), channel_id=1, replica_groups=mesh['y'=8,'c'=2,'x'=4,'z'=8] {'z'}, dimensions={0}, use_global_device_ids=true | all-gather | bytes 73728 | tf_op jit(solution)/shard_map/all_gather | solution.py:305
  169.0 1.1 dynamic-slice_bitcast_fusion
  170.2 0.7 pad_maximum_fusion
  170.9 3.4 %collective-permute-start.2 = (bf16[384,256]{1,0:T(8,128)(2,1)S(1)}, bf16[384,256]{1,0:T(8,128)(2,1)S(1)}, u32[]{:S(2)}, u32[]{:S(2)}) collective-permute-start(bf16[384,256]{1,0:T(8,128)(2,1)S(1)} %get-tuple-element.26), channel_id=1, source_target_pairs={{0,24},{8,0},{16,8},{24,16},{1,25},{9,1},{17,9},{25,17},{2,26},{10... | collective-permute-start | bytes 589832 | tf_op jit(solution)/shard_map/ppermute | solution.py:247
  174.3 2.5 %collective-permute-start = (bf16[384,256]{1,0:T(8,128)(2,1)S(1)}, bf16[384,256]{1,0:T(8,128)(2,1)S(1)}, u32[]{:S(2)}, u32[]{:S(2)}) collective-permute-start(bf16[384,256]{1,0:T(8,128)(2,1)S(1)} %get-tuple-element.27), channel_id=1, source_target_pairs={{0,8},{8,16},{16,24},{24,0},{1,9},{9,17},{17,25},{25,1},{2,10},{10... | collective-permute-start | bytes 589832 | tf_op jit(solution)/shard_map/ppermute | solution.py:247
  176.8 4.6 %collective-permute-start.1 = (bf16[384,256]{1,0:T(8,128)(2,1)S(1)}, bf16[384,256]{1,0:T(8,128)(2,1)S(1)}, u32[]{:S(2)}, u32[]{:S(2)}) collective-permute-start(bf16[384,256]{1,0:T(8,128)(2,1)S(1)} %get-tuple-element.28), channel_id=1, source_target_pairs={{0,16},{8,24},{16,0},{24,8},{1,17},{9,25},{17,1},{25,9},{2,18},{10... | collective-permute-start | bytes 589832 | tf_op jit(solution)/shard_map/ppermute | solution.py:247
  181.9 5.1 %shard_map.159 = bf16[2,24,128,128]{3,2,1,0:T(8,128)(2,1)} custom-call(s32[2,24]{1,0:T(2,128)} %refs_0_.7, s32[2]{0:T(128)} %refs_1_.3, bf16[256,256]{1,0:T(8,128)(2,1)} %get-tuple-element.19.refs_2_, bf16[64,128,256]{2,1,0:T(8,128)(2,1)} %bitcast.22, bf16[384,256]{1,0:T(8,128)(2,1)} %get-tuple-element.29.refs_4_.refs_1_), custom_call_target="tpu_custom_call" | custom-call | flops 402653184 | bytes 5898240 | tf_op jit(solution)/shard_map/pallas_call | solution.py:49
  187.9 2.1 %shard_map.160 = (f32[256,256]{1,0:T(8,128)}, f32[256,256]{1,0:T(8,128)}) custom-call(s32[1]{0:T(128)} %bitcast.10.refs_0_, bf16[384,256]{1,0:T(8,128)(2,1)} %get-tuple-element.29.refs_4_.refs_1_, bf16[384,256]{1,0:T(8,128)(2,1)} %copy-done.4, bf16[384,256]{1,0:T(8,128)(2,1)} %copy-done.5, bf16[384,256]{1,0:T(8,128)(2,1)} %copy-done.3), custom_call_target="tpu_custom_call" | custom-call | bytes 1310720 | tf_op jit(solution)/shard_map/pallas_call | solution.py:49
  190.0 1.0 copy-done.1
  191.0 3.3 %shard_map.158 = bf16[256,256]{1,0:T(8,128)(2,1)} custom-call(s32[1,16]{1,0:T(1,128)} %refs_0_.6, s32[16,128]{1,0:T(8,128)} %bitcast.27, bf16[16,128,256]{2,1,0:T(8,128)(2,1)} %copy-done.1, f32[256,256]{1,0:T(8,128)} %get-tuple-element.17.refs_3_, bf16[384,256]{1,0:T(8,128)(2,1)} %get-tuple-element.29.refs_4_.refs_1_, bf16[384,256]{1,0:T(8,128)(2,1)} %copy-done.4, ...), custom_call_target="tpu_custom_call" | custom-call | flops 268435456 | bytes 2236416 | tf_op jit(solution)/shard_map/pallas_call | solution.py:49
  (34 shorter events, 2.2 us)
Async XLA Ops:
  7.2 25.7 %copy-start.2 = (bf16[256,256]{1,0:T(8,128)(2,1)S(1)}, bf16[256,256]{1,0:T(8,128)(2,1)}, u32[]{:S(2)}) copy-start(bf16[256,256]{1,0:T(8,128)(2,1)} %refs_7_.1) | copy-start | bytes 393220
  7.2 25.7 %copy-start.6 = (bf16[256,256]{1,0:T(8,128)(2,1)S(1)}, bf16[256,256]{1,0:T(8,128)(2,1)}, u32[]{:S(2)}) copy-start(bf16[256,256]{1,0:T(8,128)(2,1)} %refs_8_.1) | copy-start | bytes 393220
  7.2 25.7 %copy-start.9 = (f32[256]{0:T(256)S(1)}, f32[256]{0:T(256)}, u32[]{:S(2)}) copy-start(f32[256]{0:T(256)} %param.20) | copy-start | bytes 3076
  7.2 50.4 %copy-start = (bf16[256,2048]{1,0:T(8,128)(2,1)S(1)}, bf16[256,2048]{1,0:T(8,128)(2,1)}, u32[]{:S(2)}) copy-start(bf16[256,2048]{1,0:T(8,128)(2,1)} %refs_9_.1) | copy-start | bytes 3145732
  7.2 76.6 %all-gather.2.cloned.1.call-start = ((), (), s32[]{:S(2)}) async-start(), calls=%async_computation.6 | async-start | bytes 4718592 | tf_op jit(solution)/shard_map/all_gather | solution.py:263
  24.3 33.3 %all-to-all-start = ((bf16[16,128,256]{2,1,0:T(8,128)(2,1)}), bf16[16,128,256]{2,1,0:T(8,128)(2,1)S(1)}, u32[]{:S(2)}, u32[]{:S(2)}) async-start(bf16[16,128,256]{2,1,0:T(8,128)(2,1)} %shard_map.154), calls=%async_computation | async-start | bytes 2097152 | tf_op jit(solution)/shard_map/all_to_all | solution.py:243
  32.9 136.2 %reduce-scatter.2.cloned.1.call-start = ((), (), s32[]{:S(2)}) async-start(), calls=%async_computation.7 | async-start | bytes 4718592 | tf_op jit(solution)/shard_map/reduce_scatter | solution.py:294
  94.1 1.0 copy-start.7
  139.0 5.2 %slice-start = ((bf16[32,256]{1,0:T(8,128)(2,1)}), bf16[16,256]{1,0:T(8,128)(2,1)S(1)}, s32[]{:S(2)}) async-start(bf16[32,256]{1,0:T(8,128)(2,1)} %reduce_sum.25.after_ref), calls=%async_computation.8 | async-start | bytes 16384 | tf_op jit(solution)/shard_map/slice | solution.py:305
  139.0 42.3 %copy-start.8 = (bf16[32,256]{1,0:T(8,128)(2,1)S(1)}, bf16[32,256]{1,0:T(8,128)(2,1)}, u32[]{:S(2)}) copy-start(bf16[32,256]{1,0:T(8,128)(2,1)} %reduce_sum.25.after_ref) | copy-start | bytes 49156
  139.0 51.0 %all-to-all-start.4 = ((bf16[16,128,256]{2,1,0:T(8,128)(2,1)}), bf16[16,128,256]{2,1,0:T(8,128)(2,1)S(1)}, u32[]{:S(2)}, u32[]{:S(2)}) async-start(bf16[16,128,256]{2,1,0:T(8,128)(2,1)} %shard_map.157), calls=%async_computation.4 | async-start | bytes 2097152 | tf_op jit(solution)/shard_map/all_to_all | solution.py:243
  170.9 16.1 %collective-permute-start.2 = (bf16[384,256]{1,0:T(8,128)(2,1)S(1)}, bf16[384,256]{1,0:T(8,128)(2,1)S(1)}, u32[]{:S(2)}, u32[]{:S(2)}) collective-permute-start(bf16[384,256]{1,0:T(8,128)(2,1)S(1)} %get-tuple-element.26), channel_id=1, source_target_pairs={{0,24},{8,0},{16,8},{24,16},{1,25},{9,1},{17,9},{25,17},{2,26},{10... | collective-permute-start | bytes 589832 | tf_op jit(solution)/shard_map/ppermute | solution.py:247
  174.3 12.8 %collective-permute-start = (bf16[384,256]{1,0:T(8,128)(2,1)S(1)}, bf16[384,256]{1,0:T(8,128)(2,1)S(1)}, u32[]{:S(2)}, u32[]{:S(2)}) collective-permute-start(bf16[384,256]{1,0:T(8,128)(2,1)S(1)} %get-tuple-element.27), channel_id=1, source_target_pairs={{0,8},{8,16},{16,24},{24,0},{1,9},{9,17},{17,25},{25,1},{2,10},{10... | collective-permute-start | bytes 589832 | tf_op jit(solution)/shard_map/ppermute | solution.py:247
  176.8 10.3 %collective-permute-start.1 = (bf16[384,256]{1,0:T(8,128)(2,1)S(1)}, bf16[384,256]{1,0:T(8,128)(2,1)S(1)}, u32[]{:S(2)}, u32[]{:S(2)}) collective-permute-start(bf16[384,256]{1,0:T(8,128)(2,1)S(1)} %get-tuple-element.28), channel_id=1, source_target_pairs={{0,16},{8,24},{16,0},{24,8},{1,17},{9,25},{17,1},{25,9},{2,18},{10... | collective-permute-start | bytes 589832 | tf_op jit(solution)/shard_map/ppermute | solution.py:247
  187.1 0.7 copy-start.3
  187.1 0.7 copy-start.4
  187.1 0.8 copy-start.5
  190.0 1.0 copy-start.1
Sparse Core Ops, SparseCore 0:
  21.3 62.4 all-gather.1
  94.2 59.7 reduce-scatter.1

commit v8 on v7

--- a/solution.py
+++ b/solution.py
@@ -1,4 +1,3 @@
-import functools
 import math
 
 import jax
@@ -53,7 +52,7 @@
         out_specs=tuple(out_specs or [VMEM] * len(outs)),
         scratch_shapes=[
             *(pltpu.VMEM(a.shape, a.dtype) for a in arrays),
-            pltpu.SemaphoreType.DMA((count,)),
+            pltpu.SemaphoreType.DMA((max(count, 1),)),
             *scratch,
         ],
         compiler_params=pltpu.CompilerParams(vmem_limit_bytes=vmem << 20),
@@ -94,7 +93,7 @@
 ):
     index_ref, count_ref = scalars
     blocks_ref, outer_ref, pre_ref, w_ref, dout_ref, feat_ref, wself_ref, cut_ref = arrays
-    out_ref, dagg_ref, back_ref, part_ref, self_ref, term_ref = outs
+    out_ref, dagg_ref, back_ref, self_ref, term_ref = outs
     tile_copy = pltpu.make_async_copy(gathered[0], tiles.at[pl.ds(0, 2 * BANDS)], tile_sem)
     tile_copy.start()
     slots = blocks_ref.shape[1]
@@ -149,18 +148,17 @@
     width = d_pre.shape[1]
     groups = back_ref.shape[0]
     cut = cut_ref.shape[1] // groups
-    share = part_ref.shape[1] - SPARE_ROWS
-    grads = [
-        lax.dot_general(left, d_pre, TN, preferred_element_type=F32).astype(BF)
-        for left in (feat_ref[...], agg)
-    ]
+    share = 2 * width // groups
+    for i, left in enumerate((feat_ref[...], agg)):
+        grad = lax.dot_general(left, d_pre, TN, preferred_element_type=F32).astype(BF)
+        for g in range(groups // 2):
+            spot = i * groups // 2 + g
+            back_ref[spot, pl.ds(cut, share), :] = grad[g * share : (g + 1) * share]
     bias = jnp.sum(d_pre.astype(F32), axis=0, keepdims=True)
     row = lax.broadcasted_iota(jnp.int32, (SPARE_ROWS, width), 0)
     bias = jnp.where(row == 0, bias, 0.0).astype(BF)
-    for x in range(NX):
-        grad, at = grads[2 * x // NX], x % 2 * share
-        part_ref[x, pl.ds(0, share), :] = grad[at : at + share]
-        part_ref[x, pl.ds(share, SPARE_ROWS), :] = bias
+    for g in range(groups):
+        back_ref[g, pl.ds(cut + share, SPARE_ROWS), :] = bias
     d_agg = jnp.concatenate(d_aggs, axis=0)
     for g in range(0, groups, 2):
         rows = lax.dot_general(
@@ -185,58 +183,35 @@
 
 
 def base_body(scalars, arrays, copies, outs):
-    (count_ref,), (rows_ref, back_ref, self_ref, *term_refs), (out_ref,) = scalars, arrays, outs
+    (count_ref,), (rows_ref, back_ref, self_ref), (out_ref,) = scalars, arrays, outs
+    cut = rows_ref.shape[1]
     wait(copies)
     total = self_ref[...]
-    for term_ref in term_refs:
-        total = total + term_ref[pl.ds(0, total.shape[0]), :].astype(F32)
     for g in range(0, back_ref.shape[0], 2):
         hot = jnp.concatenate(
             [hot_columns(rows_ref, count_ref, g + i, total.shape[0]) for i in range(2)], axis=1
         )
-        rows = jnp.concatenate([back_ref[g], back_ref[g + 1]], axis=0)
+        rows = jnp.concatenate([back_ref[g + i, pl.ds(0, cut), :] for i in range(2)], axis=0)
         total = total + jnp.dot(hot, rows, preferred_element_type=F32)
-    out_ref[...] = total.astype(BF)
-
-
-def grads_body(scale, scalars, arrays, copies, outs):
-    (x_ref,) = scalars
-    wait(copies)
-    share = sum(out_ref.shape[0] for out_ref in outs) // len(arrays)
-    for by, rows_ref in enumerate(arrays):
-        x = (x_ref[0] - by) & (NX - 1)
-        grads = rows_ref[pl.ds(rows_ref.shape[0] - share, share), :].astype(F32) * scale
-        for i, out_ref in enumerate(outs):
-            held = out_ref.shape[0] // share
-
-            @pl.when(lax.div(x, held) == i)
-            def _(out_ref=out_ref, grads=grads, spot=(x & (held - 1)) * share):
-                out_ref[pl.ds(pl.multiple_of(spot, share), share), :] = grads
-
-
-def share_body(scalars, arrays, copies, outs):
+    out_ref[...] = total
+
+
+def behind_body(scalars, arrays, copies, outs, returned, parts_ref, sem):
+    rows = parts_ref.shape[1]
+    first = returned[0].shape[1] - rows
+    copy = pltpu.make_async_copy(returned[0].at[:, pl.ds(first, rows)], parts_ref, sem)
+    copy.start()
+    sum_body(scalars, (parts_ref,), [copy], outs)
+
+
+def sum_body(scalars, arrays, copies, outs):
     (parts_ref,), (out_ref,) = arrays, outs
     wait(copies)
     total = parts_ref[0].astype(F32)
     for i in range(1, parts_ref.shape[0]):
         total = total + parts_ref[i].astype(F32)
-    total = total.astype(BF)
-    share = out_ref.shape[1] - SPARE_ROWS
-    last = total.shape[0] - SPARE_ROWS
     for i in range(out_ref.shape[0]):
-        out_ref[i, pl.ds(0, share), :] = total[i * share : (i + 1) * share]
-        out_ref[i, pl.ds(share, SPARE_ROWS), :] = total[last:]
-
-
-def gate(x, after):
-    return pl.pallas_call(
-        lambda x_ref, after_ref, out_ref: None,
-        out_shape=sds(x.shape, x.dtype),
-        in_specs=[HBM, HBM],
-        out_specs=HBM,
-        input_output_aliases={0: 0},
-        compiler_params=pltpu.CompilerParams(vmem_limit_bytes=60 << 20),
-    )(x, after)
+        out_ref[i] = total.astype(BF)
 
 
 def a2a(x, axis):
@@ -269,12 +244,13 @@
     outer = jnp.dot(cut_weight, arrived, preferred_element_type=F32)
     own_pre = jnp.dot(features, w_self, preferred_element_type=F32) + bias
 
+    share = 2 * width // NG
     outs = [
-        node_bf, node_bf, cut_bf, sds((NX, 2 * width // NX + SPARE_ROWS, width), BF), node_f32,
+        node_bf, node_bf, sds((NG, cut + share + SPARE_ROWS, width), BF), node_f32,
         sds(gathered.shape, BF),
     ]
     spared = (2 * BANDS + 1, 128, width)
-    output, d_agg, back, part, self_back, terms = call(
+    output, d_agg, back, self_back, terms = call(
         main_body,
         [block_index, block_count],
         [block_values, outer, own_pre, w_neigh, d_out, features, w_self, cut_weight],
@@ -295,40 +271,44 @@
     terms = terms.reshape(NX, nodes, width)
     me = lax.axis_index("x")
 
-    share = 2 * width // BANDS
+    returned = a2a(back, ("y", "c"))
+    (grad_blocks,) = call(
+        blocks_body, [block_index, block_count], [d_agg, gathered], [sds(block_values.shape, BF)],
+        flops=2 * tiles_here * slots * 128 * 128 * width,
+    )
+    (part,) = call(
+        behind_body, [], [], [sds((NX, share + SPARE_ROWS, width), BF)],
+        scratch=[pltpu.VMEM((NG, share + SPARE_ROWS, width), BF), pltpu.SemaphoreType.DMA],
+        direct=[returned], extra=[grad_blocks],
+    )
     part = a2a(part, "x")
-    (part,) = call(share_body, [], [part], [sds((NZ, share + SPARE_ROWS, width), BF)])
-    part = jnp.sum(a2a(part, "z").astype(F32), axis=0).astype(BF)
-    part = a2a(jnp.broadcast_to(part[None], (NG, *part.shape)), ("y", "c"))
     part = jnp.sum(part.astype(F32), axis=0).astype(BF)
-    returned = a2a(gate(back, part), ("y", "c"))
-    grads = lax.all_gather(part[:share], "z", axis=0, tiled=True)
+    part = a2a(jnp.broadcast_to(part[None], (NZ, *part.shape)), "z")
     moved = []
     for by in range(NX):
         rows = lax.dynamic_index_in_dim(terms, (me + by) & (NX - 1), 0, keepdims=False)
-        rows = jnp.concatenate([rows, grads], axis=0)
         moved.append(shift(rows, "x", NX, by) if by else rows)
-    grad_self, grad_neigh = call(
-        functools.partial(grads_body, scale), [me.astype(jnp.int32).reshape(1)], moved,
-        [sds((width, width), F32)] * 2,
-    )
-
-    (grad_blocks,) = call(
-        blocks_body, [block_index, block_count], [d_agg, gathered], [sds(block_values.shape, BF)],
-        extra=[moved[0]], flops=2 * tiles_here * slots * 128 * 128 * width,
-    )
-    (d_features,) = call(
-        base_body, [send_count], [rows2, returned, self_back, *moved], [node_bf],
+    (base,) = call(
+        base_body, [send_count], [rows2, returned, self_back], [node_f32],
         flops=2 * NG * cut * width * nodes,
     )
+    (part,) = call(
+        sum_body, [], [part], [sds((NY, share + SPARE_ROWS, width), BF)], extra=[base, terms]
+    )
+    part = a2a(part, "y")
+    grads = lax.all_gather(part, "c", axis=1).reshape(NG, share + SPARE_ROWS, width)
+    grads = grads.astype(F32) * scale
+    weight_grads = grads[:, :share].reshape(2, width, width)
+
+    d_features = (base + sum(rows.astype(F32) for rows in moved)).astype(BF)
 
     return (
         output,
         d_features,
         grad_blocks,
-        grad_self,
-        grad_neigh,
-        part[share].astype(F32) * scale,
+        weight_grads[0],
+        weight_grads[1],
+        grads[0, share],
     )
 
 

time: 202 us -> 198 us (0.980)
  the two profiles are of different devices: /device:TPU:10 before, /device:TPU:1 now
where the time goes in v8:
time: 198 us; the launch traced here: 197 us
  waiting for transfers between devices  85.1 us (43%)
  starting transfers between devices  36.6 us (18%)
  blocking collectives  27.2 us (14%)
  Pallas kernels  25.1 us (13%)
  between operations  14.2 us (7%)
  local copies, waits for them, and re-layouts  4.96 us (3%)
  matrix products  2.03 us (1%)
    all_to_all x4, waiting for transfers between devices, a2a(): return lax.all_to_all(x, axis, 0, 0, tiled=True)  64.7 us
    all_to_all x4, starting transfers between devices, a2a(): return lax.all_to_all(x, axis, 0, 0, tiled=True)  28 us
    pallas_call x6, Pallas kernels, call(): pl.pallas_call(kernel, out_shape=tuple(outs), in_specs=[SMEM] * first + [...  25.1 us
    all_gather x1, waiting for transfers between devices, local(): lax.all_gather(gathered, 'z', axis=0, tiled=True)  20.4 us
    all_gather x1, blocking collectives, local(): gathered = lax.all_gather(features, 'x', axis=0, tiled=True)  13.3 us
    all_to_all x1, blocking collectives, a2a(): return lax.all_to_all(x, axis, 0, 0, tiled=True)  9.32 us
    ppermute x3, starting transfers between devices, shift(): return lax.ppermute(x, axis, [(i, (i + by) % n) for i in range(n)])  8.52 us
    all_gather x1, blocking collectives, local(): lax.all_gather(part, 'c', axis=1).reshape(NG, share + SPARE_ROWS, width)  4.59 us
  transfers between devices with their start and end apart: 9, of which 4 were waited for; matrix products, arithmetic and copies ran while one was open for 3% of the time, Pallas kernels for 8%

profile of v8, /device:TPU:1, one launch (start us, length us, event | category | flops | bytes accessed | tf_op | source)
XLA Modules:
  0.0 197.1 jit_solution(15417035149119150460)
XLA Ops:
  7.2 13.3 %all_gather.12 = bf16[1024,256]{1,0:T(8,128)(2,1)} all-gather(bf16[256,256]{1,0:T(8,128)(2,1)} %refs_7_.1), channel_id=1, replica_groups=mesh['y'=8,'c'=2,'x'=4,'z'=8] {'x'}, dimensions={0}, use_global_device_ids=true | all-gather | bytes 655360 | tf_op jit(solution)/shard_map/all_gather | solution.py:237
  20.6 3.2 %shard_map.154 = bf16[16,128,256]{2,1,0:T(8,128)(2,1)} custom-call(s32[1,16]{1,0:T(1,128)} %refs_0_.6, s32[16,128]{1,0:T(8,128)} %bitcast.35, bf16[256,256]{1,0:T(8,128)(2,1)} %refs_7_.1), custom_call_target="tpu_custom_call" | custom-call | flops 268435456 | bytes 1187840 | tf_op jit(solution)/shard_map/pallas_call | solution.py:48
  23.8 11.2 %all-to-all-start = ((bf16[16,128,256]{2,1,0:T(8,128)(2,1)}), bf16[16,128,256]{2,1,0:T(8,128)(2,1)S(1)}, u32[]{:S(2)}, u32[]{:S(2)}) async-start(bf16[16,128,256]{2,1,0:T(8,128)(2,1)} %shard_map.154), calls=%async_computation | async-start | bytes 2097152 | tf_op jit(solution)/shard_map/all_to_all | solution.py:218
  36.0 27.0 %all-to-all-done = bf16[16,128,256]{2,1,0:T(8,128)(2,1)S(1)} async-done(((bf16[16,128,256]{2,1,0:T(8,128)(2,1)}), bf16[16,128,256]{2,1,0:T(8,128)(2,1)S(1)}, u32[]{:S(2)}, u32[]{:S(2)}) %all-to-all-start) | async-done | bytes 1048608 | tf_op jit(solution)/shard_map/all_to_all | solution.py:218
  63.0 1.1 convolution_bitcast_fusion.refs_3_
  64.2 20.4 %all-gather.3.cloned.1.call-done = bf16[8192,256]{1,0:T(8,128)(2,1)} async-done(((bf16[1024,256]{1,0:T(8,128)(2,1)}), bf16[8192,256]{1,0:T(8,128)(2,1)}) %all-gather.3.cloned.1.call-update) | async-done | bytes 4194320 | tf_op jit(solution)/shard_map/all_gather | solution.py:238
  84.6 10.2 %shard_map.155 = (bf16[256,256]{1,0:T(8,128)(2,1)}, bf16[256,256]{1,0:T(8,128)(2,1)}, bf16[16,176,256]{2,1,0:T(8,128)(2,1)}, f32[256,256]{1,0:T(8,128)}, bf16[64,128,256]{2,1,0:T(8,128)(2,1)}) custom-call(s32[2,24]{1,0:T(2,128)} %refs_0_.7, s32[2]{0:T(128)} %refs_1_.3, bf16[2,24,128,128]{3,2,1,0:T(8,128)(2,1)} %refs_2_.3, ...), custom_call_target="tpu_custom_call" | custom-call | flops 1073741824 | bytes 14024704 | tf_op jit(solution)/shard_map/pallas_call | solution.py:48
  94.9 7.4 %all-to-all-start.1 = ((bf16[16,176,256]{2,1,0:T(8,128)(2,1)}), bf16[16,176,256]{2,1,0:T(8,128)(2,1)S(1)}, u32[]{:S(2)}, u32[]{:S(2)}) async-start(bf16[16,176,256]{2,1,0:T(8,128)(2,1)} %get-tuple-element.12), calls=%async_computation.1 | async-start | bytes 2883584 | tf_op jit(solution)/shard_map/all_to_all | solution.py:218
  102.3 5.1 %shard_map.157.refs_1_ = bf16[2,24,128,128]{3,2,1,0:T(8,128)(2,1)} custom-call(s32[2,24]{1,0:T(2,128)} %refs_0_.7, s32[2]{0:T(128)} %refs_1_.3, bf16[256,256]{1,0:T(8,128)(2,1)} %get-tuple-element.15.refs_2_, bf16[64,128,256]{2,1,0:T(8,128)(2,1)} %bitcast.25), custom_call_target="tpu_custom_call" | custom-call | flops 402653184 | bytes 5898240 | tf_op jit(solution)/shard_map/pallas_call | solution.py:48
  107.4 30.7 %all-to-all-done.1.refs_2_.refs_0_ = bf16[16,176,256]{2,1,0:T(8,128)(2,1)S(1)} async-done(((bf16[16,176,256]{2,1,0:T(8,128)(2,1)}), bf16[16,176,256]{2,1,0:T(8,128)(2,1)S(1)}, u32[]{:S(2)}, u32[]{:S(2)}) %all-to-all-start.1) | async-done | bytes 1441824 | tf_op jit(solution)/shard_map/all_to_all | solution.py:218
  138.1 1.1 copy-done
  139.2 1.7 shard_map.158
  141.0 9.3 %all_to_all.25 = bf16[4,48,256]{2,1,0:T(8,128)(2,1)S(1)} all-to-all(bf16[4,48,256]{2,1,0:T(8,128)(2,1)} %shard_map.158), channel_id=1, replica_groups=mesh['y'=8,'c'=2,'x'=4,'z'=8] {'x'}, dimensions={0} | all-to-all | bytes 196608 | tf_op jit(solution)/shard_map/all_to_all | solution.py:218
  151.0 3.9 %all-to-all-start.3 = ((bf16[8,48,256]{2,1,0:T(8,128)(2,1)}), bf16[8,48,256]{2,1,0:T(8,128)(2,1)S(1)}, u32[]{:S(2)}, u32[]{:S(2)}) async-start(bf16[8,48,256]{2,1,0:T(8,128)(2,1)} %broadcast_in_dim.2), calls=%async_computation.4 | async-start | bytes 393216 | tf_op jit(solution)/shard_map/all_to_all | solution.py:218
  154.9 1.1 dynamic-slice_bitcast_fusion.2
  155.9 2.3 %collective-permute-start = (bf16[256,256]{1,0:T(8,128)(2,1)S(1)}, bf16[256,256]{1,0:T(8,128)(2,1)S(1)}, u32[]{:S(2)}, u32[]{:S(2)}) collective-permute-start(bf16[256,256]{1,0:T(8,128)(2,1)S(1)} %get-tuple-element.18), channel_id=1, source_target_pairs={{0,8},{8,16},{16,24},{24,0},{1,9},{9,17},{17,25},{25,1},{2,10},{10... | collective-permute-start | bytes 393224 | tf_op jit(solution)/shard_map/ppermute | solution.py:222
  158.2 3.6 %collective-permute-start.1 = (bf16[256,256]{1,0:T(8,128)(2,1)S(1)}, bf16[256,256]{1,0:T(8,128)(2,1)S(1)}, u32[]{:S(2)}, u32[]{:S(2)}) collective-permute-start(bf16[256,256]{1,0:T(8,128)(2,1)S(1)} %get-tuple-element.20), channel_id=1, source_target_pairs={{0,16},{8,24},{16,0},{24,8},{1,17},{9,25},{17,1},{25,9},{2,18},{10... | collective-permute-start | bytes 393224 | tf_op jit(solution)/shard_map/ppermute | solution.py:222
  161.8 2.6 %collective-permute-start.2 = (bf16[256,256]{1,0:T(8,128)(2,1)S(1)}, bf16[256,256]{1,0:T(8,128)(2,1)S(1)}, u32[]{:S(2)}, u32[]{:S(2)}) collective-permute-start(bf16[256,256]{1,0:T(8,128)(2,1)S(1)} %get-tuple-element.19), channel_id=1, source_target_pairs={{0,24},{8,0},{16,8},{24,16},{1,25},{9,1},{17,9},{25,17},{2,26},{10... | collective-permute-start | bytes 393224 | tf_op jit(solution)/shard_map/ppermute | solution.py:222
  164.5 3.2 %shard_map.156.refs_1_ = f32[256,256]{1,0:T(8,128)} custom-call(s32[1,16]{1,0:T(1,128)} %refs_0_.6, s32[16,128]{1,0:T(8,128)} %bitcast.36, bf16[16,176,256]{2,1,0:T(8,128)(2,1)} %copy-done, f32[256,256]{1,0:T(8,128)} %get-tuple-element.13.refs_3_), custom_call_target="tpu_custom_call" | custom-call | flops 268435456 | bytes 1974272 | tf_op jit(solution)/shard_map/pallas_call | solution.py:48
  168.4 1.6 shard_map.159
  170.1 5.5 %all-to-all-start.4 = ((bf16[8,48,256]{2,1,0:T(8,128)(2,1)}), bf16[8,48,256]{2,1,0:T(8,128)(2,1)S(1)}, u32[]{:S(2)}, u32[]{:S(2)}) async-start(bf16[8,48,256]{2,1,0:T(8,128)(2,1)} %shard_map.159), calls=%async_computation.5 | async-start | bytes 393216 | tf_op jit(solution)/shard_map/all_to_all | solution.py:218
  175.6 1.6 fusion.3
  177.2 7.0 %all-to-all-done.4 = bf16[8,48,256]{2,1,0:T(8,128)(2,1)S(1)} async-done(((bf16[8,48,256]{2,1,0:T(8,128)(2,1)}), bf16[8,48,256]{2,1,0:T(8,128)(2,1)S(1)}, u32[]{:S(2)}, u32[]{:S(2)}) %all-to-all-start.4) | async-done | bytes 196640 | tf_op jit(solution)/shard_map/all_to_all | solution.py:218
  184.2 4.6 %all-gather = bf16[8,96,256]{2,1,0:T(8,128)(2,1)S(1)} all-gather(bf16[8,48,256]{2,1,0:T(8,128)(2,1)S(1)} %all-to-all-done.4), channel_id=2, replica_groups=mesh['y'=8,'c'=2,'x'=4,'z'=8] {'c'}, dimensions={1}, use_global_device_ids=true | all-gather | bytes 589824 | tf_op jit(solution)/shard_map/all_gather | solution.py:299
  (28 shorter events, 3.9 us)
Async XLA Ops:
  7.2 77.4 %all-gather.3.cloned.1.call-start = ((), (), s32[]{:S(2)}) async-start(), calls=%async_computation.6 | async-start | bytes 4718592 | tf_op jit(solution)/shard_map/all_gather | solution.py:238
  20.6 14.5 %copy-start.3 = (bf16[256,256]{1,0:T(8,128)(2,1)S(1)}, bf16[256,256]{1,0:T(8,128)(2,1)}, u32[]{:S(2)}) copy-start(bf16[256,256]{1,0:T(8,128)(2,1)} %refs_7_.1) | copy-start | bytes 393220
  20.6 14.5 %copy-start.5 = (bf16[256,256]{1,0:T(8,128)(2,1)S(1)}, bf16[256,256]{1,0:T(8,128)(2,1)}, u32[]{:S(2)}) copy-start(bf16[256,256]{1,0:T(8,128)(2,1)} %refs_8_.1) | copy-start | bytes 393220
  20.6 14.5 %copy-start.6 = (f32[256]{0:T(256)S(1)}, f32[256]{0:T(256)}, u32[]{:S(2)}) copy-start(f32[256]{0:T(256)} %param.20) | copy-start | bytes 3076
  23.8 39.2 %copy-start.1 = (bf16[256,2048]{1,0:T(8,128)(2,1)S(1)}, bf16[256,2048]{1,0:T(8,128)(2,1)}, u32[]{:S(2)}) copy-start(bf16[256,2048]{1,0:T(8,128)(2,1)} %refs_9_.1) | copy-start | bytes 3145732
  23.8 39.2 %all-to-all-start = ((bf16[16,128,256]{2,1,0:T(8,128)(2,1)}), bf16[16,128,256]{2,1,0:T(8,128)(2,1)S(1)}, u32[]{:S(2)}, u32[]{:S(2)}) async-start(bf16[16,128,256]{2,1,0:T(8,128)(2,1)} %shard_map.154), calls=%async_computation | async-start | bytes 2097152 | tf_op jit(solution)/shard_map/all_to_all | solution.py:218
  35.1 119.8 %reduce-scatter.2.cloned.1.call-start = ((), (), s32[]{:S(2)}) async-start(), calls=%async_computation.7 | async-start | bytes 4718592 | tf_op jit(solution)/shard_map/reduce_scatter | solution.py:270
  94.9 43.2 %all-to-all-start.1 = ((bf16[16,176,256]{2,1,0:T(8,128)(2,1)}), bf16[16,176,256]{2,1,0:T(8,128)(2,1)S(1)}, u32[]{:S(2)}, u32[]{:S(2)}) async-start(bf16[16,176,256]{2,1,0:T(8,128)(2,1)} %get-tuple-element.12), calls=%async_computation.1 | async-start | bytes 2883584 | tf_op jit(solution)/shard_map/all_to_all | solution.py:218
  138.1 1.1 copy-start
  151.0 16.8 %all-to-all-start.3 = ((bf16[8,48,256]{2,1,0:T(8,128)(2,1)}), bf16[8,48,256]{2,1,0:T(8,128)(2,1)S(1)}, u32[]{:S(2)}, u32[]{:S(2)}) async-start(bf16[8,48,256]{2,1,0:T(8,128)(2,1)} %broadcast_in_dim.2), calls=%async_computation.4 | async-start | bytes 393216 | tf_op jit(solution)/shard_map/all_to_all | solution.py:218
  155.9 19.6 %collective-permute-start = (bf16[256,256]{1,0:T(8,128)(2,1)S(1)}, bf16[256,256]{1,0:T(8,128)(2,1)S(1)}, u32[]{:S(2)}, u32[]{:S(2)}) collective-permute-start(bf16[256,256]{1,0:T(8,128)(2,1)S(1)} %get-tuple-element.18), channel_id=1, source_target_pairs={{0,8},{8,16},{16,24},{24,0},{1,9},{9,17},{17,25},{25,1},{2,10},{10... | collective-permute-start | bytes 393224 | tf_op jit(solution)/shard_map/ppermute | solution.py:222
  158.2 17.3 %collective-permute-start.1 = (bf16[256,256]{1,0:T(8,128)(2,1)S(1)}, bf16[256,256]{1,0:T(8,128)(2,1)S(1)}, u32[]{:S(2)}, u32[]{:S(2)}) collective-permute-start(bf16[256,256]{1,0:T(8,128)(2,1)S(1)} %get-tuple-element.20), channel_id=1, source_target_pairs={{0,16},{8,24},{16,0},{24,8},{1,17},{9,25},{17,1},{25,9},{2,18},{10... | collective-permute-start | bytes 393224 | tf_op jit(solution)/shard_map/ppermute | solution.py:222
  161.8 13.7 %collective-permute-start.2 = (bf16[256,256]{1,0:T(8,128)(2,1)S(1)}, bf16[256,256]{1,0:T(8,128)(2,1)S(1)}, u32[]{:S(2)}, u32[]{:S(2)}) collective-permute-start(bf16[256,256]{1,0:T(8,128)(2,1)S(1)} %get-tuple-element.19), channel_id=1, source_target_pairs={{0,24},{8,0},{16,8},{24,16},{1,25},{9,1},{17,9},{25,17},{2,26},{10... | collective-permute-start | bytes 393224 | tf_op jit(solution)/shard_map/ppermute | solution.py:222
  167.7 7.8 %copy-start.2 = (f32[256,256]{1,0:T(8,128)S(1)}, f32[256,256]{1,0:T(8,128)}, u32[]{:S(2)}) copy-start(f32[256,256]{1,0:T(8,128)} %shard_map.156.refs_1_) | copy-start | bytes 786436
  167.8 0.7 copy-start.4
  170.1 14.1 %all-to-all-start.4 = ((bf16[8,48,256]{2,1,0:T(8,128)(2,1)}), bf16[8,48,256]{2,1,0:T(8,128)(2,1)S(1)}, u32[]{:S(2)}, u32[]{:S(2)}) async-start(bf16[8,48,256]{2,1,0:T(8,128)(2,1)} %shard_map.159), calls=%async_computation.5 | async-start | bytes 393216 | tf_op jit(solution)/shard_map/all_to_all | solution.py:218
Sparse Core Ops, SparseCore 0:
  20.7 63.8 all-gather.2
  95.0 56.8 reduce-scatter.1

commit v9 on v8

--- a/solution.py
+++ b/solution.py
@@ -26,7 +26,7 @@
 
 
 def call(
-    body, scalars, arrays, outs, out_specs=None, scratch=(), direct=(), extra=(), flops=0, vmem=60
+    body, scalars, arrays, outs, out_specs=None, scratch=(), direct=(), extra=(), flops=0, vmem=63
 ):
     count, first = len(arrays), len(scalars)
 
@@ -293,7 +293,7 @@
         flops=2 * NG * cut * width * nodes,
     )
     (part,) = call(
-        sum_body, [], [part], [sds((NY, share + SPARE_ROWS, width), BF)], extra=[base, terms]
+        sum_body, [], [part], [sds((NY, share + SPARE_ROWS, width), BF)], extra=[terms]
     )
     part = a2a(part, "y")
     grads = lax.all_gather(part, "c", axis=1).reshape(NG, share + SPARE_ROWS, width)

time: 198 us -> 195 us (0.985)
  waiting for transfers between devices: 85.1 us -> 81.9 us
    all_to_all x4, waiting for transfers between devices: 64.7 us -> 61.5 us  [a2a(): return lax.all_to_all(x, axis, 0, 0, tiled=True)]
where the time goes in v9:
time: 195 us; the launch traced here: 194 us
  waiting for transfers between devices  81.9 us (42%)
  starting transfers between devices  37.6 us (19%)
  blocking collectives  27.2 us (14%)
  Pallas kernels  25.1 us (13%)
  between operations  14.2 us (7%)
  local copies, waits for them, and re-layouts  3.84 us (2%)
  matrix products  2.03 us (1%)
    all_to_all x4, waiting for transfers between devices, a2a(): return lax.all_to_all(x, axis, 0, 0, tiled=True)  61.5 us
    all_to_all x4, starting transfers between devices, a2a(): return lax.all_to_all(x, axis, 0, 0, tiled=True)  29 us
    pallas_call x6, Pallas kernels, call(): pl.pallas_call(kernel, out_shape=tuple(outs), in_specs=[SMEM] * first + [...  25.1 us
    all_gather x1, waiting for transfers between devices, local(): lax.all_gather(gathered, 'z', axis=0, tiled=True)  20.4 us
    all_gather x1, blocking collectives, local(): gathered = lax.all_gather(features, 'x', axis=0, tiled=True)  13.3 us
    all_to_all x1, blocking collectives, a2a(): return lax.all_to_all(x, axis, 0, 0, tiled=True)  9.32 us
    ppermute x3, starting transfers between devices, shift(): return lax.ppermute(x, axis, [(i, (i + by) % n) for i in range(n)])  8.52 us
    all_gather x1, blocking collectives, local(): lax.all_gather(part, 'c', axis=1).reshape(NG, share + SPARE_ROWS, width)  4.59 us
  transfers between devices with their start and end apart: 9, of which 4 were waited for; matrix products, arithmetic and copies ran while one was open for 3% of the time, Pallas kernels for 8%

profile of v9, /device:TPU:1, one launch (start us, length us, event | category | flops | bytes accessed | tf_op | source)
XLA Modules:
  0.0 193.8 jit_solution(10728364738576460937)
XLA Ops:
  7.2 13.3 %all_gather.12 = bf16[1024,256]{1,0:T(8,128)(2,1)} all-gather(bf16[256,256]{1,0:T(8,128)(2,1)} %refs_7_.1), channel_id=1, replica_groups=mesh['y'=8,'c'=2,'x'=4,'z'=8] {'x'}, dimensions={0}, use_global_device_ids=true | all-gather | bytes 655360 | tf_op jit(solution)/shard_map/all_gather | solution.py:237
  20.6 3.2 %shard_map.154 = bf16[16,128,256]{2,1,0:T(8,128)(2,1)} custom-call(s32[1,16]{1,0:T(1,128)} %refs_0_.6, s32[16,128]{1,0:T(8,128)} %bitcast.35, bf16[256,256]{1,0:T(8,128)(2,1)} %refs_7_.1), custom_call_target="tpu_custom_call" | custom-call | flops 268435456 | bytes 1187840 | tf_op jit(solution)/shard_map/pallas_call | solution.py:48
  23.8 11.2 %all-to-all-start = ((bf16[16,128,256]{2,1,0:T(8,128)(2,1)}), bf16[16,128,256]{2,1,0:T(8,128)(2,1)S(1)}, u32[]{:S(2)}, u32[]{:S(2)}) async-start(bf16[16,128,256]{2,1,0:T(8,128)(2,1)} %shard_map.154), calls=%async_computation | async-start | bytes 2097152 | tf_op jit(solution)/shard_map/all_to_all | solution.py:218
  35.1 0.9 convolution_add_fusion.refs_4_
  36.0 27.0 %all-to-all-done = bf16[16,128,256]{2,1,0:T(8,128)(2,1)S(1)} async-done(((bf16[16,128,256]{2,1,0:T(8,128)(2,1)}), bf16[16,128,256]{2,1,0:T(8,128)(2,1)S(1)}, u32[]{:S(2)}, u32[]{:S(2)}) %all-to-all-start) | async-done | bytes 1048608 | tf_op jit(solution)/shard_map/all_to_all | solution.py:218
  63.0 1.1 convolution_bitcast_fusion.refs_3_
  64.2 20.4 %all-gather.3.cloned.1.call-done = bf16[8192,256]{1,0:T(8,128)(2,1)} async-done(((bf16[1024,256]{1,0:T(8,128)(2,1)}), bf16[8192,256]{1,0:T(8,128)(2,1)}) %all-gather.3.cloned.1.call-update) | async-done | bytes 4194320 | tf_op jit(solution)/shard_map/all_gather | solution.py:238
  84.6 10.2 %shard_map.155 = (bf16[256,256]{1,0:T(8,128)(2,1)}, bf16[256,256]{1,0:T(8,128)(2,1)}, bf16[16,176,256]{2,1,0:T(8,128)(2,1)}, f32[256,256]{1,0:T(8,128)}, bf16[64,128,256]{2,1,0:T(8,128)(2,1)}) custom-call(s32[2,24]{1,0:T(2,128)} %refs_0_.7, s32[2]{0:T(128)} %refs_1_.3, bf16[2,24,128,128]{3,2,1,0:T(8,128)(2,1)} %refs_2_.3, ...), custom_call_target="tpu_custom_call" | custom-call | flops 1073741824 | bytes 14024704 | tf_op jit(solution)/shard_map/pallas_call | solution.py:48
  94.9 7.4 %all-to-all-start.1 = ((bf16[16,176,256]{2,1,0:T(8,128)(2,1)}), bf16[16,176,256]{2,1,0:T(8,128)(2,1)}, u32[]{:S(2)}, u32[]{:S(2)}) async-start(bf16[16,176,256]{2,1,0:T(8,128)(2,1)} %get-tuple-element.12), calls=%async_computation.1 | async-start | bytes 2883584 | tf_op jit(solution)/shard_map/all_to_all | solution.py:218
  102.3 5.1 %shard_map.157.refs_1_ = bf16[2,24,128,128]{3,2,1,0:T(8,128)(2,1)} custom-call(s32[2,24]{1,0:T(2,128)} %refs_0_.7, s32[2]{0:T(128)} %refs_1_.3, bf16[256,256]{1,0:T(8,128)(2,1)} %get-tuple-element.15.refs_2_, bf16[64,128,256]{2,1,0:T(8,128)(2,1)} %bitcast.25), custom_call_target="tpu_custom_call" | custom-call | flops 402653184 | bytes 5898240 | tf_op jit(solution)/shard_map/pallas_call | solution.py:48
  107.4 30.8 %all-to-all-done.1.refs_2_.refs_0_ = bf16[16,176,256]{2,1,0:T(8,128)(2,1)} async-done(((bf16[16,176,256]{2,1,0:T(8,128)(2,1)}), bf16[16,176,256]{2,1,0:T(8,128)(2,1)}, u32[]{:S(2)}, u32[]{:S(2)}) %all-to-all-start.1) | async-done | bytes 1441824 | tf_op jit(solution)/shard_map/all_to_all | solution.py:218
  138.2 1.7 shard_map.158
  139.9 9.3 %all_to_all.25 = bf16[4,48,256]{2,1,0:T(8,128)(2,1)S(1)} all-to-all(bf16[4,48,256]{2,1,0:T(8,128)(2,1)} %shard_map.158), channel_id=1, replica_groups=mesh['y'=8,'c'=2,'x'=4,'z'=8] {'x'}, dimensions={0} | all-to-all | bytes 196608 | tf_op jit(solution)/shard_map/all_to_all | solution.py:218
  149.9 3.9 %all-to-all-start.3 = ((bf16[8,48,256]{2,1,0:T(8,128)(2,1)}), bf16[8,48,256]{2,1,0:T(8,128)(2,1)S(1)}, u32[]{:S(2)}, u32[]{:S(2)}) async-start(bf16[8,48,256]{2,1,0:T(8,128)(2,1)} %broadcast_in_dim.2), calls=%async_computation.4 | async-start | bytes 393216 | tf_op jit(solution)/shard_map/all_to_all | solution.py:218
  153.8 1.1 dynamic-slice_bitcast_fusion.2
  154.9 2.3 %collective-permute-start = (bf16[256,256]{1,0:T(8,128)(2,1)S(1)}, bf16[256,256]{1,0:T(8,128)(2,1)S(1)}, u32[]{:S(2)}, u32[]{:S(2)}) collective-permute-start(bf16[256,256]{1,0:T(8,128)(2,1)S(1)} %get-tuple-element.18), channel_id=1, source_target_pairs={{0,8},{8,16},{16,24},{24,0},{1,9},{9,17},{17,25},{25,1},{2,10},{10... | collective-permute-start | bytes 393224 | tf_op jit(solution)/shard_map/ppermute | solution.py:222
  157.2 3.6 %collective-permute-start.1 = (bf16[256,256]{1,0:T(8,128)(2,1)S(1)}, bf16[256,256]{1,0:T(8,128)(2,1)S(1)}, u32[]{:S(2)}, u32[]{:S(2)}) collective-permute-start(bf16[256,256]{1,0:T(8,128)(2,1)S(1)} %get-tuple-element.20), channel_id=1, source_target_pairs={{0,16},{8,24},{16,0},{24,8},{1,17},{9,25},{17,1},{25,9},{2,18},{10... | collective-permute-start | bytes 393224 | tf_op jit(solution)/shard_map/ppermute | solution.py:222
  160.8 2.6 %collective-permute-start.2 = (bf16[256,256]{1,0:T(8,128)(2,1)S(1)}, bf16[256,256]{1,0:T(8,128)(2,1)S(1)}, u32[]{:S(2)}, u32[]{:S(2)}) collective-permute-start(bf16[256,256]{1,0:T(8,128)(2,1)S(1)} %get-tuple-element.19), channel_id=1, source_target_pairs={{0,24},{8,0},{16,8},{24,16},{1,25},{9,1},{17,9},{25,17},{2,26},{10... | collective-permute-start | bytes 393224 | tf_op jit(solution)/shard_map/ppermute | solution.py:222
  164.1 1.6 shard_map.159
  165.8 6.5 %all-to-all-start.4 = ((bf16[8,48,256]{2,1,0:T(8,128)(2,1)}), bf16[8,48,256]{2,1,0:T(8,128)(2,1)S(1)}, u32[]{:S(2)}, u32[]{:S(2)}) async-start(bf16[8,48,256]{2,1,0:T(8,128)(2,1)} %shard_map.159), calls=%async_computation.5 | async-start | bytes 393216 | tf_op jit(solution)/shard_map/all_to_all | solution.py:218
  172.3 3.2 %shard_map.156 = f32[256,256]{1,0:T(8,128)} custom-call(s32[1,16]{1,0:T(1,128)} %refs_0_.6, s32[16,128]{1,0:T(8,128)} %bitcast.36, bf16[16,176,256]{2,1,0:T(8,128)(2,1)} %all-to-all-done.1.refs_2_.refs_0_, f32[256,256]{1,0:T(8,128)} %get-tuple-element.13.refs_3_), custom_call_target="tpu_custom_call" | custom-call | flops 268435456 | bytes 1974272 | tf_op jit(solution)/shard_map/pallas_call | solution.py:48
  175.5 1.7 fusion.3
  177.2 3.7 %all-to-all-done.4 = bf16[8,48,256]{2,1,0:T(8,128)(2,1)S(1)} async-done(((bf16[8,48,256]{2,1,0:T(8,128)(2,1)}), bf16[8,48,256]{2,1,0:T(8,128)(2,1)S(1)}, u32[]{:S(2)}, u32[]{:S(2)}) %all-to-all-start.4) | async-done | bytes 196640 | tf_op jit(solution)/shard_map/all_to_all | solution.py:218
  180.9 4.6 %all-gather = bf16[8,96,256]{2,1,0:T(8,128)(2,1)S(1)} all-gather(bf16[8,48,256]{2,1,0:T(8,128)(2,1)S(1)} %all-to-all-done.4), channel_id=2, replica_groups=mesh['y'=8,'c'=2,'x'=4,'z'=8] {'c'}, dimensions={1}, use_global_device_ids=true | all-gather | bytes 589824 | tf_op jit(solution)/shard_map/all_gather | solution.py:299
  (24 shorter events, 3.0 us)
Async XLA Ops:
  7.2 77.4 %all-gather.3.cloned.1.call-start = ((), (), s32[]{:S(2)}) async-start(), calls=%async_computation.6 | async-start | bytes 4718592 | tf_op jit(solution)/shard_map/all_gather | solution.py:238
  20.6 14.5 %copy-start.1 = (bf16[256,256]{1,0:T(8,128)(2,1)S(1)}, bf16[256,256]{1,0:T(8,128)(2,1)}, u32[]{:S(2)}) copy-start(bf16[256,256]{1,0:T(8,128)(2,1)} %refs_7_.1) | copy-start | bytes 393220
  20.6 14.5 %copy-start.3 = (bf16[256,256]{1,0:T(8,128)(2,1)S(1)}, bf16[256,256]{1,0:T(8,128)(2,1)}, u32[]{:S(2)}) copy-start(bf16[256,256]{1,0:T(8,128)(2,1)} %refs_8_.1) | copy-start | bytes 393220
  20.6 14.5 %copy-start.4 = (f32[256]{0:T(256)S(1)}, f32[256]{0:T(256)}, u32[]{:S(2)}) copy-start(f32[256]{0:T(256)} %param.20) | copy-start | bytes 3076
  23.8 39.2 %copy-start = (bf16[256,2048]{1,0:T(8,128)(2,1)S(1)}, bf16[256,2048]{1,0:T(8,128)(2,1)}, u32[]{:S(2)}) copy-start(bf16[256,2048]{1,0:T(8,128)(2,1)} %refs_9_.1) | copy-start | bytes 3145732
  23.8 39.2 %all-to-all-start = ((bf16[16,128,256]{2,1,0:T(8,128)(2,1)}), bf16[16,128,256]{2,1,0:T(8,128)(2,1)S(1)}, u32[]{:S(2)}, u32[]{:S(2)}) async-start(bf16[16,128,256]{2,1,0:T(8,128)(2,1)} %shard_map.154), calls=%async_computation | async-start | bytes 2097152 | tf_op jit(solution)/shard_map/all_to_all | solution.py:218
  35.1 118.8 %reduce-scatter.2.cloned.1.call-start = ((), (), s32[]{:S(2)}) async-start(), calls=%async_computation.7 | async-start | bytes 4718592 | tf_op jit(solution)/shard_map/reduce_scatter | solution.py:270
  94.9 43.3 %all-to-all-start.1 = ((bf16[16,176,256]{2,1,0:T(8,128)(2,1)}), bf16[16,176,256]{2,1,0:T(8,128)(2,1)}, u32[]{:S(2)}, u32[]{:S(2)}) async-start(bf16[16,176,256]{2,1,0:T(8,128)(2,1)} %get-tuple-element.12), calls=%async_computation.1 | async-start | bytes 2883584 | tf_op jit(solution)/shard_map/all_to_all | solution.py:218
  149.9 13.5 %all-to-all-start.3 = ((bf16[8,48,256]{2,1,0:T(8,128)(2,1)}), bf16[8,48,256]{2,1,0:T(8,128)(2,1)S(1)}, u32[]{:S(2)}, u32[]{:S(2)}) async-start(bf16[8,48,256]{2,1,0:T(8,128)(2,1)} %broadcast_in_dim.2), calls=%async_computation.4 | async-start | bytes 393216 | tf_op jit(solution)/shard_map/all_to_all | solution.py:218
  154.9 20.6 %collective-permute-start = (bf16[256,256]{1,0:T(8,128)(2,1)S(1)}, bf16[256,256]{1,0:T(8,128)(2,1)S(1)}, u32[]{:S(2)}, u32[]{:S(2)}) collective-permute-start(bf16[256,256]{1,0:T(8,128)(2,1)S(1)} %get-tuple-element.18), channel_id=1, source_target_pairs={{0,8},{8,16},{16,24},{24,0},{1,9},{9,17},{17,25},{25,1},{2,10},{10... | collective-permute-start | bytes 393224 | tf_op jit(solution)/shard_map/ppermute | solution.py:222
  157.2 18.3 %collective-permute-start.1 = (bf16[256,256]{1,0:T(8,128)(2,1)S(1)}, bf16[256,256]{1,0:T(8,128)(2,1)S(1)}, u32[]{:S(2)}, u32[]{:S(2)}) collective-permute-start(bf16[256,256]{1,0:T(8,128)(2,1)S(1)} %get-tuple-element.20), channel_id=1, source_target_pairs={{0,16},{8,24},{16,0},{24,8},{1,17},{9,25},{17,1},{25,9},{2,18},{10... | collective-permute-start | bytes 393224 | tf_op jit(solution)/shard_map/ppermute | solution.py:222
  160.8 14.7 %collective-permute-start.2 = (bf16[256,256]{1,0:T(8,128)(2,1)S(1)}, bf16[256,256]{1,0:T(8,128)(2,1)S(1)}, u32[]{:S(2)}, u32[]{:S(2)}) collective-permute-start(bf16[256,256]{1,0:T(8,128)(2,1)S(1)} %get-tuple-element.19), channel_id=1, source_target_pairs={{0,24},{8,0},{16,8},{24,16},{1,25},{9,1},{17,9},{25,17},{2,26},{10... | collective-permute-start | bytes 393224 | tf_op jit(solution)/shard_map/ppermute | solution.py:222
  163.5 0.7 copy-start.2
  165.8 15.1 %all-to-all-start.4 = ((bf16[8,48,256]{2,1,0:T(8,128)(2,1)}), bf16[8,48,256]{2,1,0:T(8,128)(2,1)S(1)}, u32[]{:S(2)}, u32[]{:S(2)}) async-start(bf16[8,48,256]{2,1,0:T(8,128)(2,1)} %shard_map.159), calls=%async_computation.5 | async-start | bytes 393216 | tf_op jit(solution)/shard_map/all_to_all | solution.py:218
Sparse Core Ops, SparseCore 0:
  20.7 63.8 all-gather.2
  95.0 56.8 reduce-scatter.1

commit v10 on v9

--- a/solution.py
+++ b/solution.py
@@ -93,7 +93,7 @@
 ):
     index_ref, count_ref = scalars
     blocks_ref, outer_ref, pre_ref, w_ref, dout_ref, feat_ref, wself_ref, cut_ref = arrays
-    out_ref, dagg_ref, back_ref, self_ref, term_ref = outs
+    out_ref, dagg_ref, back_ref, part_ref, self_ref, term_ref = outs
     tile_copy = pltpu.make_async_copy(gathered[0], tiles.at[pl.ds(0, 2 * BANDS)], tile_sem)
     tile_copy.start()
     slots = blocks_ref.shape[1]
@@ -153,19 +153,19 @@
         grad = lax.dot_general(left, d_pre, TN, preferred_element_type=F32).astype(BF)
         for g in range(groups // 2):
             spot = i * groups // 2 + g
-            back_ref[spot, pl.ds(cut, share), :] = grad[g * share : (g + 1) * share]
+            part_ref[spot, pl.ds(0, share), :] = grad[g * share : (g + 1) * share]
     bias = jnp.sum(d_pre.astype(F32), axis=0, keepdims=True)
     row = lax.broadcasted_iota(jnp.int32, (SPARE_ROWS, width), 0)
     bias = jnp.where(row == 0, bias, 0.0).astype(BF)
     for g in range(groups):
-        back_ref[g, pl.ds(cut + share, SPARE_ROWS), :] = bias
+        part_ref[g, pl.ds(share, SPARE_ROWS), :] = bias
     d_agg = jnp.concatenate(d_aggs, axis=0)
     for g in range(0, groups, 2):
         rows = lax.dot_general(
             cut_ref[:, pl.ds(g * cut, 2 * cut)], d_agg, TN, preferred_element_type=F32
         ).astype(BF)
-        back_ref[g, pl.ds(0, cut), :] = rows[:cut]
-        back_ref[g + 1, pl.ds(0, cut), :] = rows[cut:]
+        back_ref[g] = rows[:cut]
+        back_ref[g + 1] = rows[cut:]
     self_ref[...] = lax.dot_general(d_pre, wself_ref[...], NT, preferred_element_type=F32)
     wait(stores)
 
@@ -184,24 +184,15 @@
 
 def base_body(scalars, arrays, copies, outs):
     (count_ref,), (rows_ref, back_ref, self_ref), (out_ref,) = scalars, arrays, outs
-    cut = rows_ref.shape[1]
     wait(copies)
     total = self_ref[...]
     for g in range(0, back_ref.shape[0], 2):
         hot = jnp.concatenate(
             [hot_columns(rows_ref, count_ref, g + i, total.shape[0]) for i in range(2)], axis=1
         )
-        rows = jnp.concatenate([back_ref[g + i, pl.ds(0, cut), :] for i in range(2)], axis=0)
+        rows = jnp.concatenate([back_ref[g], back_ref[g + 1]], axis=0)
         total = total + jnp.dot(hot, rows, preferred_element_type=F32)
     out_ref[...] = total
-
-
-def behind_body(scalars, arrays, copies, outs, returned, parts_ref, sem):
-    rows = parts_ref.shape[1]
-    first = returned[0].shape[1] - rows
-    copy = pltpu.make_async_copy(returned[0].at[:, pl.ds(first, rows)], parts_ref, sem)
-    copy.start()
-    sum_body(scalars, (parts_ref,), [copy], outs)
 
 
 def sum_body(scalars, arrays, copies, outs):
@@ -212,6 +203,17 @@
         total = total + parts_ref[i].astype(F32)
     for i in range(out_ref.shape[0]):
         out_ref[i] = total.astype(BF)
+
+
+def gate(x, after):
+    return pl.pallas_call(
+        lambda x_ref, after_ref, out_ref: None,
+        out_shape=sds(x.shape, x.dtype),
+        in_specs=[HBM, HBM],
+        out_specs=HBM,
+        input_output_aliases={0: 0},
+        compiler_params=pltpu.CompilerParams(vmem_limit_bytes=63 << 20),
+    )(x, after)
 
 
 def a2a(x, axis):
@@ -246,11 +248,11 @@
 
     share = 2 * width // NG
     outs = [
-        node_bf, node_bf, sds((NG, cut + share + SPARE_ROWS, width), BF), node_f32,
+        node_bf, node_bf, cut_bf, sds((NG, share + SPARE_ROWS, width), BF), node_f32,
         sds(gathered.shape, BF),
     ]
     spared = (2 * BANDS + 1, 128, width)
-    output, d_agg, back, self_back, terms = call(
+    output, d_agg, back, part, self_back, terms = call(
         main_body,
         [block_index, block_count],
         [block_values, outer, own_pre, w_neigh, d_out, features, w_self, cut_weight],
@@ -271,19 +273,18 @@
     terms = terms.reshape(NX, nodes, width)
     me = lax.axis_index("x")
 
-    returned = a2a(back, ("y", "c"))
+    part = jnp.sum(a2a(part, ("y", "c")).astype(F32), axis=0).astype(BF)
+    returned = a2a(gate(back, part), ("y", "c"))
+    part = lax.all_gather(part, "x", axis=0)
     (grad_blocks,) = call(
         blocks_body, [block_index, block_count], [d_agg, gathered], [sds(block_values.shape, BF)],
         flops=2 * tiles_here * slots * 128 * 128 * width,
     )
     (part,) = call(
-        behind_body, [], [], [sds((NX, share + SPARE_ROWS, width), BF)],
-        scratch=[pltpu.VMEM((NG, share + SPARE_ROWS, width), BF), pltpu.SemaphoreType.DMA],
-        direct=[returned], extra=[grad_blocks],
-    )
-    part = a2a(part, "x")
-    part = jnp.sum(part.astype(F32), axis=0).astype(BF)
-    part = a2a(jnp.broadcast_to(part[None], (NZ, *part.shape)), "z")
+        sum_body, [], [part], [sds((NZ, share + SPARE_ROWS, width), BF)],
+        extra=[returned, grad_blocks],
+    )
+    part = a2a(part, "z")
     moved = []
     for by in range(NX):
         rows = lax.dynamic_index_in_dim(terms, (me + by) & (NX - 1), 0, keepdims=False)

time: 195 us -> 195 us (level)
  blocking collectives: 27.2 us -> 50.8 us
  waiting for transfers between devices: 81.9 us -> 61 us
  starting transfers between devices: 37.6 us -> 33.3 us
    all_to_all x4, waiting for transfers between devices: 61.5 us -> 41.5 us  [a2a(): return lax.all_to_all(x, axis, 0, 0, tiled=True)]
    all_to_all x1, blocking collectives: 9.32 us -> 21.8 us  [a2a(): return lax.all_to_all(x, axis, 0, 0, tiled=True)]
    all_gather x0 -> x1, blocking collectives: none -> 11 us  [local(): part = lax.all_gather(part, 'x', axis=0)]
    all_to_all x4, starting transfers between devices: 29 us -> 22.7 us  [a2a(): return lax.all_to_all(x, axis, 0, 0, tiled=True)]
    ppermute x3, starting transfers between devices: 8.52 us -> 10.5 us  [shift(): return lax.ppermute(x, axis, [(i, (i + by) % n) for i in range(n)])]
where the time goes in v10:
time: 195 us; the launch traced here: 194 us
  waiting for transfers between devices  61 us (31%)
  blocking collectives  50.8 us (26%)
  starting transfers between devices  33.3 us (17%)
  Pallas kernels  24.8 us (13%)
  between operations  14.3 us (7%)
  local copies, waits for them, and re-layouts  4.11 us (2%)
  matrix products  3.26 us (2%)
  other arithmetic  2.46 us (1%)
    all_to_all x4, waiting for transfers between devices, a2a(): return lax.all_to_all(x, axis, 0, 0, tiled=True)  41.5 us
    pallas_call x6, Pallas kernels, call(): pl.pallas_call(kernel, out_shape=tuple(outs), in_specs=[SMEM] * first + [...  24.8 us
    all_to_all x4, starting transfers between devices, a2a(): return lax.all_to_all(x, axis, 0, 0, tiled=True)  22.7 us
    all_to_all x1, blocking collectives, a2a(): return lax.all_to_all(x, axis, 0, 0, tiled=True)  21.8 us
    all_gather x1, waiting for transfers between devices, local(): lax.all_gather(gathered, 'z', axis=0, tiled=True)  19.5 us
    all_gather x1, blocking collectives, local(): gathered = lax.all_gather(features, 'x', axis=0, tiled=True)  13.5 us
    all_gather x1, blocking collectives, local(): part = lax.all_gather(part, 'x', axis=0)  11 us
    ppermute x3, starting transfers between devices, shift(): return lax.ppermute(x, axis, [(i, (i + by) % n) for i in range(n)])  10.5 us
  transfers between devices with their start and end apart: 9, of which 4 were waited for; matrix products, arithmetic and copies ran while one was open for 3% of the time, Pallas kernels for 8%

profile of v10, /device:TPU:1, one launch (start us, length us, event | category | flops | bytes accessed | tf_op | source)
XLA Modules:
  0.0 194.0 jit_solution(14780211072871097484)
XLA Ops:
  7.2 13.5 %all_gather.18 = bf16[1024,256]{1,0:T(8,128)(2,1)} all-gather(bf16[256,256]{1,0:T(8,128)(2,1)} %refs_7_.1), channel_id=1, replica_groups=mesh['y'=8,'c'=2,'x'=4,'z'=8] {'x'}, dimensions={0}, use_global_device_ids=true | all-gather | bytes 655360 | tf_op jit(solution)/shard_map/all_gather | solution.py:239
  20.7 3.1 %shard_map.154 = bf16[16,128,256]{2,1,0:T(8,128)(2,1)} custom-call(s32[1,16]{1,0:T(1,128)} %refs_0_.6, s32[16,128]{1,0:T(8,128)} %bitcast.37, bf16[256,256]{1,0:T(8,128)(2,1)} %refs_7_.1), custom_call_target="tpu_custom_call" | custom-call | flops 268435456 | bytes 1187840 | tf_op jit(solution)/shard_map/pallas_call | solution.py:48
  23.8 11.1 %all-to-all-start = ((bf16[16,128,256]{2,1,0:T(8,128)(2,1)}), bf16[16,128,256]{2,1,0:T(8,128)(2,1)S(1)}, u32[]{:S(2)}, u32[]{:S(2)}) async-start(bf16[16,128,256]{2,1,0:T(8,128)(2,1)} %shard_map.154), calls=%async_computation | async-start | bytes 2097152 | tf_op jit(solution)/shard_map/all_to_all | solution.py:220
  35.9 27.0 %all-to-all-done = bf16[16,128,256]{2,1,0:T(8,128)(2,1)S(1)} async-done(((bf16[16,128,256]{2,1,0:T(8,128)(2,1)}), bf16[16,128,256]{2,1,0:T(8,128)(2,1)S(1)}, u32[]{:S(2)}, u32[]{:S(2)}) %all-to-all-start) | async-done | bytes 1048608 | tf_op jit(solution)/shard_map/all_to_all | solution.py:220
  62.9 2.4 %convolution_bitcast_fusion.refs_3_ = f32[256,256]{1,0:T(8,128)} fusion(bf16[256,2048]{1,0:T(8,128)(2,1)} %refs_9_.1, bf16[2048,256]{1,0:T(8,128)(2,1)S(1)} %bitcast.28), kind=kOutput, calls=%fused_computation.1 | convolution fusion | flops 268435456 | bytes 2359296 | tf_op jit(solution)/shard_map/dot_general | solution.py:246
  65.3 19.5 %all-gather.4.cloned.1.call-done = bf16[8192,256]{1,0:T(8,128)(2,1)} async-done(((bf16[1024,256]{1,0:T(8,128)(2,1)}), bf16[8192,256]{1,0:T(8,128)(2,1)}) %all-gather.4.cloned.1.call-update) | async-done | bytes 4194320 | tf_op jit(solution)/shard_map/all_gather | solution.py:240
  84.8 10.2 %shard_map.155 = (bf16[256,256]{1,0:T(8,128)(2,1)}, bf16[256,256]{1,0:T(8,128)(2,1)}, bf16[16,128,256]{2,1,0:T(8,128)(2,1)}, bf16[16,48,256]{2,1,0:T(8,128)(2,1)...) custom-call(s32[2,24]{1,0:T(2,128)} %refs_0_.7, s32[2]{0:T(128)} %refs_1_.3, bf16[2,24,128,128]{3,2,1,0:T(8,128)(2,1)} %refs_2_.3, ...), custom_call_target="tpu_custom_call" | custom-call | flops 1073741824 | bytes 14024704 | tf_op jit(solution)/shard_map/pallas_call | solution.py:48
  96.0 21.8 %all_to_all.25 = bf16[16,48,256]{2,1,0:T(8,128)(2,1)S(1)} all-to-all(bf16[16,48,256]{2,1,0:T(8,128)(2,1)S(1)} %copy-done.3), channel_id=1, replica_groups=mesh['y'=8,'c'=2,'x'=4,'z'=8] {'y','c'}, dimensions={0} | all-to-all | bytes 786432 | tf_op jit(solution)/shard_map/all_to_all | solution.py:220
  118.4 4.4 %all-to-all-start.2 = ((bf16[16,128,256]{2,1,0:T(8,128)(2,1)}), bf16[16,128,256]{2,1,0:T(8,128)(2,1)}, u32[]{:S(2)}, u32[]{:S(2)}) async-start(bf16[16,128,256]{2,1,0:T(8,128)(2,1)} %shard_map.156), calls=%async_computation.2 | async-start | bytes 2097152 | tf_op jit(solution)/shard_map/all_to_all | solution.py:220
  122.8 5.2 %shard_map.158.refs_2_ = bf16[2,24,128,128]{3,2,1,0:T(8,128)(2,1)} custom-call(s32[2,24]{1,0:T(2,128)} %refs_0_.7, s32[2]{0:T(128)} %refs_1_.3, bf16[256,256]{1,0:T(8,128)(2,1)} %get-tuple-element.17.refs_2_, bf16[64,128,256]{2,1,0:T(8,128)(2,1)} %bitcast.26), custom_call_target="tpu_custom_call" | custom-call | flops 402653184 | bytes 5898240 | tf_op jit(solution)/shard_map/pallas_call | solution.py:48
  128.0 11.0 %all-gather = bf16[192,256]{1,0:T(8,128)(2,1)} all-gather(bf16[48,256]{1,0:T(8,128)(2,1)S(1)} %copy-done.4), channel_id=2, replica_groups=mesh['y'=8,'c'=2,'x'=4,'z'=8] {'x'}, dimensions={0}, use_global_device_ids=true | all-gather | bytes 122880 | tf_op jit(solution)/shard_map/all_gather | solution.py:278
  138.9 10.8 %all-to-all-done.2.refs_2_.refs_1_ = bf16[16,128,256]{2,1,0:T(8,128)(2,1)} async-done(((bf16[16,128,256]{2,1,0:T(8,128)(2,1)}), bf16[16,128,256]{2,1,0:T(8,128)(2,1)}, u32[]{:S(2)}, u32[]{:S(2)}) %all-to-all-start.2) | async-done | bytes 1048608 | tf_op jit(solution)/shard_map/all_to_all | solution.py:220
  149.8 1.6 shard_map.159
  151.4 3.9 %all-to-all-start.3 = ((bf16[8,48,256]{2,1,0:T(8,128)(2,1)}), bf16[8,48,256]{2,1,0:T(8,128)(2,1)S(1)}, u32[]{:S(2)}, u32[]{:S(2)}) async-start(bf16[8,48,256]{2,1,0:T(8,128)(2,1)} %shard_map.159), calls=%async_computation.4 | async-start | bytes 393216 | tf_op jit(solution)/shard_map/all_to_all | solution.py:220
  155.3 1.1 dynamic-slice_bitcast_fusion.2
  156.4 3.1 %collective-permute-start = (bf16[256,256]{1,0:T(8,128)(2,1)S(1)}, bf16[256,256]{1,0:T(8,128)(2,1)S(1)}, u32[]{:S(2)}, u32[]{:S(2)}) collective-permute-start(bf16[256,256]{1,0:T(8,128)(2,1)S(1)} %get-tuple-element.20), channel_id=1, source_target_pairs={{0,8},{8,16},{16,24},{24,0},{1,9},{9,17},{17,25},{25,1},{2,10},{10... | collective-permute-start | bytes 393224 | tf_op jit(solution)/shard_map/ppermute | solution.py:224
  159.5 4.3 %collective-permute-start.1 = (bf16[256,256]{1,0:T(8,128)(2,1)S(1)}, bf16[256,256]{1,0:T(8,128)(2,1)S(1)}, u32[]{:S(2)}, u32[]{:S(2)}) collective-permute-start(bf16[256,256]{1,0:T(8,128)(2,1)S(1)} %get-tuple-element.22), channel_id=1, source_target_pairs={{0,16},{8,24},{16,0},{24,8},{1,17},{9,25},{17,1},{25,9},{2,18},{10... | collective-permute-start | bytes 393224 | tf_op jit(solution)/shard_map/ppermute | solution.py:224
  163.8 3.1 %collective-permute-start.2 = (bf16[256,256]{1,0:T(8,128)(2,1)S(1)}, bf16[256,256]{1,0:T(8,128)(2,1)S(1)}, u32[]{:S(2)}, u32[]{:S(2)}) collective-permute-start(bf16[256,256]{1,0:T(8,128)(2,1)S(1)} %get-tuple-element.21), channel_id=1, source_target_pairs={{0,24},{8,0},{16,8},{24,16},{1,25},{9,1},{17,9},{25,17},{2,26},{10... | collective-permute-start | bytes 393224 | tf_op jit(solution)/shard_map/ppermute | solution.py:224
  167.6 1.6 shard_map.160
  169.2 3.4 %all-to-all-start.4 = ((bf16[8,48,256]{2,1,0:T(8,128)(2,1)}), bf16[8,48,256]{2,1,0:T(8,128)(2,1)S(1)}, u32[]{:S(2)}, u32[]{:S(2)}) async-start(bf16[8,48,256]{2,1,0:T(8,128)(2,1)} %shard_map.160), calls=%async_computation.5 | async-start | bytes 393216 | tf_op jit(solution)/shard_map/all_to_all | solution.py:220
  172.6 3.1 %shard_map.157 = f32[256,256]{1,0:T(8,128)} custom-call(s32[1,16]{1,0:T(1,128)} %refs_0_.6, s32[16,128]{1,0:T(8,128)} %bitcast.38, bf16[16,128,256]{2,1,0:T(8,128)(2,1)} %all-to-all-done.2.refs_2_.refs_1_, f32[256,256]{1,0:T(8,128)} %get-tuple-element.15.refs_3_), custom_call_target="tpu_custom_call" | custom-call | flops 268435456 | bytes 1581056 | tf_op jit(solution)/shard_map/pallas_call | solution.py:48
  175.8 1.7 fusion.3
  177.5 3.6 %all-to-all-done.4 = bf16[8,48,256]{2,1,0:T(8,128)(2,1)S(1)} async-done(((bf16[8,48,256]{2,1,0:T(8,128)(2,1)}), bf16[8,48,256]{2,1,0:T(8,128)(2,1)S(1)}, u32[]{:S(2)}, u32[]{:S(2)}) %all-to-all-start.4) | async-done | bytes 196640 | tf_op jit(solution)/shard_map/all_to_all | solution.py:220
  181.1 4.6 %all-gather.1 = bf16[8,96,256]{2,1,0:T(8,128)(2,1)S(1)} all-gather(bf16[8,48,256]{2,1,0:T(8,128)(2,1)S(1)} %all-to-all-done.4), channel_id=3, replica_groups=mesh['y'=8,'c'=2,'x'=4,'z'=8] {'c'}, dimensions={1}, use_global_device_ids=true | all-gather | bytes 589824 | tf_op jit(solution)/shard_map/all_gather | solution.py:300
  (27 shorter events, 4.8 us)
Async XLA Ops:
  7.2 27.8 %copy-start = (bf16[256,256]{1,0:T(8,128)(2,1)S(1)}, bf16[256,256]{1,0:T(8,128)(2,1)}, u32[]{:S(2)}) copy-start(bf16[256,256]{1,0:T(8,128)(2,1)} %refs_7_.1) | copy-start | bytes 393220
  7.2 27.8 %copy-start.2 = (bf16[256,256]{1,0:T(8,128)(2,1)S(1)}, bf16[256,256]{1,0:T(8,128)(2,1)}, u32[]{:S(2)}) copy-start(bf16[256,256]{1,0:T(8,128)(2,1)} %refs_8_.1) | copy-start | bytes 393220
  7.2 27.8 %copy-start.5 = (f32[256]{0:T(256)S(1)}, f32[256]{0:T(256)}, u32[]{:S(2)}) copy-start(f32[256]{0:T(256)} %param.20) | copy-start | bytes 3076
  7.2 77.6 %all-gather.4.cloned.1.call-start = ((), (), s32[]{:S(2)}) async-start(), calls=%async_computation.6 | async-start | bytes 4718592 | tf_op jit(solution)/shard_map/all_gather | solution.py:240
  23.8 39.1 %all-to-all-start = ((bf16[16,128,256]{2,1,0:T(8,128)(2,1)}), bf16[16,128,256]{2,1,0:T(8,128)(2,1)S(1)}, u32[]{:S(2)}, u32[]{:S(2)}) async-start(bf16[16,128,256]{2,1,0:T(8,128)(2,1)} %shard_map.154), calls=%async_computation | async-start | bytes 2097152 | tf_op jit(solution)/shard_map/all_to_all | solution.py:220
  34.9 120.4 %reduce-scatter.2.cloned.1.call-start = ((), (), s32[]{:S(2)}) async-start(), calls=%async_computation.7 | async-start | bytes 4718592 | tf_op jit(solution)/shard_map/reduce_scatter | solution.py:272
  95.0 1.0 copy-start.3
  118.4 9.6 %copy-start.4 = (bf16[48,256]{1,0:T(8,128)(2,1)S(1)}, bf16[48,256]{1,0:T(8,128)(2,1)}, u32[]{:S(2)}) copy-start(bf16[48,256]{1,0:T(8,128)(2,1)} %reduce_sum.12.after_ref) | copy-start | bytes 73732
  118.4 31.4 %all-to-all-start.2 = ((bf16[16,128,256]{2,1,0:T(8,128)(2,1)}), bf16[16,128,256]{2,1,0:T(8,128)(2,1)}, u32[]{:S(2)}, u32[]{:S(2)}) async-start(bf16[16,128,256]{2,1,0:T(8,128)(2,1)} %shard_map.156), calls=%async_computation.2 | async-start | bytes 2097152 | tf_op jit(solution)/shard_map/all_to_all | solution.py:220
  151.4 15.5 %all-to-all-start.3 = ((bf16[8,48,256]{2,1,0:T(8,128)(2,1)}), bf16[8,48,256]{2,1,0:T(8,128)(2,1)S(1)}, u32[]{:S(2)}, u32[]{:S(2)}) async-start(bf16[8,48,256]{2,1,0:T(8,128)(2,1)} %shard_map.159), calls=%async_computation.4 | async-start | bytes 393216 | tf_op jit(solution)/shard_map/all_to_all | solution.py:220
  156.4 19.4 %collective-permute-start = (bf16[256,256]{1,0:T(8,128)(2,1)S(1)}, bf16[256,256]{1,0:T(8,128)(2,1)S(1)}, u32[]{:S(2)}, u32[]{:S(2)}) collective-permute-start(bf16[256,256]{1,0:T(8,128)(2,1)S(1)} %get-tuple-element.20), channel_id=1, source_target_pairs={{0,8},{8,16},{16,24},{24,0},{1,9},{9,17},{17,25},{25,1},{2,10},{10... | collective-permute-start | bytes 393224 | tf_op jit(solution)/shard_map/ppermute | solution.py:224
  159.5 16.3 %collective-permute-start.1 = (bf16[256,256]{1,0:T(8,128)(2,1)S(1)}, bf16[256,256]{1,0:T(8,128)(2,1)S(1)}, u32[]{:S(2)}, u32[]{:S(2)}) collective-permute-start(bf16[256,256]{1,0:T(8,128)(2,1)S(1)} %get-tuple-element.22), channel_id=1, source_target_pairs={{0,16},{8,24},{16,0},{24,8},{1,17},{9,25},{17,1},{25,9},{2,18},{10... | collective-permute-start | bytes 393224 | tf_op jit(solution)/shard_map/ppermute | solution.py:224
  163.8 12.0 %collective-permute-start.2 = (bf16[256,256]{1,0:T(8,128)(2,1)S(1)}, bf16[256,256]{1,0:T(8,128)(2,1)S(1)}, u32[]{:S(2)}, u32[]{:S(2)}) collective-permute-start(bf16[256,256]{1,0:T(8,128)(2,1)S(1)} %get-tuple-element.21), channel_id=1, source_target_pairs={{0,24},{8,0},{16,8},{24,16},{1,25},{9,1},{17,9},{25,17},{2,26},{10... | collective-permute-start | bytes 393224 | tf_op jit(solution)/shard_map/ppermute | solution.py:224
  166.9 0.7 copy-start.1
  169.2 11.9 %all-to-all-start.4 = ((bf16[8,48,256]{2,1,0:T(8,128)(2,1)}), bf16[8,48,256]{2,1,0:T(8,128)(2,1)S(1)}, u32[]{:S(2)}, u32[]{:S(2)}) async-start(bf16[8,48,256]{2,1,0:T(8,128)(2,1)} %shard_map.160), calls=%async_computation.5 | async-start | bytes 393216 | tf_op jit(solution)/shard_map/all_to_all | solution.py:220
Sparse Core Ops, SparseCore 0:
  20.9 63.8 all-gather.3
  95.1 56.8 reduce-scatter.1

commit v11 on v9

--- a/solution.py
+++ b/solution.py
@@ -16,6 +16,7 @@
 BANDS = NX * NZ
 SPARE_ROWS = 16
 STORE = 8
+FIRST = NZ * (2 * NX - 1)
 VMEM = pl.BlockSpec(memory_space=pltpu.VMEM)
 SMEM = pl.BlockSpec(memory_space=pltpu.SMEM)
 HBM = pl.BlockSpec(memory_space=pltpu.HBM)
@@ -88,14 +89,25 @@
     return (z * NX + x) * 2 + (index & 1)
 
 
+def tile_spot(index_ref, t, k):
+    index = index_ref[t, k]
+    z = lax.shift_right_logical(index, 1) & (NZ - 1)
+    tile = lax.shift_right_logical(index, 4) * 2 + (index & 1)
+    return jnp.where(tile == 2 * NX - 1, FIRST + z, z * (2 * NX - 1) + tile)
+
+
 def main_body(
     scalars, arrays, copies, outs, gathered, tiles, acc, terms, tile_sem, term_sems
 ):
     index_ref, count_ref = scalars
     blocks_ref, outer_ref, pre_ref, w_ref, dout_ref, feat_ref, wself_ref, cut_ref = arrays
     out_ref, dagg_ref, back_ref, self_ref, term_ref = outs
-    tile_copy = pltpu.make_async_copy(gathered[0], tiles.at[pl.ds(0, 2 * BANDS)], tile_sem)
-    tile_copy.start()
+    tile_copies = [
+        pltpu.make_async_copy(gathered[0], tiles.at[pl.ds(0, FIRST)], tile_sem.at[0]),
+        pltpu.make_async_copy(gathered[1], tiles.at[pl.ds(FIRST, NZ)], tile_sem.at[1]),
+    ]
+    for copy in tile_copies:
+        copy.start()
     slots = blocks_ref.shape[1]
     spare = 2 * BANDS
     tiles[spare] = jnp.zeros(tiles.shape[1:], BF)
@@ -106,13 +118,13 @@
 
     lax.fori_loop(0, spare, clear, 0)
     wait(copies)
-    tile_copy.wait()
+    wait(tile_copies)
     aggs, d_pres, d_aggs = [], [], []
     for t in range(2):
         rows = pl.ds(t * 128, 128)
-        spots = [
-            jnp.where(k < count_ref[t], spot_of(index_ref, t, k), spare)
-            for k in range(slots)
+        spots, term_spots = [
+            [jnp.where(k < count_ref[t], spot(index_ref, t, k), spare) for k in range(slots)]
+            for spot in (tile_spot, spot_of)
         ]
         total = outer_ref[rows, :]
         for k in range(0, slots, 2):
@@ -128,7 +140,7 @@
         dagg_ref[rows, :] = d_agg
         for k in range(slots):
             term = lax.dot_general(blocks_ref[t, k], d_agg, TN, preferred_element_type=F32)
-            acc[spots[k]] = acc[spots[k]] + term
+            acc[term_spots[k]] = acc[term_spots[k]] + term
         d_aggs.append(d_agg)
         aggs.append(agg)
         d_pres.append(d_pre)
@@ -171,13 +183,16 @@
 
 
 def blocks_body(scalars, arrays, copies, outs):
-    (index_ref, count_ref), (dagg_ref, tiles), (out_ref,) = scalars, arrays, outs
+    (index_ref, count_ref), (dagg_ref, first, last), (out_ref,) = scalars, arrays, outs
     wait(copies)
     for t in range(2):
         d_agg = dagg_ref[pl.ds(t * 128, 128), :]
         for k in range(out_ref.shape[1]):
             live = jnp.where(k < count_ref[t], 1.0, 0.0)
-            tile = tiles[spot_of(index_ref, t, k)]
+            spot = tile_spot(index_ref, t, k)
+            tile = jnp.where(
+                spot < FIRST, first[jnp.minimum(spot, FIRST - 1)], last[jnp.maximum(spot - FIRST, 0)]
+            )
             grad = lax.dot_general(d_agg, tile, NT, preferred_element_type=F32)
             out_ref[t, k] = (grad * live).astype(BF)
 
@@ -234,8 +249,11 @@
     node_bf, node_f32 = sds((nodes, width), BF), sds((nodes, width), F32)
     cut_bf = sds((NG, cut, width), BF)
 
-    gathered = lax.all_gather(features, "x", axis=0, tiled=True)
-    gathered = lax.all_gather(gathered, "z", axis=0, tiled=True).reshape(2 * BANDS, 128, width)
+    along_x = lax.all_gather(features, "x", axis=0, tiled=True)
+    gathered = [
+        lax.all_gather(rows, "z", axis=0, tiled=True).reshape(-1, 128, width)
+        for rows in (along_x[:-128], along_x[-128:])
+    ]
 
     (outgoing,) = call(
         pick_body, [send_count], [rows2, features], [cut_bf], flops=2 * NG * cut * width * nodes,
@@ -247,7 +265,7 @@
     share = 2 * width // NG
     outs = [
         node_bf, node_bf, sds((NG, cut + share + SPARE_ROWS, width), BF), node_f32,
-        sds(gathered.shape, BF),
+        sds((2 * BANDS, 128, width), BF),
     ]
     spared = (2 * BANDS + 1, 128, width)
     output, d_agg, back, self_back, terms = call(
@@ -259,11 +277,11 @@
         scratch=[
             pltpu.VMEM(spared, BF),
             pltpu.VMEM(spared, F32),
-            pltpu.VMEM(gathered.shape, BF),
-            pltpu.SemaphoreType.DMA,
+            pltpu.VMEM((2 * BANDS, 128, width), BF),
+            pltpu.SemaphoreType.DMA((2,)),
             pltpu.SemaphoreType.DMA((STORE,)),
         ],
-        direct=[gathered],
+        direct=gathered,
         flops=1 << 30,
     )
 
@@ -273,7 +291,7 @@
 
     returned = a2a(back, ("y", "c"))
     (grad_blocks,) = call(
-        blocks_body, [block_index, block_count], [d_agg, gathered], [sds(block_values.shape, BF)],
+        blocks_body, [block_index, block_count], [d_agg, *gathered], [sds(block_values.shape, BF)],
         flops=2 * tiles_here * slots * 128 * 128 * width,
     )
     (part,) = call(

time: 195 us -> 194 us (level)
  waiting for transfers between devices: 81.9 us -> 53 us
  blocking collectives: 27.2 us -> 54.5 us
    all_gather x1 -> x2, blocking collectives: 13.3 us -> 40.6 us  [the longest x1 29.3 us: local(): lax.all_gather(rows, 'z', axis=0, tiled=True).reshape(-1, 128, width)]
    all_to_all x4, waiting for transfers between devices: 61.5 us -> 34.5 us  [a2a(): return lax.all_to_all(x, axis, 0, 0, tiled=True)]
  transfers between devices with their start and end apart: 9 -> 9, of which waited for: 4 -> 3; matrix products, arithmetic and copies ran while one was open for 3% -> 3% of each run, Pallas kernels for 8% -> 8%
where the time goes in v11:
time: 194 us
  blocking collectives  54.5 us (28%)
  waiting for transfers between devices  53 us (27%)
  starting transfers between devices  38.3 us (20%)
  Pallas kernels  25 us (13%)
  between operations  14.2 us (7%)
  local copies, waits for them, and re-layouts  4.7 us (2%)
  matrix products  2.03 us (1%)
    all_to_all x4, waiting for transfers between devices, a2a(): return lax.all_to_all(x, axis, 0, 0, tiled=True)  34.5 us
    all_to_all x4, starting transfers between devices, a2a(): return lax.all_to_all(x, axis, 0, 0, tiled=True)  29.7 us
    all_gather x1, blocking collectives, local(): lax.all_gather(rows, 'z', axis=0, tiled=True).reshape(-1, 128, width)  29.3 us
    pallas_call x6, Pallas kernels, call(): pl.pallas_call(kernel, out_shape=tuple(outs), in_specs=[SMEM] * first + [...  25 us
    all_gather x1, waiting for transfers between devices, local(): lax.all_gather(rows, 'z', axis=0, tiled=True).reshape(-1, 128, width)  18.5 us
    all_gather x1, blocking collectives, local(): along_x = lax.all_gather(features, 'x', axis=0, tiled=True)  11.3 us
    all_to_all x1, blocking collectives, a2a(): return lax.all_to_all(x, axis, 0, 0, tiled=True)  9.3 us
    ppermute x3, starting transfers between devices, shift(): return lax.ppermute(x, axis, [(i, (i + by) % n) for i in range(n)])  8.53 us
  transfers between devices with their start and end apart: 9, of which 3 were waited for; matrix products, arithmetic and copies ran while one was open for 3% of the time, Pallas kernels for 8%

profile of v11, /device:TPU:1, one launch (start us, length us, event | category | flops | bytes accessed | tf_op | source)
XLA Modules:
  0.0 193.6 jit_solution(2308855071797242934)
XLA Ops:
  7.2 11.3 %all_gather.15 = bf16[1024,256]{1,0:T(8,128)(2,1)S(1)} all-gather(bf16[256,256]{1,0:T(8,128)(2,1)} %refs_7_.1), channel_id=1, replica_groups=mesh['y'=8,'c'=2,'x'=4,'z'=8] {'x'}, dimensions={0}, use_global_device_ids=true | all-gather | bytes 655360 | tf_op jit(solution)/shard_map/all_gather | solution.py:252
  19.4 3.1 %shard_map.154 = bf16[16,128,256]{2,1,0:T(8,128)(2,1)} custom-call(s32[1,16]{1,0:T(1,128)} %refs_0_.6, s32[16,128]{1,0:T(8,128)} %bitcast.38, bf16[256,256]{1,0:T(8,128)(2,1)} %refs_7_.1), custom_call_target="tpu_custom_call" | custom-call | flops 268435456 | bytes 1187840 | tf_op jit(solution)/shard_map/pallas_call | solution.py:49
  22.5 12.2 %all-to-all-start = ((bf16[16,128,256]{2,1,0:T(8,128)(2,1)}), bf16[16,128,256]{2,1,0:T(8,128)(2,1)S(1)}, u32[]{:S(2)}, u32[]{:S(2)}) async-start(bf16[16,128,256]{2,1,0:T(8,128)(2,1)} %shard_map.154), calls=%async_computation | async-start | bytes 2097152 | tf_op jit(solution)/shard_map/all_to_all | solution.py:233
  34.7 29.3 %all_gather.17 = bf16[1024,256]{1,0:T(8,128)(2,1)} all-gather(bf16[128,256]{1,0:T(8,128)(2,1)S(1)} %slice.26), channel_id=1, replica_groups=mesh['y'=8,'c'=2,'x'=4,'z'=8] {'z'}, dimensions={0}, use_global_device_ids=true | all-gather | bytes 589824 | tf_op jit(solution)/shard_map/all_gather | solution.py:254
  64.1 0.9 convolution_add_fusion.refs_4_
  65.0 1.1 convolution_bitcast_fusion.refs_3_
  66.1 18.5 %all-gather.3.cloned.1.call-done = bf16[7168,256]{1,0:T(8,128)(2,1)} async-done(((bf16[896,256]{1,0:T(8,128)(2,1)}), bf16[7168,256]{1,0:T(8,128)(2,1)}) %all-gather.3.cloned.1.call-update) | async-done | bytes 3670032 | tf_op jit(solution)/shard_map/all_gather | solution.py:254
  84.6 10.3 %shard_map.155 = (bf16[256,256]{1,0:T(8,128)(2,1)}, bf16[256,256]{1,0:T(8,128)(2,1)}, bf16[16,176,256]{2,1,0:T(8,128)(2,1)}, f32[256,256]{1,0:T(8,128)}, bf16[64,128,256]{2,1,0:T(8,128)(2,1)}) custom-call(s32[2,24]{1,0:T(2,128)} %refs_0_.7, s32[2]{0:T(128)} %refs_1_.3, bf16[2,24,128,128]{3,2,1,0:T(8,128)(2,1)} %refs_2_.3, ...), custom_call_target="tpu_custom_call" | custom-call | flops 1073741824 | bytes 14024704 | tf_op jit(solution)/shard_map/pallas_call | solution.py:49
  94.9 7.4 %all-to-all-start.1 = ((bf16[16,176,256]{2,1,0:T(8,128)(2,1)}), bf16[16,176,256]{2,1,0:T(8,128)(2,1)}, u32[]{:S(2)}, u32[]{:S(2)}) async-start(bf16[16,176,256]{2,1,0:T(8,128)(2,1)} %get-tuple-element.12), calls=%async_computation.1 | async-start | bytes 2883584 | tf_op jit(solution)/shard_map/all_to_all | solution.py:233
  102.4 5.1 %shard_map.157.refs_1_ = bf16[2,24,128,128]{3,2,1,0:T(8,128)(2,1)} custom-call(s32[2,24]{1,0:T(2,128)} %refs_0_.7, s32[2]{0:T(128)} %refs_1_.3, bf16[256,256]{1,0:T(8,128)(2,1)} %get-tuple-element.15.refs_2_, bf16[56,128,256]{2,1,0:T(8,128)(2,1)} %bitcast.26, bf16[8,128,256]{2,1,0:T(8,128)(2,1)} %bitcast.28), custom_call_target="tpu_custom_call" | custom-call | flops 402653184 | bytes 5898240 | tf_op jit(solution)/shard_map/pallas_call | solution.py:49
  107.5 30.8 %all-to-all-done.1.refs_2_.refs_0_ = bf16[16,176,256]{2,1,0:T(8,128)(2,1)} async-done(((bf16[16,176,256]{2,1,0:T(8,128)(2,1)}), bf16[16,176,256]{2,1,0:T(8,128)(2,1)}, u32[]{:S(2)}, u32[]{:S(2)}) %all-to-all-start.1) | async-done | bytes 1441824 | tf_op jit(solution)/shard_map/all_to_all | solution.py:233
  138.3 1.7 shard_map.158
  140.0 9.3 %all_to_all.25 = bf16[4,48,256]{2,1,0:T(8,128)(2,1)S(1)} all-to-all(bf16[4,48,256]{2,1,0:T(8,128)(2,1)} %shard_map.158), channel_id=1, replica_groups=mesh['y'=8,'c'=2,'x'=4,'z'=8] {'x'}, dimensions={0} | all-to-all | bytes 196608 | tf_op jit(solution)/shard_map/all_to_all | solution.py:233
  150.0 3.6 %all-to-all-start.3 = ((bf16[8,48,256]{2,1,0:T(8,128)(2,1)}), bf16[8,48,256]{2,1,0:T(8,128)(2,1)S(1)}, u32[]{:S(2)}, u32[]{:S(2)}) async-start(bf16[8,48,256]{2,1,0:T(8,128)(2,1)} %broadcast_in_dim.2), calls=%async_computation.4 | async-start | bytes 393216 | tf_op jit(solution)/shard_map/all_to_all | solution.py:233
  153.7 1.1 dynamic-slice_bitcast_fusion.2
  154.7 2.3 %collective-permute-start = (bf16[256,256]{1,0:T(8,128)(2,1)S(1)}, bf16[256,256]{1,0:T(8,128)(2,1)S(1)}, u32[]{:S(2)}, u32[]{:S(2)}) collective-permute-start(bf16[256,256]{1,0:T(8,128)(2,1)S(1)} %get-tuple-element.18), channel_id=1, source_target_pairs={{0,8},{8,16},{16,24},{24,0},{1,9},{9,17},{17,25},{25,1},{2,10},{10... | collective-permute-start | bytes 393224 | tf_op jit(solution)/shard_map/ppermute | solution.py:237
  157.0 3.6 %collective-permute-start.1 = (bf16[256,256]{1,0:T(8,128)(2,1)S(1)}, bf16[256,256]{1,0:T(8,128)(2,1)S(1)}, u32[]{:S(2)}, u32[]{:S(2)}) collective-permute-start(bf16[256,256]{1,0:T(8,128)(2,1)S(1)} %get-tuple-element.20), channel_id=1, source_target_pairs={{0,16},{8,24},{16,0},{24,8},{1,17},{9,25},{17,1},{25,9},{2,18},{10... | collective-permute-start | bytes 393224 | tf_op jit(solution)/shard_map/ppermute | solution.py:237
  160.6 2.6 %collective-permute-start.2 = (bf16[256,256]{1,0:T(8,128)(2,1)S(1)}, bf16[256,256]{1,0:T(8,128)(2,1)S(1)}, u32[]{:S(2)}, u32[]{:S(2)}) collective-permute-start(bf16[256,256]{1,0:T(8,128)(2,1)S(1)} %get-tuple-element.19), channel_id=1, source_target_pairs={{0,24},{8,0},{16,8},{24,16},{1,25},{9,1},{17,9},{25,17},{2,26},{10... | collective-permute-start | bytes 393224 | tf_op jit(solution)/shard_map/ppermute | solution.py:237
  164.0 1.6 shard_map.159
  165.6 6.5 %all-to-all-start.4 = ((bf16[8,48,256]{2,1,0:T(8,128)(2,1)}), bf16[8,48,256]{2,1,0:T(8,128)(2,1)S(1)}, u32[]{:S(2)}, u32[]{:S(2)}) async-start(bf16[8,48,256]{2,1,0:T(8,128)(2,1)} %shard_map.159), calls=%async_computation.5 | async-start | bytes 393216 | tf_op jit(solution)/shard_map/all_to_all | solution.py:233
  172.1 3.2 %shard_map.156 = f32[256,256]{1,0:T(8,128)} custom-call(s32[1,16]{1,0:T(1,128)} %refs_0_.6, s32[16,128]{1,0:T(8,128)} %bitcast.39, bf16[16,176,256]{2,1,0:T(8,128)(2,1)} %all-to-all-done.1.refs_2_.refs_0_, f32[256,256]{1,0:T(8,128)} %get-tuple-element.13.refs_3_), custom_call_target="tpu_custom_call" | custom-call | flops 268435456 | bytes 1974272 | tf_op jit(solution)/shard_map/pallas_call | solution.py:49
  175.4 1.7 fusion.3
  177.1 3.6 %all-to-all-done.4 = bf16[8,48,256]{2,1,0:T(8,128)(2,1)S(1)} async-done(((bf16[8,48,256]{2,1,0:T(8,128)(2,1)}), bf16[8,48,256]{2,1,0:T(8,128)(2,1)S(1)}, u32[]{:S(2)}, u32[]{:S(2)}) %all-to-all-start.4) | async-done | bytes 196640 | tf_op jit(solution)/shard_map/all_to_all | solution.py:233
  180.7 4.6 %all-gather = bf16[8,96,256]{2,1,0:T(8,128)(2,1)S(1)} all-gather(bf16[8,48,256]{2,1,0:T(8,128)(2,1)S(1)} %all-to-all-done.4), channel_id=2, replica_groups=mesh['y'=8,'c'=2,'x'=4,'z'=8] {'c'}, dimensions={1}, use_global_device_ids=true | all-gather | bytes 589824 | tf_op jit(solution)/shard_map/all_gather | solution.py:317
  (27 shorter events, 3.9 us)
Async XLA Ops:
  7.2 77.5 %all-gather.3.cloned.1.call-start = ((), (), s32[]{:S(2)}) async-start(), calls=%async_computation.6 | async-start | bytes 4128768 | tf_op jit(solution)/shard_map/all_gather | solution.py:254
  22.5 41.6 %copy-start.1 = (bf16[256,256]{1,0:T(8,128)(2,1)S(1)}, bf16[256,256]{1,0:T(8,128)(2,1)}, u32[]{:S(2)}) copy-start(bf16[256,256]{1,0:T(8,128)(2,1)} %refs_7_.1) | copy-start | bytes 393220
  22.5 41.6 %copy-start.3 = (bf16[256,256]{1,0:T(8,128)(2,1)S(1)}, bf16[256,256]{1,0:T(8,128)(2,1)}, u32[]{:S(2)}) copy-start(bf16[256,256]{1,0:T(8,128)(2,1)} %refs_8_.1) | copy-start | bytes 393220
  22.5 41.6 %copy-start.4 = (f32[256]{0:T(256)S(1)}, f32[256]{0:T(256)}, u32[]{:S(2)}) copy-start(f32[256]{0:T(256)} %param.20) | copy-start | bytes 3076
  22.5 42.5 %copy-start = (bf16[256,2048]{1,0:T(8,128)(2,1)S(1)}, bf16[256,2048]{1,0:T(8,128)(2,1)}, u32[]{:S(2)}) copy-start(bf16[256,2048]{1,0:T(8,128)(2,1)} %refs_9_.1) | copy-start | bytes 3145732
  22.5 42.5 %all-to-all-start = ((bf16[16,128,256]{2,1,0:T(8,128)(2,1)}), bf16[16,128,256]{2,1,0:T(8,128)(2,1)S(1)}, u32[]{:S(2)}, u32[]{:S(2)}) async-start(bf16[16,128,256]{2,1,0:T(8,128)(2,1)} %shard_map.154), calls=%async_computation | async-start | bytes 2097152 | tf_op jit(solution)/shard_map/all_to_all | solution.py:233
  34.7 119.0 %reduce-scatter.2.cloned.1.call-start = ((), (), s32[]{:S(2)}) async-start(), calls=%async_computation.7 | async-start | bytes 4718592 | tf_op jit(solution)/shard_map/reduce_scatter | solution.py:288
  94.9 43.3 %all-to-all-start.1 = ((bf16[16,176,256]{2,1,0:T(8,128)(2,1)}), bf16[16,176,256]{2,1,0:T(8,128)(2,1)}, u32[]{:S(2)}, u32[]{:S(2)}) async-start(bf16[16,176,256]{2,1,0:T(8,128)(2,1)} %get-tuple-element.12), calls=%async_computation.1 | async-start | bytes 2883584 | tf_op jit(solution)/shard_map/all_to_all | solution.py:233
  150.0 13.3 %all-to-all-start.3 = ((bf16[8,48,256]{2,1,0:T(8,128)(2,1)}), bf16[8,48,256]{2,1,0:T(8,128)(2,1)S(1)}, u32[]{:S(2)}, u32[]{:S(2)}) async-start(bf16[8,48,256]{2,1,0:T(8,128)(2,1)} %broadcast_in_dim.2), calls=%async_computation.4 | async-start | bytes 393216 | tf_op jit(solution)/shard_map/all_to_all | solution.py:233
  154.7 20.6 %collective-permute-start = (bf16[256,256]{1,0:T(8,128)(2,1)S(1)}, bf16[256,256]{1,0:T(8,128)(2,1)S(1)}, u32[]{:S(2)}, u32[]{:S(2)}) collective-permute-start(bf16[256,256]{1,0:T(8,128)(2,1)S(1)} %get-tuple-element.18), channel_id=1, source_target_pairs={{0,8},{8,16},{16,24},{24,0},{1,9},{9,17},{17,25},{25,1},{2,10},{10... | collective-permute-start | bytes 393224 | tf_op jit(solution)/shard_map/ppermute | solution.py:237
  157.0 18.3 %collective-permute-start.1 = (bf16[256,256]{1,0:T(8,128)(2,1)S(1)}, bf16[256,256]{1,0:T(8,128)(2,1)S(1)}, u32[]{:S(2)}, u32[]{:S(2)}) collective-permute-start(bf16[256,256]{1,0:T(8,128)(2,1)S(1)} %get-tuple-element.20), channel_id=1, source_target_pairs={{0,16},{8,24},{16,0},{24,8},{1,17},{9,25},{17,1},{25,9},{2,18},{10... | collective-permute-start | bytes 393224 | tf_op jit(solution)/shard_map/ppermute | solution.py:237
  160.6 14.7 %collective-permute-start.2 = (bf16[256,256]{1,0:T(8,128)(2,1)S(1)}, bf16[256,256]{1,0:T(8,128)(2,1)S(1)}, u32[]{:S(2)}, u32[]{:S(2)}) collective-permute-start(bf16[256,256]{1,0:T(8,128)(2,1)S(1)} %get-tuple-element.19), channel_id=1, source_target_pairs={{0,24},{8,0},{16,8},{24,16},{1,25},{9,1},{17,9},{25,17},{2,26},{10... | collective-permute-start | bytes 393224 | tf_op jit(solution)/shard_map/ppermute | solution.py:237
  163.3 0.7 copy-start.2
  165.6 15.1 %all-to-all-start.4 = ((bf16[8,48,256]{2,1,0:T(8,128)(2,1)}), bf16[8,48,256]{2,1,0:T(8,128)(2,1)S(1)}, u32[]{:S(2)}, u32[]{:S(2)}) async-start(bf16[8,48,256]{2,1,0:T(8,128)(2,1)} %shard_map.159), calls=%async_computation.5 | async-start | bytes 393216 | tf_op jit(solution)/shard_map/all_to_all | solution.py:233
Sparse Core Ops, SparseCore 0:
  19.5 65.0 all-gather.2
  95.1 56.5 reduce-scatter.1
